TPU v7x, 512 devices: a whole 4x4x16 slice. The times are simulated.
512 devices in a mesh: bx: 32 (over z, x_lo), by: 16 (over x_hi, y, core).
Axes of the slice: x: 4 (x_hi: 2, x_lo: 2; x = x_hi * 2 + x_lo), y: 4, z: 16, core: 2. Of those that a mesh axis runs over, the one named last changes fastest.
Arguments:
- blocks: bfloat16 [32, 16, 32, 4096], P('bx', 'by'), as said below
- faces: bfloat16 [32, 16, 32, 4096], P('bx', 'by'), may hold values from -1.1953125 to 1.1953125
- tentative: bfloat16 [32, 16, 32, 4096], P('bx', 'by'), may hold values from -0.75 to 0.75
- aggregate: int32 [32, 16, 32], P('bx', 'by'), may hold values from 0 to 3
- ghost_labels: int32 [32, 16, 24], P('bx', 'by'), may hold values from 0 to 3, as said below
- rhs: float32 [32, 16, 6, 64, 32], P('bx', 'by'), may hold values from -6 to 6
- guess: float32 [32, 16, 6, 64, 32], P('bx', 'by'), may hold values from -6 to 6
- bounds: float32 [2], replicated, as said below
Outputs:
- smoothed: float32 [32, 16, 6, 64, 32], P('bx', 'by')
- coarse_local: float32 [32, 16, 256, 256], P('bx', 'by')
- coarse_ghost: float32 [32, 16, 4, 256, 256], P('bx', 'by')
Inputs may be any that keep to these rules, and one draw needn't show every extreme that they name: `ghost_labels`: each entry equals the aggregate number of the neighbouring brick's element across that face, 0 where the brick has no neighbour on that side. `blocks`: every diagonal entry of every block is at least 2. 0 < bounds[0] < bounds[1].
All inputs are finite; a program needn't handle non-finite values.
Results may differ from a plain program's by a relative error of at most 0.0029.
Values may be sent and summed in bfloat16 or wider, within the bound.
No kernel may reach another device: no remote copies, remote signals or barrier semaphores. Data moves between devices by JAX's collectives and lax.ppermute only.
A program may use at most 64 MiB of HBM per device.

v0:
```python
import jax
import jax.numpy as jnp
from jax import lax
from jax.sharding import PartitionSpec as P

BLOCK = 64
NAGG = 4
EX = 4
EY = 8


def with_halo(block, sides, width):
    for axis, dim in sides:
        count = lax.axis_size(axis)
        forward = [(i, i + 1) for i in range(count - 1)]
        backward = [(target, source) for source, target in forward]
        low = lax.ppermute(
            lax.slice_in_dim(block, block.shape[dim] - width, None, axis=dim), axis, forward
        )
        high = lax.ppermute(lax.slice_in_dim(block, 0, width, axis=dim), axis, backward)
        block = jnp.concatenate([low, block, high], axis=dim)
    return block


def trace_blocks(prolong):
    dof_cube = prolong.reshape(EX, EY, 4, 4, 4, prolong.shape[-1])
    width = prolong.shape[-1]
    minus_x = dof_cube[:, :, 0].reshape(EX, EY, 16, width)
    plus_x = dof_cube[:, :, 3].reshape(EX, EY, 16, width)
    minus_y = dof_cube[:, :, :, 0].reshape(EX, EY, 16, width)
    plus_y = dof_cube[:, :, :, 3].reshape(EX, EY, 16, width)
    return (minus_x, plus_x, minus_y, plus_y)


def field_traces(vector_field):
    vectors = vector_field.shape[0]
    dof_cube = vector_field.reshape(vectors, 4, 4, 4, EX, EY)
    minus_x = dof_cube[:, 0].reshape(vectors, 16, EX, EY)
    plus_x = dof_cube[:, 3].reshape(vectors, 16, EX, EY)
    minus_y = dof_cube[:, :, 0].reshape(vectors, 16, EX, EY)
    plus_y = dof_cube[:, :, 3].reshape(vectors, 16, EX, EY)
    return (minus_x, plus_x, minus_y, plus_y)


def neighbour_rows(traces, edge_rows, axis_x, axis_y):
    minus_x, plus_x, minus_y, plus_y = traces
    low_x, high_x, low_y, high_y = edge_rows
    rows_x = plus_x.shape[axis_x]
    rows_y = plus_y.shape[axis_y]
    from_low_x = jnp.concatenate(
        [jnp.expand_dims(low_x, axis_x), lax.slice_in_dim(plus_x, 0, rows_x - 1, axis=axis_x)],
        axis_x,
    )
    from_high_x = jnp.concatenate(
        [lax.slice_in_dim(minus_x, 1, rows_x, axis=axis_x), jnp.expand_dims(high_x, axis_x)], axis_x
    )
    from_low_y = jnp.concatenate(
        [jnp.expand_dims(low_y, axis_y), lax.slice_in_dim(plus_y, 0, rows_y - 1, axis=axis_y)],
        axis_y,
    )
    from_high_y = jnp.concatenate(
        [lax.slice_in_dim(minus_y, 1, rows_y, axis=axis_y), jnp.expand_dims(high_y, axis_y)], axis_y
    )
    return jnp.stack([from_low_x, from_high_x, from_low_y, from_high_y])


def galerkin(diag_blocks, couplings, prolong, labels, traces, row_ghosts, label_ghosts):
    elements = EX * EY
    coarse = prolong.shape[-1]
    near_rows = neighbour_rows(traces, row_ghosts, 0, 1).reshape(4, elements, 16, coarse)
    grid_labels = labels.reshape(EX, EY)
    label_traces = (grid_labels, grid_labels, grid_labels, grid_labels)
    near_labels = neighbour_rows(label_traces, label_ghosts, 0, 1).reshape(4, elements)
    applied = jnp.einsum(
        "epq,eqr->epr", diag_blocks, prolong, preferred_element_type=jnp.float32
    ).astype(jnp.bfloat16)
    w_self = jnp.einsum("epa,epb->eab", prolong, applied, preferred_element_type=jnp.float32)
    coupled = jnp.einsum(
        "efpt,fetr->fepr", couplings, near_rows, preferred_element_type=jnp.float32
    ).astype(jnp.bfloat16)
    w_face = jnp.einsum("epa,fepb->feab", prolong, coupled, preferred_element_type=jnp.float32)
    numbers = jnp.arange(NAGG, dtype=jnp.int32)
    own_onehot = (labels[:, None] == numbers[None, :]).astype(jnp.float32)
    other_onehot = (near_labels[:, :, None] == numbers[None, None, :]).astype(jnp.float32)
    row_index = lax.broadcasted_iota(jnp.int32, (EX, EY), 0).reshape(elements)
    col_index = lax.broadcasted_iota(jnp.int32, (EX, EY), 1).reshape(elements)
    outside = jnp.stack(
        [row_index == 0, row_index == EX - 1, col_index == 0, col_index == EY - 1]
    ).astype(jnp.float32)
    pair_self = own_onehot[:, :, None] * own_onehot[:, None, :]
    pair_face = own_onehot[None, :, :, None] * other_onehot[:, :, None, :]
    local_part = jnp.einsum("eab,epr->apbr", pair_self, w_self, precision=lax.Precision.HIGHEST)
    local_part = local_part + jnp.einsum(
        "feab,fepr->apbr",
        pair_face * (1.0 - outside)[:, :, None, None],
        w_face,
        precision=lax.Precision.HIGHEST,
    )
    ghost_part = jnp.einsum(
        "feab,fepr->fapbr",
        pair_face * outside[:, :, None, None],
        w_face,
        precision=lax.Precision.HIGHEST,
    )
    coarse_width = NAGG * coarse
    return (
        local_part.reshape(coarse_width, coarse_width),
        ghost_part.reshape(4, coarse_width, coarse_width),
    )


def operate_brick(diag_wide, couple_wide, vector_field, traces, edge_rows):
    vectors = vector_field.shape[0]
    near_rows = neighbour_rows(traces, edge_rows, 2, 3).reshape(4, vectors, 16, EX * EY)
    own_term = jnp.einsum("epq,nqe->npe", diag_wide, vector_field, precision=lax.Precision.HIGHEST)
    face_term = jnp.einsum(
        "efpt,fnte->npe", couple_wide, near_rows, precision=lax.Precision.HIGHEST
    )
    return own_term + face_term


def chebyshev(operate, inverse, rhs_values, guess_values, bounds):
    lower_bound = bounds[0]
    upper_bound = bounds[1]
    centre = 0.5 * (upper_bound + lower_bound)
    half_width = 0.5 * (upper_bound - lower_bound)
    spread = centre / half_width
    factor = 1.0 / spread
    residue = rhs_values - operate(guess_values)
    update = inverse * residue / centre
    answer = guess_values + update
    for sweep_index in range(2):
        residue = residue - operate(update)
        next_factor = 1.0 / (2.0 * spread - factor)
        update = next_factor * factor * update + 2.0 * next_factor / half_width * inverse * residue
        answer = answer + update
        factor = next_factor
    return answer


def prolong_ghosts(prolong):
    coarse = prolong.shape[-1]
    extended = with_halo(prolong.reshape(EX, EY, BLOCK * coarse), (("bx", 0), ("by", 1)), 1)
    dof_cube = extended.reshape(EX + 2, EY + 2, 4, 4, 4, coarse)
    low_x = dof_cube[0, 1 : EY + 1, 3].reshape(EY, 16, coarse)
    high_x = dof_cube[EX + 1, 1 : EY + 1, 0].reshape(EY, 16, coarse)
    low_y = dof_cube[1 : EX + 1, 0, :, 3].reshape(EX, 16, coarse)
    high_y = dof_cube[1 : EX + 1, EY + 1, :, 0].reshape(EX, 16, coarse)
    return (low_x, high_x, low_y, high_y)


def field_edges(vector_field):
    vectors = vector_field.shape[0]
    traces = field_traces(vector_field)
    extended = with_halo(vector_field.reshape(vectors * BLOCK, EX, EY), (("bx", 1), ("by", 2)), 1)
    dof_cube = extended.reshape(vectors, 4, 4, 4, EX + 2, EY + 2)
    low_x = dof_cube[:, 3, :, :, 0, 1 : EY + 1].reshape(vectors, 16, EY)
    high_x = dof_cube[:, 0, :, :, EX + 1, 1 : EY + 1].reshape(vectors, 16, EY)
    low_y = dof_cube[:, :, 3, :, 1 : EX + 1, 0].reshape(vectors, 16, EX)
    high_y = dof_cube[:, :, 0, :, 1 : EX + 1, EY + 1].reshape(vectors, 16, EX)
    return (traces, (low_x, high_x, low_y, high_y))


def on_device(blocks, faces, tentative, aggregate, ghost_labels, rhs, guess, bounds):
    elements = EX * EY
    coarse = tentative.shape[-1] // BLOCK
    diag_blocks = blocks.reshape(elements, BLOCK, BLOCK)
    couplings = faces.reshape(elements, 4, BLOCK, 16)
    prolong = tentative.reshape(elements, BLOCK, coarse)
    labels = aggregate.reshape(elements)
    side_labels = ghost_labels.reshape(2 * EY + 2 * EX)
    label_ghosts = (
        side_labels[:EY],
        side_labels[EY : 2 * EY],
        side_labels[2 * EY : 2 * EY + EX],
        side_labels[2 * EY + EX :],
    )
    traces = trace_blocks(prolong)
    row_ghosts = prolong_ghosts(prolong)
    local_part, ghost_part = galerkin(
        diag_blocks, couplings, prolong, labels, traces, row_ghosts, label_ghosts
    )
    diag_wide = diag_blocks.astype(jnp.float32)
    couple_wide = couplings.astype(jnp.float32)

    def operate(vector_field):
        field_trace_set, edge_rows = field_edges(vector_field)
        return operate_brick(diag_wide, couple_wide, vector_field, field_trace_set, edge_rows)

    inverse = 1.0 / jnp.diagonal(diag_blocks, axis1=1, axis2=2).astype(jnp.float32).T
    vectors = rhs.shape[2]
    rhs_values = rhs.reshape(vectors, BLOCK, elements)
    guess_values = guess.reshape(vectors, BLOCK, elements)
    smoothed = chebyshev(operate, inverse, rhs_values, guess_values, bounds)
    return (smoothed[None, None], local_part[None, None], ghost_part[None, None])


def solution(mesh):
    placed = (
        P("bx", "by", None, None),
        P("bx", "by", None, None),
        P("bx", "by", None, None),
        P("bx", "by", None),
        P("bx", "by", None),
        P("bx", "by", None, None, None),
        P("bx", "by", None, None, None),
        P(),
    )
    return jax.shard_map(
        on_device,
        mesh=mesh,
        in_specs=placed,
        out_specs=(
            P("bx", "by", None, None, None),
            P("bx", "by", None, None),
            P("bx", "by", None, None, None),
        ),
        check_vma=False,
    )
```

profile of v0, /device:TPU:121, one launch (start us, length us, event | category | flops | bytes accessed | tf_op | source)
XLA Modules:
  0.0 183.7 jit_solution(10881168476943183817)
XLA Ops:
  2.3 3.1 %collective-permute-start = (f32[384,1,8]{0,2,1:T(8,128)}, f32[384,1,8]{0,2,1:T(8,128)}, u32[]{:S(2)}, u32[]{:S(2)}) collective-permute-start(f32[384,1,8]{0,2,1:T(8,128)} %get-tuple-element.70), channel_id=1, source_target_pairs={{0,16},{16,32},{32,48},{48,64},{64,80},{80,96},{96,112},{112,128},... | collective-permute-start | bytes 36872 | tf_op jit(solution)/shard_map/ppermute | solution.py:17
  5.4 3.1 %collective-permute-start.1 = (f32[384,1,8]{0,2,1:T(8,128)}, f32[384,1,8]{0,2,1:T(8,128)}, u32[]{:S(2)}, u32[]{:S(2)}) collective-permute-start(f32[384,1,8]{0,2,1:T(8,128)} %get-tuple-element.69), channel_id=1, source_target_pairs={{16,0},{32,16},{48,32},{64,48},{80,64},{96,80},{112,96},{128,112},... | collective-permute-start | bytes 36872 | tf_op jit(solution)/shard_map/ppermute | solution.py:20
  8.5 1.5 slice_bitcast_fusion.1
  10.0 3.6 %collective-permute-start.12 = (bf16[1,8,4096]{2,1,0:T(8,128)(2,1)}, bf16[1,8,4096]{2,1,0:T(8,128)(2,1)}, u32[]{:S(2)}, u32[]{:S(2)}) collective-permute-start(bf16[1,8,4096]{2,1,0:T(8,128)(2,1)} %get-tuple-element.57), channel_id=1, source_target_pairs={{0,16},{16,32},{32,48},{48,64},{64,80},{80,96},{96,112},{112,128},... | collective-permute-start | bytes 196616 | tf_op jit(solution)/shard_map/ppermute | solution.py:17
  13.6 2.6 %collective-permute-start.13 = (bf16[1,8,4096]{2,1,0:T(8,128)(2,1)}, bf16[1,8,4096]{2,1,0:T(8,128)(2,1)}, u32[]{:S(2)}, u32[]{:S(2)}) collective-permute-start(bf16[1,8,4096]{2,1,0:T(8,128)(2,1)} %get-tuple-element.58), channel_id=1, source_target_pairs={{16,0},{32,16},{48,32},{64,48},{80,64},{96,80},{112,96},{128,112},... | collective-permute-start | bytes 196616 | tf_op jit(solution)/shard_map/ppermute | solution.py:20
  16.2 1.4 fusion.92
  20.4 1.0 copy.374
  33.1 6.0 %collective-permute-start.2 = (f32[384,6,1]{0,2,1:T(1,128)S(1)}, f32[384,6,1]{0,2,1:T(1,128)S(1)}, u32[]{:S(2)}, u32[]{:S(2)}) collective-permute-start(f32[384,6,1]{0,2,1:T(1,128)S(1)} %get-tuple-element.63), channel_id=1, source_target_pairs={{0,1},{1,2},{2,3},{3,4},{4,5},{5,6},{6,7},{7,8},{8,9},{9,10},{10,1... | collective-permute-start | bytes 27656 | tf_op jit(solution)/shard_map/ppermute | solution.py:17
  39.1 1.9 %collective-permute-start.3 = (f32[384,6,1]{0,2,1:T(1,128)S(1)}, f32[384,6,1]{0,2,1:T(1,128)S(1)}, u32[]{:S(2)}, u32[]{:S(2)}) collective-permute-start(f32[384,6,1]{0,2,1:T(1,128)S(1)} %get-tuple-element.64), channel_id=1, source_target_pairs={{1,0},{2,1},{3,2},{4,3},{5,4},{6,5},{7,6},{8,7},{9,8},{10,9},{11,1... | collective-permute-start | bytes 27656 | tf_op jit(solution)/shard_map/ppermute | solution.py:20
  41.6 1.3 reshape.306
  46.0 1.4 copy.393
  47.4 2.1 %copy.394 = bf16[32,4,64,16]{2,3,1,0:T(8,128)(2,1)} copy(bf16[32,4,64,16]{0,3,2,1:T(8,128)(2,1)S(1)} %bitcast.217) | data formatting | bytes 524288 | tf_op jit(solution)/shard_map/reshape | solution.py:168
  52.5 1.1 slice_reduce_fusion.5
  58.2 1.5 convolution_bitcast_fusion.6
  59.8 1.6 multiply_divide_fusion
  61.6 3.9 %collective-permute-start.4 = (f32[384,1,8]{0,2,1:T(8,128)S(1)}, f32[384,1,8]{0,2,1:T(8,128)S(1)}, u32[]{:S(2)}, u32[]{:S(2)}) collective-permute-start(f32[384,1,8]{0,2,1:T(8,128)S(1)} %get-tuple-element.68), channel_id=1, source_target_pairs={{0,16},{16,32},{32,48},{48,64},{64,80},{80,96},{96,112},{112,128},... | collective-permute-start | bytes 36872 | tf_op jit(solution)/shard_map/ppermute | solution.py:17
  65.5 2.3 %collective-permute-start.5 = (f32[384,1,8]{0,2,1:T(8,128)S(1)}, f32[384,1,8]{0,2,1:T(8,128)S(1)}, u32[]{:S(2)}, u32[]{:S(2)}) collective-permute-start(f32[384,1,8]{0,2,1:T(8,128)S(1)} %get-tuple-element.67), channel_id=1, source_target_pairs={{16,0},{32,16},{48,32},{64,48},{80,64},{96,80},{112,96},{128,112},... | collective-permute-start | bytes 36872 | tf_op jit(solution)/shard_map/ppermute | solution.py:20
  68.2 5.0 %collective-permute-done.5 = f32[384,1,8]{0,2,1:T(8,128)S(1)} collective-permute-done((f32[384,1,8]{0,2,1:T(8,128)S(1)}, f32[384,1,8]{0,2,1:T(8,128)S(1)}, u32[]{:S(2)}, u32[]{:S(2)}) %collective-permute-start.5) | collective-permute-done | bytes 12320 | tf_op jit(solution)/shard_map/ppermute | solution.py:20
  73.2 8.2 %collective-permute-start.6 = (f32[384,6,1]{0,2,1:T(1,128)S(1)}, f32[384,6,1]{0,2,1:T(1,128)S(1)}, u32[]{:S(2)}, u32[]{:S(2)}) collective-permute-start(f32[384,6,1]{0,2,1:T(1,128)S(1)} %get-tuple-element.61), channel_id=1, source_target_pairs={{0,1},{1,2},{2,3},{3,4},{4,5},{5,6},{6,7},{7,8},{8,9},{9,10},{10,1... | collective-permute-start | bytes 27656 | tf_op jit(solution)/shard_map/ppermute | solution.py:17
  81.3 2.1 %collective-permute-start.7 = (f32[384,6,1]{0,2,1:T(1,128)S(1)}, f32[384,6,1]{0,2,1:T(1,128)S(1)}, u32[]{:S(2)}, u32[]{:S(2)}) collective-permute-start(f32[384,6,1]{0,2,1:T(1,128)S(1)} %get-tuple-element.62), channel_id=1, source_target_pairs={{1,0},{2,1},{3,2},{4,3},{5,4},{6,5},{7,6},{8,7},{9,8},{10,9},{11,1... | collective-permute-start | bytes 27656 | tf_op jit(solution)/shard_map/ppermute | solution.py:20
  85.8 4.1 %collective-permute-done.7 = f32[384,6,1]{0,2,1:T(1,128)S(1)} collective-permute-done((f32[384,6,1]{0,2,1:T(1,128)S(1)}, f32[384,6,1]{0,2,1:T(1,128)S(1)}, u32[]{:S(2)}, u32[]{:S(2)}) %collective-permute-start.7) | collective-permute-done | bytes 9248 | tf_op jit(solution)/shard_map/ppermute | solution.py:20
  90.6 1.3 copy.396
  92.0 1.0 slice_reduce_fusion.3
  95.5 1.0 pad_maximum_fusion.7
  97.9 1.5 convolution_bitcast_fusion.5
  99.4 1.6 multiply_add_fusion
  101.2 5.1 %collective-permute-start.8 = (f32[384,1,8]{0,2,1:T(8,128)S(1)}, f32[384,1,8]{0,2,1:T(8,128)S(1)}, u32[]{:S(2)}, u32[]{:S(2)}) collective-permute-start(f32[384,1,8]{0,2,1:T(8,128)S(1)} %get-tuple-element.66), channel_id=1, source_target_pairs={{0,16},{16,32},{32,48},{48,64},{64,80},{80,96},{96,112},{112,128},... | collective-permute-start | bytes 36872 | tf_op jit(solution)/shard_map/ppermute | solution.py:17
  106.4 1.9 %collective-permute-start.9 = (f32[384,1,8]{0,2,1:T(8,128)S(1)}, f32[384,1,8]{0,2,1:T(8,128)S(1)}, u32[]{:S(2)}, u32[]{:S(2)}) collective-permute-start(f32[384,1,8]{0,2,1:T(8,128)S(1)} %get-tuple-element.65), channel_id=1, source_target_pairs={{16,0},{32,16},{48,32},{64,48},{80,64},{96,80},{112,96},{128,112},... | collective-permute-start | bytes 36872 | tf_op jit(solution)/shard_map/ppermute | solution.py:20
  108.7 2.1 %collective-permute-done.9 = f32[384,1,8]{0,2,1:T(8,128)S(1)} collective-permute-done((f32[384,1,8]{0,2,1:T(8,128)S(1)}, f32[384,1,8]{0,2,1:T(8,128)S(1)}, u32[]{:S(2)}, u32[]{:S(2)}) %collective-permute-start.9) | collective-permute-done | bytes 12320 | tf_op jit(solution)/shard_map/ppermute | solution.py:20
  110.8 5.2 %collective-permute-start.10 = (f32[384,6,1]{0,2,1:T(1,128)S(1)}, f32[384,6,1]{0,2,1:T(1,128)S(1)}, u32[]{:S(2)}, u32[]{:S(2)}) collective-permute-start(f32[384,6,1]{0,2,1:T(1,128)S(1)} %get-tuple-element.59), channel_id=1, source_target_pairs={{0,1},{1,2},{2,3},{3,4},{4,5},{5,6},{6,7},{7,8},{8,9},{9,10},{10,1... | collective-permute-start | bytes 27656 | tf_op jit(solution)/shard_map/ppermute | solution.py:17
  116.1 1.9 %collective-permute-start.11 = (f32[384,6,1]{0,2,1:T(1,128)S(1)}, f32[384,6,1]{0,2,1:T(1,128)S(1)}, u32[]{:S(2)}, u32[]{:S(2)}) collective-permute-start(f32[384,6,1]{0,2,1:T(1,128)S(1)} %get-tuple-element.60), channel_id=1, source_target_pairs={{1,0},{2,1},{3,2},{4,3},{5,4},{6,5},{7,6},{8,7},{9,8},{10,9},{11,1... | collective-permute-start | bytes 27656 | tf_op jit(solution)/shard_map/ppermute | solution.py:20
  120.4 4.3 %collective-permute-done.11 = f32[384,6,1]{0,2,1:T(1,128)S(1)} collective-permute-done((f32[384,6,1]{0,2,1:T(1,128)S(1)}, f32[384,6,1]{0,2,1:T(1,128)S(1)}, u32[]{:S(2)}, u32[]{:S(2)}) %collective-permute-start.11) | collective-permute-done | bytes 9248 | tf_op jit(solution)/shard_map/ppermute | solution.py:20
  125.3 1.3 copy.418
  126.8 1.0 slice_reduce_fusion.1
  130.2 1.0 pad_maximum_fusion.11
  132.7 1.5 convolution_bitcast_fusion.4
  136.2 3.0 %collective-permute-start.14 = (bf16[6,1,4096]{2,0,1:T(8,128)(2,1)S(1)}, bf16[6,1,4096]{2,0,1:T(8,128)(2,1)S(1)}, u32[]{:S(2)}, u32[]{:S(2)}) collective-permute-start(bf16[6,1,4096]{2,0,1:T(8,128)(2,1)S(1)} %get-tuple-element.55), channel_id=1, source_target_pairs={{0,1},{1,2},{2,3},{3,4},{4,5},{5,6},{6,7},{7,8},{8,9},{9,10},{10,1... | collective-permute-start | bytes 147464 | tf_op jit(solution)/shard_map/ppermute | solution.py:17
  139.2 1.9 %collective-permute-start.15 = (bf16[6,1,4096]{2,0,1:T(8,128)(2,1)S(1)}, bf16[6,1,4096]{2,0,1:T(8,128)(2,1)S(1)}, u32[]{:S(2)}, u32[]{:S(2)}) collective-permute-start(bf16[6,1,4096]{2,0,1:T(8,128)(2,1)S(1)} %get-tuple-element.56), channel_id=1, source_target_pairs={{1,0},{2,1},{3,2},{4,3},{5,4},{6,5},{7,6},{8,7},{9,8},{10,9},{11,1... | collective-permute-start | bytes 147464 | tf_op jit(solution)/shard_map/ppermute | solution.py:20
  142.8 5.6 %collective-permute-done.15 = bf16[6,1,4096]{2,0,1:T(8,128)(2,1)S(1)} collective-permute-done((bf16[6,1,4096]{2,0,1:T(8,128)(2,1)S(1)}, bf16[6,1,4096]{2,0,1:T(8,128)(2,1)S(1)}, u32[]{:S(2)}, u32[]{:S(2)}) %collective-permute-start.15) | collective-permute-done | bytes 49184 | tf_op jit(solution)/shard_map/ppermute | solution.py:20
  148.9 2.0 %reshape.294 = bf16[6,10,4,4,4,64]{5,4,3,2,0,1:T(4,128)(2,1)} reshape(bf16[6,10,4096]{2,0,1:T(8,128)(2,1)S(1)} %pad_maximum_fusion) | data formatting | bytes 983040 | tf_op jit(solution)/shard_map/reshape | solution.py:144
  152.6 3.3 %convolution_bitcast_fusion = f32[4,32,64,64,1]{2,3,0,1,4:T(8,128)} fusion(bf16[32,4,64,16]{2,3,1,0:T(8,128)(2,1)S(1)} %copy-done.3, bf16[1,32,16,64]{3,2,0,1:T(8,128)(2,1)S(1)} %bitcast.237, bf16[1,32,16,64]{3,2,0,1:T(8,128)(2,1)S(1)} %bitcast.236, bf16[1,32,16,64]{3,2,0,1:T(8,128)(2,1)S(1)} %bitcast.239, bf16[1,32,16,64]{3,2,0,1:T(8,128)(2,1)S(1)} %bitcast.238, ...), kind=kOutput, calls=%fused_computation.1 | convolution fusion | flops 84803584 | bytes 2883584 | tf_op jit(solution)/shard_map/epa,fepb->feab/dot_general | solution.py:81
  156.0 6.3 %copy.462 = f32[4,32,64,64,1]{3,1,0,4,2:T(8,128)} copy(f32[4,32,64,64,1]{2,3,0,1,4:T(8,128)} %convolution_bitcast_fusion) | data formatting | bytes 4194304 | tf_op jit(solution)/shard_map/epa,fepb->feab/transpose | solution.py:81
  162.2 6.2 %copy.464 = f32[4,32,64,64,1]{3,1,4,2,0:T(8,128)} copy(f32[4,32,64,64,1]{2,3,0,1,4:T(8,128)} %convolution_bitcast_fusion) | data formatting | bytes 4194304 | tf_op jit(solution)/shard_map/epa,fepb->feab/transpose | solution.py:81
  168.5 4.5 %convolution_bitcast_fusion.3 = f32[64,64,4,4]{1,3,2,0:T(4,128)S(1)} fusion(f32[4,32,64,64,1]{3,1,0,4,2:T(8,128)} %copy.462, f32[4,32]{1,0:T(4,128)S(1)} %broadcast_subtract_fusion, f32[4,32,4]{1,2,0:T(4,128)S(1)} %fusion.63, f32[32,4]{0,1:T(4,128)S(1)} %fusion.66), kind=kOutput, calls=%fused_computation.8 | convolution fusion | flops 100667392 | bytes 2362368 | tf_op jit(solution)/shard_map/feab,fepr->apbr/dot_general | solution.py:93
  173.0 1.0 fusion.4
  174.2 1.0 broadcast_in_dim_reshape.8
  175.2 5.9 %convolution_bitcast_fusion.1 = f32[4,4,64,4,64]{4,3,1,2,0:T(4,128)S(1)} fusion(f32[4,32,64,64,1]{3,1,4,2,0:T(8,128)} %copy.464, f32[4,32]{1,0:T(4,128)S(1)} %copy-done.27, f32[4,32,4]{1,2,0:T(4,128)S(1)} %fusion.63, f32[32,4]{0,1:T(4,128)S(1)} %fusion.66), kind=kOutput, calls=%fused_computation.5 | convolution fusion | flops 100667392 | bytes 3148800 | tf_op jit(solution)/shard_map/feab,fepr->fapbr/dot_general | solution.py:99
  181.6 2.1 %broadcast_in_dim_reshape.9 = f32[1,1,4,256,256]{4,3,2,1,0:T(8,128)} reshape(f32[4,4,64,4,64]{4,3,2,1,0:T(4,128)S(1)} %copy.454) | data formatting | bytes 2097152 | tf_op jit(solution)/shard_map/broadcast_in_dim;reshape | solution.py:195
  (224 shorter events, 45.6 us)
Async XLA Ops:
  2.3 29.3 %collective-permute-start = (f32[384,1,8]{0,2,1:T(8,128)}, f32[384,1,8]{0,2,1:T(8,128)}, u32[]{:S(2)}, u32[]{:S(2)}) collective-permute-start(f32[384,1,8]{0,2,1:T(8,128)} %get-tuple-element.70), channel_id=1, source_target_pairs={{0,16},{16,32},{32,48},{48,64},{64,80},{80,96},{96,112},{112,128},... | collective-permute-start | bytes 36872 | tf_op jit(solution)/shard_map/ppermute | solution.py:17
  5.4 26.9 %collective-permute-start.1 = (f32[384,1,8]{0,2,1:T(8,128)}, f32[384,1,8]{0,2,1:T(8,128)}, u32[]{:S(2)}, u32[]{:S(2)}) collective-permute-start(f32[384,1,8]{0,2,1:T(8,128)} %get-tuple-element.69), channel_id=1, source_target_pairs={{16,0},{32,16},{48,32},{64,48},{80,64},{96,80},{112,96},{128,112},... | collective-permute-start | bytes 36872 | tf_op jit(solution)/shard_map/ppermute | solution.py:20
  10.0 124.2 %collective-permute-start.12 = (bf16[1,8,4096]{2,1,0:T(8,128)(2,1)}, bf16[1,8,4096]{2,1,0:T(8,128)(2,1)}, u32[]{:S(2)}, u32[]{:S(2)}) collective-permute-start(bf16[1,8,4096]{2,1,0:T(8,128)(2,1)} %get-tuple-element.57), channel_id=1, source_target_pairs={{0,16},{16,32},{32,48},{48,64},{64,80},{80,96},{96,112},{112,128},... | collective-permute-start | bytes 196616 | tf_op jit(solution)/shard_map/ppermute | solution.py:17
  13.6 121.6 %collective-permute-start.13 = (bf16[1,8,4096]{2,1,0:T(8,128)(2,1)}, bf16[1,8,4096]{2,1,0:T(8,128)(2,1)}, u32[]{:S(2)}, u32[]{:S(2)}) collective-permute-start(bf16[1,8,4096]{2,1,0:T(8,128)(2,1)} %get-tuple-element.58), channel_id=1, source_target_pairs={{16,0},{32,16},{48,32},{64,48},{80,64},{96,80},{112,96},{128,112},... | collective-permute-start | bytes 196616 | tf_op jit(solution)/shard_map/ppermute | solution.py:20
  21.4 1.1 copy-start
  22.5 2.1 %copy-start.28 = (s32[1,1,24]{2,1,0:T(1,128)S(1)}, s32[1,1,24]{2,1,0:T(1,128)}, u32[]{:S(2)}) copy-start(s32[1,1,24]{2,1,0:T(1,128)} %param.12) | copy-start | bytes 292
  22.5 3.0 %copy-start.16 = (bf16[1,1,32,4096]{3,2,1,0:T(8,128)(2,1)S(1)}, bf16[1,1,32,4096]{3,2,1,0:T(8,128)(2,1)}, u32[]{:S(2)}) copy-start(bf16[1,1,32,4096]{3,2,1,0:T(8,128)(2,1)} %param.8) | copy-start | bytes 786436
  25.5 2.4 %copy-start.29 = (s32[1,1,32]{2,1,0:T(1,128)S(1)}, s32[1,1,32]{2,1,0:T(1,128)}, u32[]{:S(2)}) copy-start(s32[1,1,32]{2,1,0:T(1,128)} %param.11) | copy-start | bytes 388
  30.5 12.5 %copy-start.6 = (f32[6,4,1,4,4,8]{5,4,3,2,1,0:T(4,128)S(1)}, f32[6,4,1,4,4,8]{5,4,3,2,1,0:T(4,128)}, u32[]{:S(2)}) copy-start(f32[6,4,1,4,4,8]{5,4,3,2,1,0:T(4,128)} %get-tuple-element.50) | copy-start | bytes 36868
  33.1 12.2 %copy-start.21 = (f32[384,6,8]{0,2,1:T(8,128)}, f32[384,6,8]{0,2,1:T(8,128)S(1)}, u32[]{:S(2)}) copy-start(f32[384,6,8]{0,2,1:T(8,128)S(1)} %constant_dynamic-update-slice_fusion) | copy-start | bytes 221188
  33.1 19.0 %collective-permute-start.2 = (f32[384,6,1]{0,2,1:T(1,128)S(1)}, f32[384,6,1]{0,2,1:T(1,128)S(1)}, u32[]{:S(2)}, u32[]{:S(2)}) collective-permute-start(f32[384,6,1]{0,2,1:T(1,128)S(1)} %get-tuple-element.63), channel_id=1, source_target_pairs={{0,1},{1,2},{2,3},{3,4},{4,5},{5,6},{6,7},{7,8},{8,9},{9,10},{10,1... | collective-permute-start | bytes 27656 | tf_op jit(solution)/shard_map/ppermute | solution.py:17
  39.1 13.0 %collective-permute-start.3 = (f32[384,6,1]{0,2,1:T(1,128)S(1)}, f32[384,6,1]{0,2,1:T(1,128)S(1)}, u32[]{:S(2)}, u32[]{:S(2)}) collective-permute-start(f32[384,6,1]{0,2,1:T(1,128)S(1)} %get-tuple-element.64), channel_id=1, source_target_pairs={{1,0},{2,1},{3,2},{4,3},{5,4},{6,5},{7,6},{8,7},{9,8},{10,9},{11,1... | collective-permute-start | bytes 27656 | tf_op jit(solution)/shard_map/ppermute | solution.py:20
  47.4 2.3 %copy-start.11 = (bf16[4,8,4,1,4,64]{5,4,3,2,1,0:T(4,128)(2,1)S(1)}, bf16[4,8,4,1,4,64]{5,4,3,2,1,0:T(4,128)(2,1)}, u32[]{:S(2)}) copy-start(bf16[4,8,4,1,4,64]{5,4,3,2,1,0:T(4,128)(2,1)} %get-tuple-element.53) | copy-start | bytes 196612
  47.4 3.0 %copy-start.10 = (bf16[4,8,4,1,4,64]{5,4,3,2,1,0:T(4,128)(2,1)S(1)}, bf16[4,8,4,1,4,64]{5,4,3,2,1,0:T(4,128)(2,1)}, u32[]{:S(2)}) copy-start(bf16[4,8,4,1,4,64]{5,4,3,2,1,0:T(4,128)(2,1)} %get-tuple-element.54) | copy-start | bytes 196612
  49.7 2.3 %copy-start.22 = (f32[384,6,8]{0,2,1:T(8,128)S(1)}, f32[384,6,8]{0,2,1:T(8,128)}, u32[]{:S(2)}) copy-start(f32[384,6,8]{0,2,1:T(8,128)} %copy-done.21) | copy-start | bytes 221188
  52.0 3.4 %copy-start.8 = (f32[6,16,4,7]{3,1,2,0:T(8,128)S(1)}, f32[6,16,4,7]{3,1,2,0:T(8,128)}, u32[]{:S(2)}) copy-start(f32[6,16,4,7]{3,1,2,0:T(8,128)} %slice.336) | copy-start | bytes 32260
  52.5 3.5 %copy-start.7 = (f32[6,4,1,4,4,8]{5,3,1,4,0,2:T(4,128)S(1)}, f32[6,4,1,4,4,8]{5,3,1,4,0,2:T(4,128)}, u32[]{:S(2)}) copy-start(f32[6,4,1,4,4,8]{5,3,1,4,0,2:T(4,128)} %copy.382) | copy-start | bytes 36868
  54.3 2.0 %copy-start.17 = (f32[6,1,4,4,1,8]{5,3,2,1,0,4:T(4,128)S(1)}, f32[6,1,4,4,1,8]{5,3,2,1,0,4:T(4,128)}, u32[]{:S(2)}) copy-start(f32[6,1,4,4,1,8]{5,3,2,1,0,4:T(4,128)} %get-tuple-element.34) | copy-start | bytes 9220
  55.4 2.6 %copy-start.9 = (f32[6,16,3,8]{3,1,2,0:T(8,128)S(1)}, f32[6,16,3,8]{3,1,2,0:T(8,128)}, u32[]{:S(2)}) copy-start(f32[6,16,3,8]{3,1,2,0:T(8,128)} %slice.328) | copy-start | bytes 27652
  55.8 2.4 %copy-start.1 = (bf16[32,4,64,16]{2,3,1,0:T(8,128)(2,1)S(1)}, bf16[32,4,64,16]{2,3,1,0:T(8,128)(2,1)}, u32[]{:S(2)}) copy-start(bf16[32,4,64,16]{2,3,1,0:T(8,128)(2,1)} %copy.394) | copy-start | bytes 786436
  56.3 3.5 %copy-start.5 = (f32[1,1,6,64,32]{3,4,2,1,0:T(8,128)S(1)}, f32[1,1,6,64,32]{3,4,2,1,0:T(8,128)}, u32[]{:S(2)}) copy-start(f32[1,1,6,64,32]{3,4,2,1,0:T(8,128)} %param.14) | copy-start | bytes 147460
  56.3 3.4 %copy-start.20 = (f32[1,1,6,64,32]{3,4,2,1,0:T(8,128)S(1)}, f32[1,1,6,64,32]{3,4,2,1,0:T(8,128)}, u32[]{:S(2)}) copy-start(f32[1,1,6,64,32]{3,4,2,1,0:T(8,128)} %param.13) | copy-start | bytes 147460
  61.6 6.6 %collective-permute-start.4 = (f32[384,1,8]{0,2,1:T(8,128)S(1)}, f32[384,1,8]{0,2,1:T(8,128)S(1)}, u32[]{:S(2)}, u32[]{:S(2)}) collective-permute-start(f32[384,1,8]{0,2,1:T(8,128)S(1)} %get-tuple-element.68), channel_id=1, source_target_pairs={{0,16},{16,32},{32,48},{48,64},{64,80},{80,96},{96,112},{112,128},... | collective-permute-start | bytes 36872 | tf_op jit(solution)/shard_map/ppermute | solution.py:17
  65.5 7.7 %collective-permute-start.5 = (f32[384,1,8]{0,2,1:T(8,128)S(1)}, f32[384,1,8]{0,2,1:T(8,128)S(1)}, u32[]{:S(2)}, u32[]{:S(2)}) collective-permute-start(f32[384,1,8]{0,2,1:T(8,128)S(1)} %get-tuple-element.67), channel_id=1, source_target_pairs={{16,0},{32,16},{48,32},{64,48},{80,64},{96,80},{112,96},{128,112},... | collective-permute-start | bytes 36872 | tf_op jit(solution)/shard_map/ppermute | solution.py:20
  73.2 12.7 %collective-permute-start.6 = (f32[384,6,1]{0,2,1:T(1,128)S(1)}, f32[384,6,1]{0,2,1:T(1,128)S(1)}, u32[]{:S(2)}, u32[]{:S(2)}) collective-permute-start(f32[384,6,1]{0,2,1:T(1,128)S(1)} %get-tuple-element.61), channel_id=1, source_target_pairs={{0,1},{1,2},{2,3},{3,4},{4,5},{5,6},{6,7},{7,8},{8,9},{9,10},{10,1... | collective-permute-start | bytes 27656 | tf_op jit(solution)/shard_map/ppermute | solution.py:17
  81.3 8.6 %collective-permute-start.7 = (f32[384,6,1]{0,2,1:T(1,128)S(1)}, f32[384,6,1]{0,2,1:T(1,128)S(1)}, u32[]{:S(2)}, u32[]{:S(2)}) collective-permute-start(f32[384,6,1]{0,2,1:T(1,128)S(1)} %get-tuple-element.62), channel_id=1, source_target_pairs={{1,0},{2,1},{3,2},{4,3},{5,4},{6,5},{7,6},{8,7},{9,8},{10,9},{11,1... | collective-permute-start | bytes 27656 | tf_op jit(solution)/shard_map/ppermute | solution.py:20
  93.0 2.2 %copy-start.18 = (f32[6,4,4,4]{2,1,0,3:T(4,128)S(1)}, f32[6,4,4,4]{2,1,0,3:T(4,128)}, u32[]{:S(2)}) copy-start(f32[6,4,4,4]{2,1,0,3:T(4,128)} %get-tuple-element.23) | copy-start | bytes 4612
  95.0 2.9 %copy-start.2 = (bf16[32,4,64,16]{2,3,1,0:T(8,128)(2,1)S(1)}, bf16[32,4,64,16]{2,3,1,0:T(8,128)(2,1)}, u32[]{:S(2)}) copy-start(bf16[32,4,64,16]{2,3,1,0:T(8,128)(2,1)} %copy.394) | copy-start | bytes 786436
  97.3 2.1 %copy-start.23 = (f32[6,64,32]{1,0,2:T(8,128)S(1)}, f32[6,64,32]{1,0,2:T(8,128)}, u32[]{:S(2)}) copy-start(f32[6,64,32]{1,0,2:T(8,128)} %get-tuple-element.83) | copy-start | bytes 147460
  97.3 2.1 %copy-start.26 = (f32[64,32]{0,1:T(8,128)S(1)}, f32[64,32]{0,1:T(8,128)}, u32[]{:S(2)}) copy-start(f32[64,32]{0,1:T(8,128)} %get-tuple-element.72) | copy-start | bytes 24580
  101.2 7.5 %collective-permute-start.8 = (f32[384,1,8]{0,2,1:T(8,128)S(1)}, f32[384,1,8]{0,2,1:T(8,128)S(1)}, u32[]{:S(2)}, u32[]{:S(2)}) collective-permute-start(f32[384,1,8]{0,2,1:T(8,128)S(1)} %get-tuple-element.66), channel_id=1, source_target_pairs={{0,16},{16,32},{32,48},{48,64},{64,80},{80,96},{96,112},{112,128},... | collective-permute-start | bytes 36872 | tf_op jit(solution)/shard_map/ppermute | solution.py:17
  106.4 4.4 %collective-permute-start.9 = (f32[384,1,8]{0,2,1:T(8,128)S(1)}, f32[384,1,8]{0,2,1:T(8,128)S(1)}, u32[]{:S(2)}, u32[]{:S(2)}) collective-permute-start(f32[384,1,8]{0,2,1:T(8,128)S(1)} %get-tuple-element.65), channel_id=1, source_target_pairs={{16,0},{32,16},{48,32},{64,48},{80,64},{96,80},{112,96},{128,112},... | collective-permute-start | bytes 36872 | tf_op jit(solution)/shard_map/ppermute | solution.py:20
  110.8 9.5 %collective-permute-start.10 = (f32[384,6,1]{0,2,1:T(1,128)S(1)}, f32[384,6,1]{0,2,1:T(1,128)S(1)}, u32[]{:S(2)}, u32[]{:S(2)}) collective-permute-start(f32[384,6,1]{0,2,1:T(1,128)S(1)} %get-tuple-element.59), channel_id=1, source_target_pairs={{0,1},{1,2},{2,3},{3,4},{4,5},{5,6},{6,7},{7,8},{8,9},{9,10},{10,1... | collective-permute-start | bytes 27656 | tf_op jit(solution)/shard_map/ppermute | solution.py:17
  116.1 8.6 %collective-permute-start.11 = (f32[384,6,1]{0,2,1:T(1,128)S(1)}, f32[384,6,1]{0,2,1:T(1,128)S(1)}, u32[]{:S(2)}, u32[]{:S(2)}) collective-permute-start(f32[384,6,1]{0,2,1:T(1,128)S(1)} %get-tuple-element.60), channel_id=1, source_target_pairs={{1,0},{2,1},{3,2},{4,3},{5,4},{6,5},{7,6},{8,7},{9,8},{10,9},{11,1... | collective-permute-start | bytes 27656 | tf_op jit(solution)/shard_map/ppermute | solution.py:20
  127.7 2.2 %copy-start.19 = (f32[6,4,4,4]{2,1,0,3:T(4,128)S(1)}, f32[6,4,4,4]{2,1,0,3:T(4,128)}, u32[]{:S(2)}) copy-start(f32[6,4,4,4]{2,1,0,3:T(4,128)} %get-tuple-element.21) | copy-start | bytes 4612
  129.7 2.9 %copy-start.3 = (bf16[32,4,64,16]{2,3,1,0:T(8,128)(2,1)S(1)}, bf16[32,4,64,16]{2,3,1,0:T(8,128)(2,1)}, u32[]{:S(2)}) copy-start(bf16[32,4,64,16]{2,3,1,0:T(8,128)(2,1)} %copy.394) | copy-start | bytes 786436
  132.5 8.7 %copy-start.24 = (f32[6,64,32]{1,0,2:T(8,128)S(1)}, f32[6,64,32]{1,0,2:T(8,128)}, u32[]{:S(2)}) copy-start(f32[6,64,32]{1,0,2:T(8,128)} %get-tuple-element.83) | copy-start | bytes 147460
  132.5 8.7 %copy-start.25 = (f32[64,32]{0,1:T(8,128)S(1)}, f32[64,32]{0,1:T(8,128)}, u32[]{:S(2)}) copy-start(f32[64,32]{0,1:T(8,128)} %get-tuple-element.71) | copy-start | bytes 24580
  132.6 8.5 %copy-start.30 = (f32[6,64,32]{1,0,2:T(8,128)S(1)}, f32[6,64,32]{1,0,2:T(8,128)}, u32[]{:S(2)}) copy-start(f32[6,64,32]{1,0,2:T(8,128)} %get-tuple-element.85) | copy-start | bytes 147460
  136.2 6.6 %collective-permute-start.14 = (bf16[6,1,4096]{2,0,1:T(8,128)(2,1)S(1)}, bf16[6,1,4096]{2,0,1:T(8,128)(2,1)S(1)}, u32[]{:S(2)}, u32[]{:S(2)}) collective-permute-start(bf16[6,1,4096]{2,0,1:T(8,128)(2,1)S(1)} %get-tuple-element.55), channel_id=1, source_target_pairs={{0,1},{1,2},{2,3},{3,4},{4,5},{5,6},{6,7},{7,8},{8,9},{9,10},{10,1... | collective-permute-start | bytes 147464 | tf_op jit(solution)/shard_map/ppermute | solution.py:17
  139.2 9.2 %collective-permute-start.15 = (bf16[6,1,4096]{2,0,1:T(8,128)(2,1)S(1)}, bf16[6,1,4096]{2,0,1:T(8,128)(2,1)S(1)}, u32[]{:S(2)}, u32[]{:S(2)}) collective-permute-start(bf16[6,1,4096]{2,0,1:T(8,128)(2,1)S(1)} %get-tuple-element.56), channel_id=1, source_target_pairs={{1,0},{2,1},{3,2},{4,3},{5,4},{6,5},{7,6},{8,7},{9,8},{10,9},{11,1... | collective-permute-start | bytes 147464 | tf_op jit(solution)/shard_map/ppermute | solution.py:20
  142.8 9.7 %copy-start.13 = (bf16[4,7,16,64]{3,2,1,0:T(8,128)(2,1)S(1)}, bf16[4,7,16,64]{3,2,1,0:T(8,128)(2,1)}, u32[]{:S(2)}) copy-start(bf16[4,7,16,64]{3,2,1,0:T(8,128)(2,1)} %slice.376) | copy-start | bytes 172036
  148.9 3.6 %copy-start.12 = (bf16[4,7,16,64]{3,2,1,0:T(8,128)(2,1)S(1)}, bf16[4,7,16,64]{3,2,1,0:T(8,128)(2,1)}, u32[]{:S(2)}) copy-start(bf16[4,7,16,64]{3,2,1,0:T(8,128)(2,1)} %slice.378) | copy-start | bytes 172036
  148.9 3.7 %copy-start.15 = (bf16[3,8,1,4,4,64]{5,4,3,2,1,0:T(4,128)(2,1)S(1)}, bf16[3,8,1,4,4,64]{5,4,3,2,1,0:T(4,128)(2,1)}, u32[]{:S(2)}) copy-start(bf16[3,8,1,4,4,64]{5,4,3,2,1,0:T(4,128)(2,1)} %get-tuple-element.51) | copy-start | bytes 147460
  148.9 3.7 %copy-start.14 = (bf16[3,8,1,4,4,64]{5,4,3,2,1,0:T(4,128)(2,1)S(1)}, bf16[3,8,1,4,4,64]{5,4,3,2,1,0:T(4,128)(2,1)}, u32[]{:S(2)}) copy-start(bf16[3,8,1,4,4,64]{5,4,3,2,1,0:T(4,128)(2,1)} %get-tuple-element.52) | copy-start | bytes 147460
  148.9 3.7 %copy-start.4 = (bf16[32,64,64,1]{2,1,0,3:T(8,128)(2,1)S(1)}, bf16[32,64,64,1]{2,1,0,3:T(8,128)(2,1)}, u32[]{:S(2)}) copy-start(bf16[32,64,64,1]{2,1,0,3:T(8,128)(2,1)} %reshape.306) | copy-start | bytes 786436
  174.1 1.2 copy-start.27
where the time goes:
time: 185 us; the launch traced here: 184 us
  local copies, waits for them, and re-layouts  66.9 us (36%)
  starting transfers between devices  55.8 us (30%)
  matrix products  23.9 us (13%)
  waiting for transfers between devices  21.1 us (11%)
  other arithmetic  11.4 us (6%)
  between operations  4.66 us (3%)
    ppermute x8, starting transfers between devices, with_halo(): lax.ppermute(lax.slice_in_dim(block, block.shape[dim] - width, None, axis...  38.1 us
    ppermute x8, waiting for transfers between devices, with_halo(): lax.ppermute(lax.slice_in_dim(block, 0, width, axis=dim), axis, backward)  21.1 us
    ppermute x8, starting transfers between devices, with_halo(): lax.ppermute(lax.slice_in_dim(block, 0, width, axis=dim), axis, backward)  17.7 us
    transpose x2, local copies, waits for them, and re-layouts, galerkin(): jnp.einsum('epa,fepb->feab', prolong, coupled, preferred_element_type=jnp...  12.5 us
    unnamed x74, local copies, waits for them, and re-layouts  5.96 us
    dot_general x1, matrix products, galerkin(): jnp.einsum('feab,fepr->fapbr', pair_face * outside[:, :, None, None], w_f...  5.88 us
    dot_general x3, matrix products, operate_brick(): jnp.einsum('efpt,fnte->npe', couple_wide, near_rows, precision=lax.Precis...  4.54 us
    dot_general x1, matrix products, galerkin(): jnp.einsum('feab,fepr->apbr', pair_face * (1.0 - outside)[:, :, None, Non...  4.54 us
  transfers between devices with their start and end apart: 16, of which 5 were waited for; matrix products, arithmetic and copies ran while one was open for 35% of the time, Pallas kernels for 0%

commit v1 on v0

v1 whole, which is shorter than its diff:
```python
import jax
import jax.numpy as jnp
from jax import lax
from jax.experimental import pallas as pl
from jax.experimental.pallas import tpu as pltpu
from jax.sharding import PartitionSpec as P

EX, EY, NE, NRHS = 4, 8, 32, 6
ROWS = NRHS * NE
F32, BF16 = jnp.float32, jnp.bfloat16
VMEM = pl.BlockSpec(memory_space=pltpu.VMEM)
SMEM = pl.BlockSpec(memory_space=pltpu.SMEM)
NT = (((1,), (1,)), ((), ()))
NN = (((1,), (0,)), ((), ()))


def dot(a, b, dims=NN):
    return lax.dot_general(a, b, dims, preferred_element_type=F32)


def iota(shape, dim):
    return lax.broadcasted_iota(jnp.int32, shape, dim)


def split(x):
    hi = x.astype(BF16)
    return hi, (x - hi.astype(F32)).astype(BF16)


def trace_matrix():
    q, lane = iota((64, 128), 0), iota((64, 128), 1)
    t = lane % 16
    f = lane // 16 - 4
    along_y = 16 * (t // 4) + t % 4
    source = jnp.where(f == 0, 48 + t, jnp.where(f == 1, t, jnp.where(f == 2, along_y + 12, along_y)))
    return (q == jnp.where(f < 0, lane, source)).astype(F32).astype(BF16)


def with_traces(v):
    hi, lo = split(v)
    pick = trace_matrix()
    return dot(hi, pick) + dot(lo, pick)


def pack_field(rows):
    hi, lo = split(rows)
    return jnp.where(
        iota(rows.shape, 1) >= 64, hi.astype(F32), pltpu.roll(lo.astype(F32), 64, 1)
    ).astype(BF16)


def unpack_field(message):
    wide = message.astype(F32)
    return wide + pltpu.roll(wide, 64, 1)


def edges_x(traces, low):
    start = 0 if low else NE - EY
    return jnp.concatenate([traces[n * NE + start : n * NE + start + EY] for n in range(NRHS)], 0)


def field_messages(traces, t_ref):
    t_ref[...] = traces
    pad = jnp.zeros((8, 128), F32)
    return (
        pack_field(edges_x(traces, True)),
        pack_field(edges_x(traces, False)),
        pack_field(jnp.concatenate([t_ref[pl.ds(0, 24, stride=8), :], pad], 0)),
        pack_field(jnp.concatenate([t_ref[pl.ds(7, 24, stride=8), :], pad], 0)),
    )


def parities():
    return lax.axis_index("bx") % 2, lax.axis_index("by") % 2


def swap(even, first, second):
    a, b = first.astype(F32), second.astype(F32)
    return (
        jnp.where(even, a, b).astype(first.dtype),
        jnp.where(even, b, a).astype(first.dtype),
    )


def store_messages(outs, first_row, messages):
    px, py = parities()
    x_low, x_high, y_low, y_high = messages
    x_even, x_odd = swap(px == 0, x_high, x_low)
    y_even, y_odd = swap(py == 0, y_high, y_low)
    for out, value in zip(outs, (x_even, x_odd, y_even, y_odd)):
        out[first_row : first_row + value.shape[0], :] = value


def received(refs, first_row, sizes):
    px, py = parities()
    x_even, x_odd, y_even, y_odd = [
        ref[first_row : first_row + size, :] for ref, size in zip(refs, sizes)
    ]
    x_high, x_low = swap(px == 0, x_even, x_odd)
    y_high, y_low = swap(py == 0, y_even, y_odd)
    return x_low, x_high, y_low, y_high


FIELD_SIZES = (48, 48, 32, 32)
TENT_SIZES = (64, 64, 64, 64)


def pack_kernel(guess, tent, t16, plus_y, minus_y, xe, xo, ye, yo, stage, t32, traces_ref):
    lane = iota((256, 128), 1)
    for k in range(4):
        for ph in range(8):
            chunk = tent[:, (ph * 4 + k) * 128 : (ph * 4 + k + 1) * 128].astype(F32)
            stage[k, pl.ds(ph, NE, stride=8), :] = chunk
    for k in range(4):
        both = stage[k]
        other = pltpu.roll(both, 64, 1)
        t32[pl.ds(2 * k, 256, stride=8), :] = jnp.where(lane < 64, both, other)
        t32[pl.ds(2 * k + 1, 256, stride=8), :] = jnp.where(lane < 64, other, both)
    t16[...] = t32[...].astype(BF16)
    sub = iota((8, 128), 0)
    for e in range(NE):
        plus, minus = [], []
        for h in range(2):
            base = e * 64 + 32 * h
            a, b = t32[base + 8 : base + 16, :], t32[base + 24 : base + 32, :]
            plus.append(jnp.where(sub < 4, pltpu.roll(a, 4, 0), b))
            a, b = t32[base : base + 8, :], t32[base + 16 : base + 24, :]
            minus.append(jnp.where(sub < 4, a, pltpu.roll(b, 4, 0)))
        plus_y[e * 16 : e * 16 + 16, :] = jnp.concatenate(plus, 0).astype(BF16)
        minus_y[e * 16 : e * 16 + 16, :] = jnp.concatenate(minus, 0).astype(BF16)

    lane16 = iota((16, 128), 1)

    def tent_x(first, row):
        parts = []
        for iy in range(4):
            a = (first + iy) * 64 + row
            b = (first + iy + 4) * 64 + row
            parts.append(jnp.where(lane16 < 64, t32[a : a + 16, :], t32[b : b + 16, :]))
        return jnp.concatenate(parts, 0).astype(BF16)

    def tent_y(ref, iy):
        return jnp.concatenate([ref[(8 * ix + iy) * 16 : (8 * ix + iy) * 16 + 16, :] for ix in range(4)], 0)

    fields = field_messages(with_traces(guess[...].reshape(ROWS, 64)), traces_ref)
    tents = (tent_x(0, 0), tent_x(24, 48), tent_y(minus_y, 0), tent_y(plus_y, 7))
    store_messages((xe, xo, ye, yo), 0, tents)
    store_messages((xe, xo, ye, yo), 64, fields)


def prep_kernel(blocks, faces, w, inverse, stage, fstage, w32):
    lane = iota((256, 128), 1)
    lane_e = iota((NE, 128), 1)
    diag = jnp.zeros((NE, 128), F32)
    for k in range(4):
        for ph in range(8):
            c = ph * 4 + k
            chunk = blocks[:, c * 128 : (c + 1) * 128].astype(F32)
            diag = diag + jnp.where((lane_e == 2 * c) | (lane_e == 65 + 2 * c), chunk, 0.0)
            stage[k, pl.ds(ph, NE, stride=8), :] = chunk
    diag = diag + pltpu.roll(diag, 64, 1)
    inverse[...] = 1.0 / diag[:, :64]
    for f in range(4):
        for ph in range(8):
            c = f * 8 + ph
            fstage[f, pl.ds(ph, NE, stride=8), :] = faces[:, c * 128 : (c + 1) * 128].astype(F32)
    folded = jnp.concatenate([fstage[f].astype(BF16) for f in range(4)], 1)
    row, col = iota((512, 128), 0), iota((512, 128), 1)
    face_of, lo_of, t_of = row // 128, (row // 16) % 8, row % 16
    target = 64 + face_of * 16 + t_of
    for k in range(4):
        both = stage[k]
        other = pltpu.roll(both, 64, 1)
        for s, part in enumerate((both, other)):
            p_lo = 2 * k + s
            pick = ((col == target) & (lo_of == p_lo)).astype(F32).astype(BF16)
            coupled = dot(folded, pick)
            w32[pl.ds(p_lo, 256, stride=8), :] = jnp.where(lane < 64, part, coupled)
    w[...] = w32[...].astype(BF16)


def apply(v, ghosts, w, traces, x_ref, ghost_low, ghost_high, a_ref):
    x_low, x_high, y_low, y_high = [unpack_field(g) for g in ghosts]
    ghost_low[pl.ds(0, 24, stride=8), :] = y_low[:24]
    ghost_high[pl.ds(7, 24, stride=8), :] = y_high[:24]
    lane, row = iota((NE, 128), 1), iota((NE, 128), 0)
    for n in range(NRHS):
        own = traces[n * NE : (n + 1) * NE]
        from_low_x = jnp.concatenate([x_low[n * 8 : n * 8 + 8], own[:24]], 0)
        from_high_x = jnp.concatenate([own[8:], x_high[n * 8 : n * 8 + 8]], 0)
        from_low_y = jnp.where(
            row % 8 == 0, ghost_low[n * NE : (n + 1) * NE, :], pltpu.roll(own, 1, 0)
        )
        from_high_y = jnp.where(
            row % 8 == 7, ghost_high[n * NE : (n + 1) * NE, :], pltpu.roll(own, NE - 1, 0)
        )
        x_ref[n * NE : (n + 1) * NE, :] = jnp.where(
            lane < 64,
            own,
            jnp.where(
                lane < 80,
                from_low_x,
                jnp.where(lane < 96, from_high_x, jnp.where(lane < 112, from_low_y, from_high_y)),
            ),
        )
    x_ref[ROWS:, :] = jnp.zeros((64, 128), F32)
    for e in range(NE):
        hi, lo = split(x_ref[pl.ds(e, 8, stride=NE), :])
        out = dot(jnp.concatenate([hi, lo], 0), w[e * 64 : e * 64 + 64, :], NT)
        a_ref[pl.ds(e, 8, stride=NE), 0:64] = out[:8] + out[8:]
    return a_ref[:ROWS, 0:64]


def factors(bounds):
    low, high = bounds[0:1, 0:1], bounds[0:1, 1:2]
    centre = 0.5 * (high + low)
    half_width = 0.5 * (high - low)
    spread = centre / half_width
    first = 1.0 / spread
    second = 1.0 / (2.0 * spread - first)
    third = 1.0 / (2.0 * spread - second)
    return centre, half_width, first, second, third


def expand(inverse):
    return jnp.concatenate([inverse] * NRHS, 0)


def first_kernel(guess, rhs, w, inverse, bounds, g0, g1, g2, g3, residue, update, answer,
                 xe, xo, ye, yo, x_ref, low_ref, high_ref, a_ref):
    centre = factors(bounds)[0]
    ghosts = received((g0, g1, g2, g3), 64, FIELD_SIZES)
    v = guess[...].reshape(ROWS, 64)
    applied = apply(v, ghosts, w, with_traces(v), x_ref, low_ref, high_ref, a_ref)
    r = rhs[...].reshape(ROWS, 64) - applied
    u = expand(inverse[...]) * r / centre
    residue[...] = r
    update[...] = u
    answer[...] = v + u
    store_messages((xe, xo, ye, yo), 0, field_messages(with_traces(u), low_ref))


def next_kernel(step, residue, update, answer, w, inverse, bounds, g0, g1, g2, g3, *refs):
    centre, half_width, first, second, third = factors(bounds)
    ghosts = received((g0, g1, g2, g3), 0, FIELD_SIZES)
    u = update[...]
    x_ref, low_ref, high_ref, a_ref = refs[-4:]
    applied = apply(u, ghosts, w, with_traces(u), x_ref, low_ref, high_ref, a_ref)
    r = residue[...] - applied
    factor, new = (first, second) if step == 0 else (second, third)
    u = new * factor * u + (2.0 * new / half_width) * expand(inverse[...]) * r
    x = answer[...] + u
    if step == 0:
        residue_out, update_out, answer_out, xe, xo, ye, yo = refs[:-4]
        residue_out[...] = r
        update_out[...] = u
        answer_out[...] = x
        store_messages((xe, xo, ye, yo), 0, field_messages(with_traces(u), low_ref))
    else:
        refs[0][...] = x.reshape(NRHS, NE, 64)


def galerkin_kernel(labels, side_labels, t16, plus_y, minus_y, w, g0, g1, g2, g3, local, ghost,
                    tt, xlow, xhigh, ylow, yhigh, masks, big, side):
    lane16 = iota((16, 128), 1)
    x_low, x_high, y_low, y_high = received((g0, g1, g2, g3), 0, TENT_SIZES)
    for ref, value in ((xlow, x_low), (xhigh, x_high)):
        wide = value.astype(F32)
        other = pltpu.roll(wide, 64, 1)
        lane64 = iota((64, 128), 1)
        ref[0:64, :] = jnp.where(lane64 < 64, wide, other).astype(BF16)
        ref[64:128, :] = jnp.where(lane64 < 64, other, wide).astype(BF16)
    ylow[...] = y_low
    yhigh[...] = y_high
    lane256 = iota((16, 256), 1)
    for b in range(4):
        masks[b * 16 : b * 16 + 16, :] = (lane256 // 64 == b).astype(F32).astype(BF16)
    lane128 = iota((64, 128), 1)
    for pair in range(NE // 2):
        turned = t16[pair * 128 : pair * 128 + 128, :].astype(F32).T[:64]
        first, second = labels[2 * pair], labels[2 * pair + 1]
        for a in range(4):
            keep = jnp.where(
                lane128 < 64,
                jnp.where(first == a, 1.0, 0.0),
                jnp.where(second == a, 1.0, 0.0),
            )
            tt[a * 64 : a * 64 + 64, pair * 128 : pair * 128 + 128] = (turned * keep).astype(BF16)
    side[...] = jnp.zeros_like(side)
    z = lambda count: jnp.zeros((count, 128), BF16)

    def masked(piece, label):
        mask = masks[pl.ds(pl.multiple_of(label * 16, 16), 16), :]
        return jnp.concatenate([piece, piece], 1) * jnp.concatenate([mask] * 4, 0)

    def row_of_elements(ix, carry):
        for iy in range(EY):
            e = ix * EY + iy
            own = pl.ds(pl.multiple_of(e * 64, 64), 64)
            before = pl.multiple_of(jnp.maximum(e - 8, 0) * 64, 64)
            after = pl.multiple_of(jnp.minimum(e + 8, 31) * 64, 64)
            rows0 = jnp.where(
                ix == 0,
                xlow[iy * 16 : iy * 16 + 16, :].astype(F32),
                t16[pl.ds(before + 48, 16), :].astype(F32),
            ).astype(BF16)
            rows1 = jnp.where(
                ix == 3,
                xhigh[iy * 16 : iy * 16 + 16, :].astype(F32),
                t16[pl.ds(after, 16), :].astype(F32),
            ).astype(BF16)
            edge = pl.ds(pl.multiple_of(ix * 16, 16), 16)
            rows2 = ylow[edge, :] if iy == 0 else plus_y[pl.ds(pl.multiple_of((e - 1) * 16, 16), 16), :]
            rows3 = yhigh[edge, :] if iy == 7 else minus_y[pl.ds(pl.multiple_of((e + 1) * 16, 16), 16), :]
            columns = [jnp.concatenate([t16[own, :], z(64)], 0)]
            for f, rows in enumerate((rows0, rows1, rows2, rows3)):
                parts = [z(64 + 16 * f), rows] + ([z(48 - 16 * f)] if f < 3 else [])
                columns.append(jnp.concatenate(parts, 0))
            pieces = dot(w[own, :], jnp.concatenate(columns, 1)).astype(BF16)
            piece = lambda s: pieces[:, s * 128 : s * 128 + 128]
            label0 = jnp.where(ix == 0, side_labels[iy], labels[jnp.maximum(e - 8, 0)])
            label1 = jnp.where(ix == 3, side_labels[8 + iy], labels[jnp.minimum(e + 8, 31)])
            big[0, own, :] = masked(piece(0), labels[e])
            big[1, own, :] = masked(piece(1), label0)
            big[2, own, :] = masked(piece(2), label1)
            if iy == 0:
                big[3, own, :] = jnp.zeros((64, 256), BF16)
                side[0, pl.ds(pl.multiple_of(ix * 128, 128), 64), :] = masked(piece(3), side_labels[16 + ix])
            else:
                big[3, own, :] = masked(piece(3), labels[e - 1])
            if iy == 7:
                big[4, own, :] = jnp.zeros((64, 256), BF16)
                side[1, pl.ds(pl.multiple_of(ix * 128, 128) + 64, 64), :] = masked(piece(4), side_labels[20 + ix])
            else:
                big[4, own, :] = masked(piece(4), labels[e + 1])
        return carry

    lax.fori_loop(0, EX, row_of_elements, 0)
    local[...] = (
        dot(tt[...], big[0])
        + dot(tt[:, 512:], big[1, 512:, :])
        + dot(tt[:, :1536], big[2, :1536, :])
        + dot(tt[...], big[3])
        + dot(tt[...], big[4])
    )
    ghost[0] = dot(tt[:, :512], big[1, :512, :])
    ghost[1] = dot(tt[:, 1536:], big[2, 1536:, :])
    for f in range(2):
        lhs = jnp.concatenate(
            [tt[:, (4 * ix + 3 * f) * 128 : (4 * ix + 3 * f + 1) * 128] for ix in range(4)], 1
        )
        ghost[2 + f] = dot(lhs, side[f])


def call(kernel, outs, scratch, operands, flops, moved, specs=None):
    return pl.pallas_call(
        kernel,
        out_shape=outs,
        in_specs=specs or [VMEM] * len(operands),
        out_specs=jax.tree.map(lambda _: VMEM, outs),
        scratch_shapes=scratch,
        cost_estimate=pl.CostEstimate(flops=flops, bytes_accessed=moved, transcendentals=0),
        compiler_params=pltpu.CompilerParams(vmem_limit_bytes=48 * 1024 * 1024),
    )(*operands)


def exchange(messages):
    out = []
    for message, axis, first in zip(messages, ("bx", "bx", "by", "by"), (0, 1, 0, 1)):
        pairs = []
        for i in range(first, lax.axis_size(axis) - 1, 2):
            pairs += [(i, i + 1), (i + 1, i)]
        out.append(lax.ppermute(message, axis, pairs))
    return out


def shaped(*shape, dtype=F32):
    return jax.ShapeDtypeStruct(shape, dtype)


FIELD_SCRATCH = [
    pltpu.VMEM((ROWS + 64, 128), F32),
    pltpu.VMEM((ROWS, 128), F32),
    pltpu.VMEM((ROWS, 128), F32),
    pltpu.VMEM((ROWS + 64, 128), F32),
]


def on_device(blocks, faces, tentative, aggregate, ghost_labels, rhs, guess, bounds):
    blocks, faces, tentative = [a.reshape(NE, 4096) for a in (blocks, faces, tentative)]
    rhs = jnp.swapaxes(rhs[0, 0], 1, 2)
    guess = jnp.swapaxes(guess[0, 0], 1, 2)
    bounds = bounds.reshape(1, 2)
    message = lambda rows: [shaped(r, 128, dtype=BF16) for r in rows]
    both = [f + t for f, t in zip(FIELD_SIZES, TENT_SIZES)]
    t16, plus_y, minus_y, *sends = call(
        pack_kernel,
        [shaped(2048, 128, dtype=BF16), shaped(512, 128, dtype=BF16), shaped(512, 128, dtype=BF16)] + message(both),
        [pltpu.VMEM((4, 256, 128), F32), pltpu.VMEM((2048, 128), F32), pltpu.VMEM((ROWS, 128), F32)],
        (guess, tentative), 10**6, 2**20,
    )
    first_ghosts = exchange(sends)
    w, inverse = call(
        prep_kernel,
        [shaped(2048, 128, dtype=BF16), shaped(NE, 64)],
        [pltpu.VMEM((4, 256, 128), F32), pltpu.VMEM((4, 256, 128), F32), pltpu.VMEM((2048, 128), F32)],
        (blocks, faces), 10**8, 2**20,
    )
    field = shaped(ROWS, 64)
    residue, update, answer, *sends = call(
        first_kernel, [field] * 3 + message(FIELD_SIZES), FIELD_SCRATCH,
        (guess, rhs, w, inverse, bounds, *first_ghosts), 10**8, 2**20,
    )
    ghosts = exchange(sends)
    local, ghost = call(
        galerkin_kernel,
        [shaped(256, 256), shaped(4, 256, 256)],
        [
            pltpu.VMEM((256, 2048), BF16),
            pltpu.VMEM((128, 128), BF16),
            pltpu.VMEM((128, 128), BF16),
            pltpu.VMEM((64, 128), BF16),
            pltpu.VMEM((64, 128), BF16),
            pltpu.VMEM((64, 256), BF16),
            pltpu.VMEM((5, 2048, 256), BF16),
            pltpu.VMEM((2, 512, 256), BF16),
        ],
        (aggregate.reshape(NE), ghost_labels.reshape(24), t16, plus_y, minus_y, w, *first_ghosts),
        4 * 10**9, 4 * 2**20,
        [SMEM, SMEM] + [VMEM] * 8,
    )
    residue, update, answer, *sends = call(
        lambda *refs: next_kernel(0, *refs), [field] * 3 + message(FIELD_SIZES), FIELD_SCRATCH,
        (residue, update, answer, w, inverse, bounds, *ghosts), 10**8, 2**20,
    )
    ghosts = exchange(sends)
    (smoothed,) = call(
        lambda *refs: next_kernel(1, *refs), [shaped(NRHS, NE, 64)], FIELD_SCRATCH,
        (residue, update, answer, w, inverse, bounds, *ghosts), 10**8, 2**20,
    )
    return jnp.swapaxes(smoothed, 1, 2)[None, None], local[None, None], ghost[None, None]


def solution(mesh):
    b = lambda extra: P("bx", "by", *([None] * extra))
    return jax.shard_map(
        on_device,
        mesh=mesh,
        in_specs=(b(2), b(2), b(2), b(1), b(1), b(3), b(3), P()),
        out_specs=(b(3), b(2), b(3)),
        check_vma=False,
    )
```

time: 185 us -> 64 us (0.35)
  the two profiles are of different devices: /device:TPU:121 before, /device:TPU:102 now
where the time goes in v1:
time: 64 us; the launch traced here: 63.5 us
  starting transfers between devices  45 us (70%)
  Pallas kernels  9.17 us (14%)
  waiting for transfers between devices  4.35 us (7%)
  local copies, waits for them, and re-layouts  4.09 us (6%)
  between operations  0.85 us (1%)
    ppermute x12, starting transfers between devices, exchange(): out.append(lax.ppermute(message, axis, pairs))  45 us
    pallas_call x6, Pallas kernels, call(): pl.pallas_call(kernel, out_shape=outs, in_specs=specs or [VMEM] * len(ope...  9.17 us
    ppermute x12, waiting for transfers between devices, exchange(): out.append(lax.ppermute(message, axis, pairs))  4.35 us
    unnamed x18, local copies, waits for them, and re-layouts  4.09 us
  transfers between devices with their start and end apart: 12, of which 2 were waited for; matrix products, arithmetic and copies ran while one was open for 0% of the time, Pallas kernels for 9%

profile of v1, /device:TPU:102, one launch (start us, length us, event | category | flops | bytes accessed | tf_op | source)
XLA Modules:
  0.0 63.5 jit_solution(12616566104677630192)
XLA Ops:
  0.6 0.0 copy-start
  0.6 0.9 %copy-done = f32[1,1,6,64,32]{3,4,2,1,0:T(8,128)S(1)} copy-done((f32[1,1,6,64,32]{3,4,2,1,0:T(8,128)S(1)}, f32[1,1,6,64,32]{3,4,2,1,0:T(8,128)}, u32[]{:S(2)}) %copy-start) | copy-done | bytes 49176
  1.5 0.0 copy-start.2
  1.5 0.9 %copy-done.2 = bf16[1,1,32,4096]{3,2,1,0:T(8,128)(2,1)S(1)} copy-done((bf16[1,1,32,4096]{3,2,1,0:T(8,128)(2,1)S(1)}, bf16[1,1,32,4096]{3,2,1,0:T(8,128)(2,1)}, u32[]{:S(2)}) %copy-start.2) | copy-done | bytes 262168
  2.5 0.0 copy-start.3
  2.5 0.4 shard_map.104
  2.9 2.7 %collective-permute-start = (bf16[112,128]{1,0:T(8,128)(2,1)S(1)}, bf16[112,128]{1,0:T(8,128)(2,1)S(1)}, u32[]{:S(2)}, u32[]{:S(2)}) collective-permute-start(bf16[112,128]{1,0:T(8,128)(2,1)S(1)} %get-tuple-element.30), channel_id=1, source_target_pairs={{0,16},{16,0},{32,48},{48,32},{64,80},{80,64},{96,112},{112,96},{1... | collective-permute-start | bytes 86024 | tf_op jit(solution)/shard_map/ppermute | solution.py:373
  5.7 5.7 %collective-permute-start.1 = (bf16[112,128]{1,0:T(8,128)(2,1)S(1)}, bf16[112,128]{1,0:T(8,128)(2,1)S(1)}, u32[]{:S(2)}, u32[]{:S(2)}) collective-permute-start(bf16[112,128]{1,0:T(8,128)(2,1)S(1)} %get-tuple-element.31), channel_id=1, source_target_pairs={{16,32},{32,16},{48,64},{64,48},{80,96},{96,80},{112,128},{128,112... | collective-permute-start | bytes 86024 | tf_op jit(solution)/shard_map/ppermute | solution.py:373
  11.3 1.9 %collective-permute-start.2 = (bf16[96,128]{1,0:T(8,128)(2,1)S(1)}, bf16[96,128]{1,0:T(8,128)(2,1)S(1)}, u32[]{:S(2)}, u32[]{:S(2)}) collective-permute-start(bf16[96,128]{1,0:T(8,128)(2,1)S(1)} %get-tuple-element.32), channel_id=1, source_target_pairs={{0,1},{1,0},{2,3},{3,2},{4,5},{5,4},{6,7},{7,6},{8,9},{9,8},{10,11... | collective-permute-start | bytes 73736 | tf_op jit(solution)/shard_map/ppermute | solution.py:373
  13.3 5.9 %collective-permute-start.3 = (bf16[96,128]{1,0:T(8,128)(2,1)S(1)}, bf16[96,128]{1,0:T(8,128)(2,1)S(1)}, u32[]{:S(2)}, u32[]{:S(2)}) collective-permute-start(bf16[96,128]{1,0:T(8,128)(2,1)S(1)} %get-tuple-element.33), channel_id=1, source_target_pairs={{1,2},{2,1},{3,4},{4,3},{5,6},{6,5},{7,8},{8,7},{9,10},{10,9},{11,... | collective-permute-start | bytes 73736 | tf_op jit(solution)/shard_map/ppermute | solution.py:373
  19.1 0.0 copy-done.3
  19.1 0.0 copy-start.4
  19.2 0.9 %copy-done.4 = bf16[1,1,32,4096]{3,2,1,0:T(8,128)(2,1)S(1)} copy-done((bf16[1,1,32,4096]{3,2,1,0:T(8,128)(2,1)S(1)}, bf16[1,1,32,4096]{3,2,1,0:T(8,128)(2,1)}, u32[]{:S(2)}) %copy-start.4) | copy-done | bytes 262168
  20.1 0.0 copy-start.1
  20.1 0.0 copy-start.5
  20.1 0.8 %shard_map.103 = (bf16[2048,128]{1,0:T(8,128)(2,1)S(1)}, f32[32,64]{1,0:T(8,128)S(1)}) custom-call(bf16[32,4096]{1,0:T(8,128)(2,1)S(1)} %bitcast.20, bf16[32,4096]{1,0:T(8,128)(2,1)S(1)} %bitcast.21), custom_call_target="tpu_custom_call" | custom-call | flops 100000000 | bytes 1048576 | tf_op jit(solution)/shard_map/pallas_call | solution.py:356
  20.9 0.0 collective-permute-done.2.g2
  21.0 1.1 %collective-permute-done.3.g3 = bf16[96,128]{1,0:T(8,128)(2,1)S(1)} collective-permute-done((bf16[96,128]{1,0:T(8,128)(2,1)S(1)}, bf16[96,128]{1,0:T(8,128)(2,1)S(1)}, u32[]{:S(2)}, u32[]{:S(2)}) %collective-permute-start.3) | collective-permute-done | bytes 24608 | tf_op jit(solution)/shard_map/ppermute | solution.py:373
  22.0 0.0 collective-permute-done.g0
  22.0 0.0 collective-permute-done.1.g1
  22.0 0.0 copy-start.6
  22.0 0.0 copy-done.1
  22.0 0.0 copy-done.5
  22.1 0.6 copy-done.6
  22.7 0.9 %shard_map.105 = (f32[192,64]{1,0:T(8,128)S(1)}, f32[192,64]{1,0:T(8,128)S(1)}, f32[192,64]{1,0:T(8,128)S(1)}, bf16[48,128]{1,0:T(8,128)(2,1)S(1)}, bf16[48,128]...) custom-call(f32[6,32,64]{2,1,0:T(8,128)S(1)} %bitcast.18, f32[6,32,64]{2,1,0:T(8,128)S(1)} %bitcast.22, ...), custom_call_target="tpu_custom_call" | custom-call | flops 100000000 | bytes 1048576 | tf_op jit(solution)/shard_map/pallas_call | solution.py:356
  23.5 1.9 %collective-permute-start.4 = (bf16[48,128]{1,0:T(8,128)(2,1)S(1)}, bf16[48,128]{1,0:T(8,128)(2,1)S(1)}, u32[]{:S(2)}, u32[]{:S(2)}) collective-permute-start(bf16[48,128]{1,0:T(8,128)(2,1)S(1)} %get-tuple-element.37), channel_id=1, source_target_pairs={{0,16},{16,0},{32,48},{48,32},{64,80},{80,64},{96,112},{112,96},{1... | collective-permute-start | bytes 36872 | tf_op jit(solution)/shard_map/ppermute | solution.py:373
  25.5 5.3 %collective-permute-start.5 = (bf16[48,128]{1,0:T(8,128)(2,1)S(1)}, bf16[48,128]{1,0:T(8,128)(2,1)S(1)}, u32[]{:S(2)}, u32[]{:S(2)}) collective-permute-start(bf16[48,128]{1,0:T(8,128)(2,1)S(1)} %get-tuple-element.38), channel_id=1, source_target_pairs={{16,32},{32,16},{48,64},{64,48},{80,96},{96,80},{112,128},{128,112... | collective-permute-start | bytes 36872 | tf_op jit(solution)/shard_map/ppermute | solution.py:373
  30.8 1.9 %collective-permute-start.6 = (bf16[32,128]{1,0:T(8,128)(2,1)S(1)}, bf16[32,128]{1,0:T(8,128)(2,1)S(1)}, u32[]{:S(2)}, u32[]{:S(2)}) collective-permute-start(bf16[32,128]{1,0:T(8,128)(2,1)S(1)} %get-tuple-element.39), channel_id=1, source_target_pairs={{0,1},{1,0},{2,3},{3,2},{4,5},{5,4},{6,7},{7,6},{8,9},{9,8},{10,11... | collective-permute-start | bytes 24584 | tf_op jit(solution)/shard_map/ppermute | solution.py:373
  32.7 5.3 %collective-permute-start.7 = (bf16[32,128]{1,0:T(8,128)(2,1)S(1)}, bf16[32,128]{1,0:T(8,128)(2,1)S(1)}, u32[]{:S(2)}, u32[]{:S(2)}) collective-permute-start(bf16[32,128]{1,0:T(8,128)(2,1)S(1)} %get-tuple-element.40), channel_id=1, source_target_pairs={{1,2},{2,1},{3,4},{4,3},{5,6},{6,5},{7,8},{8,7},{9,10},{10,9},{11,... | collective-permute-start | bytes 24584 | tf_op jit(solution)/shard_map/ppermute | solution.py:373
  38.0 0.0 collective-permute-done.6.refs_8_
  38.0 3.3 %collective-permute-done.7.refs_9_ = bf16[32,128]{1,0:T(8,128)(2,1)S(1)} collective-permute-done((bf16[32,128]{1,0:T(8,128)(2,1)S(1)}, bf16[32,128]{1,0:T(8,128)(2,1)S(1)}, u32[]{:S(2)}, u32[]{:S(2)}) %collective-permute-start.7) | collective-permute-done | bytes 8224 | tf_op jit(solution)/shard_map/ppermute | solution.py:373
  41.3 0.0 collective-permute-done.4.refs_6_
  41.3 0.0 collective-permute-done.5.refs_7_
  41.3 0.9 %shard_map.106 = (f32[192,64]{1,0:T(8,128)S(1)}, f32[192,64]{1,0:T(8,128)S(1)}, f32[192,64]{1,0:T(8,128)S(1)}, bf16[48,128]{1,0:T(8,128)(2,1)S(1)}, bf16[48,128]...) custom-call(f32[192,64]{1,0:T(8,128)S(1)} %get-tuple-element.34.refs_0_, ...), custom_call_target="tpu_custom_call" | custom-call | flops 100000000 | bytes 1048576 | tf_op jit(solution)/shard_map/pallas_call | solution.py:356
  42.1 1.9 %collective-permute-start.10 = (bf16[32,128]{1,0:T(8,128)(2,1)S(1)}, bf16[32,128]{1,0:T(8,128)(2,1)S(1)}, u32[]{:S(2)}, u32[]{:S(2)}) collective-permute-start(bf16[32,128]{1,0:T(8,128)(2,1)S(1)} %get-tuple-element.46), channel_id=1, source_target_pairs={{0,1},{1,0},{2,3},{3,2},{4,5},{5,4},{6,7},{7,6},{8,9},{9,8},{10,11... | collective-permute-start | bytes 24584 | tf_op jit(solution)/shard_map/ppermute | solution.py:373
  44.1 5.3 %collective-permute-start.11 = (bf16[32,128]{1,0:T(8,128)(2,1)S(1)}, bf16[32,128]{1,0:T(8,128)(2,1)S(1)}, u32[]{:S(2)}, u32[]{:S(2)}) collective-permute-start(bf16[32,128]{1,0:T(8,128)(2,1)S(1)} %get-tuple-element.47), channel_id=1, source_target_pairs={{1,2},{2,1},{3,4},{4,3},{5,6},{6,5},{7,8},{8,7},{9,10},{10,9},{11,... | collective-permute-start | bytes 24584 | tf_op jit(solution)/shard_map/ppermute | solution.py:373
  49.4 1.9 %collective-permute-start.8 = (bf16[48,128]{1,0:T(8,128)(2,1)S(1)}, bf16[48,128]{1,0:T(8,128)(2,1)S(1)}, u32[]{:S(2)}, u32[]{:S(2)}) collective-permute-start(bf16[48,128]{1,0:T(8,128)(2,1)S(1)} %get-tuple-element.44), channel_id=1, source_target_pairs={{0,16},{16,0},{32,48},{48,32},{64,80},{80,64},{96,112},{112,96},{1... | collective-permute-start | bytes 36872 | tf_op jit(solution)/shard_map/ppermute | solution.py:373
  51.3 5.3 %collective-permute-start.9 = (bf16[48,128]{1,0:T(8,128)(2,1)S(1)}, bf16[48,128]{1,0:T(8,128)(2,1)S(1)}, u32[]{:S(2)}, u32[]{:S(2)}) collective-permute-start(bf16[48,128]{1,0:T(8,128)(2,1)S(1)} %get-tuple-element.45), channel_id=1, source_target_pairs={{16,32},{32,16},{48,64},{64,48},{80,96},{96,80},{112,128},{128,112... | collective-permute-start | bytes 36872 | tf_op jit(solution)/shard_map/ppermute | solution.py:373
  56.6 0.0 copy-start.7
  56.6 0.0 copy-start.8
  56.6 0.6 copy-done.7
  57.3 0.0 copy-done.8
  57.3 4.9 %shard_map.108 = (f32[256,256]{1,0:T(8,128)}, f32[4,256,256]{2,1,0:T(8,128)}) custom-call(s32[32]{0:T(128)S(1)} %bitcast.26, s32[24]{0:T(128)S(1)} %bitcast.27, bf16[2048,128]{1,0:T(8,128)(2,1)S(1)} %get-tuple-element.48.t16, bf16[512,128]{1,0:T(8,128)(2,1)S(1)} %get-tuple-element.49.plus_y, bf16[512,128]{1,0:T(8,128)(2,1)S(1)} %get-tuple-element.50.minus_y, ...), custom_call_target="tpu_custom_call" | custom-call | flops 4000000000 | bytes 4194304 | tf_op jit(solution)/shard_map/pallas_call | solution.py:356
  62.2 0.0 collective-permute-done.10.refs_8_
  62.2 0.0 collective-permute-done.11.refs_9_
  62.2 0.0 collective-permute-done.8.refs_6_
  62.2 0.0 collective-permute-done.9.refs_7_
  62.2 1.3 %shard_map.107 = f32[6,32,64]{2,1,0:T(8,128)} custom-call(f32[192,64]{1,0:T(8,128)S(1)} %get-tuple-element.41.refs_0_, f32[192,64]{1,0:T(8,128)S(1)} %get-tuple-element.42.refs_1_, f32[192,64]{1,0:T(8,128)S(1)} %get-tuple-element.43.refs_2_, bf16[2048,128]{1,0:T(8,128)(2,1)S(1)} %get-tuple-element.28.w.refs_3_, ...), custom_call_target="tpu_custom_call" | custom-call | flops 100000000 | bytes 1048576 | tf_op jit(solution)/shard_map/pallas_call | solution.py:356
Async XLA Ops:
  0.6 0.9 %copy-start = (f32[1,1,6,64,32]{3,4,2,1,0:T(8,128)S(1)}, f32[1,1,6,64,32]{3,4,2,1,0:T(8,128)}, u32[]{:S(2)}) copy-start(f32[1,1,6,64,32]{3,4,2,1,0:T(8,128)} %param.14) | copy-start | bytes 147460
  1.5 0.9 %copy-start.2 = (bf16[1,1,32,4096]{3,2,1,0:T(8,128)(2,1)S(1)}, bf16[1,1,32,4096]{3,2,1,0:T(8,128)(2,1)}, u32[]{:S(2)}) copy-start(bf16[1,1,32,4096]{3,2,1,0:T(8,128)(2,1)} %param.10) | copy-start | bytes 786436
  2.5 16.7 %copy-start.3 = (bf16[1,1,32,4096]{3,2,1,0:T(8,128)(2,1)S(1)}, bf16[1,1,32,4096]{3,2,1,0:T(8,128)(2,1)}, u32[]{:S(2)}) copy-start(bf16[1,1,32,4096]{3,2,1,0:T(8,128)(2,1)} %param.8) | copy-start | bytes 786436
  2.9 19.1 %collective-permute-start = (bf16[112,128]{1,0:T(8,128)(2,1)S(1)}, bf16[112,128]{1,0:T(8,128)(2,1)S(1)}, u32[]{:S(2)}, u32[]{:S(2)}) collective-permute-start(bf16[112,128]{1,0:T(8,128)(2,1)S(1)} %get-tuple-element.30), channel_id=1, source_target_pairs={{0,16},{16,0},{32,48},{48,32},{64,80},{80,64},{96,112},{112,96},{1... | collective-permute-start | bytes 86024 | tf_op jit(solution)/shard_map/ppermute | solution.py:373
  5.7 16.4 %collective-permute-start.1 = (bf16[112,128]{1,0:T(8,128)(2,1)S(1)}, bf16[112,128]{1,0:T(8,128)(2,1)S(1)}, u32[]{:S(2)}, u32[]{:S(2)}) collective-permute-start(bf16[112,128]{1,0:T(8,128)(2,1)S(1)} %get-tuple-element.31), channel_id=1, source_target_pairs={{16,32},{32,16},{48,64},{64,48},{80,96},{96,80},{112,128},{128,112... | collective-permute-start | bytes 86024 | tf_op jit(solution)/shard_map/ppermute | solution.py:373
  11.3 9.6 %collective-permute-start.2 = (bf16[96,128]{1,0:T(8,128)(2,1)S(1)}, bf16[96,128]{1,0:T(8,128)(2,1)S(1)}, u32[]{:S(2)}, u32[]{:S(2)}) collective-permute-start(bf16[96,128]{1,0:T(8,128)(2,1)S(1)} %get-tuple-element.32), channel_id=1, source_target_pairs={{0,1},{1,0},{2,3},{3,2},{4,5},{5,4},{6,7},{7,6},{8,9},{9,8},{10,11... | collective-permute-start | bytes 73736 | tf_op jit(solution)/shard_map/ppermute | solution.py:373
  13.3 8.8 %collective-permute-start.3 = (bf16[96,128]{1,0:T(8,128)(2,1)S(1)}, bf16[96,128]{1,0:T(8,128)(2,1)S(1)}, u32[]{:S(2)}, u32[]{:S(2)}) collective-permute-start(bf16[96,128]{1,0:T(8,128)(2,1)S(1)} %get-tuple-element.33), channel_id=1, source_target_pairs={{1,2},{2,1},{3,4},{4,3},{5,6},{6,5},{7,8},{8,7},{9,10},{10,9},{11,... | collective-permute-start | bytes 73736 | tf_op jit(solution)/shard_map/ppermute | solution.py:373
  19.1 1.0 %copy-start.4 = (bf16[1,1,32,4096]{3,2,1,0:T(8,128)(2,1)S(1)}, bf16[1,1,32,4096]{3,2,1,0:T(8,128)(2,1)}, u32[]{:S(2)}) copy-start(bf16[1,1,32,4096]{3,2,1,0:T(8,128)(2,1)} %param.9) | copy-start | bytes 786436
  20.1 1.9 %copy-start.1 = (f32[1,1,6,64,32]{3,4,2,1,0:T(8,128)S(1)}, f32[1,1,6,64,32]{3,4,2,1,0:T(8,128)}, u32[]{:S(2)}) copy-start(f32[1,1,6,64,32]{3,4,2,1,0:T(8,128)} %param.14) | copy-start | bytes 147460
  20.1 1.9 %copy-start.5 = (f32[1,1,6,64,32]{3,4,2,1,0:T(8,128)S(1)}, f32[1,1,6,64,32]{3,4,2,1,0:T(8,128)}, u32[]{:S(2)}) copy-start(f32[1,1,6,64,32]{3,4,2,1,0:T(8,128)} %param.13) | copy-start | bytes 147460
  22.0 0.7 %copy-start.6 = (f32[2]{0:T(128)S(1)}, f32[2]{0:T(128)}, u32[]{:S(2)}) copy-start(f32[2]{0:T(128)} %param.15) | copy-start | bytes 28
  23.5 17.7 %collective-permute-start.4 = (bf16[48,128]{1,0:T(8,128)(2,1)S(1)}, bf16[48,128]{1,0:T(8,128)(2,1)S(1)}, u32[]{:S(2)}, u32[]{:S(2)}) collective-permute-start(bf16[48,128]{1,0:T(8,128)(2,1)S(1)} %get-tuple-element.37), channel_id=1, source_target_pairs={{0,16},{16,0},{32,48},{48,32},{64,80},{80,64},{96,112},{112,96},{1... | collective-permute-start | bytes 36872 | tf_op jit(solution)/shard_map/ppermute | solution.py:373
  25.5 15.8 %collective-permute-start.5 = (bf16[48,128]{1,0:T(8,128)(2,1)S(1)}, bf16[48,128]{1,0:T(8,128)(2,1)S(1)}, u32[]{:S(2)}, u32[]{:S(2)}) collective-permute-start(bf16[48,128]{1,0:T(8,128)(2,1)S(1)} %get-tuple-element.38), channel_id=1, source_target_pairs={{16,32},{32,16},{48,64},{64,48},{80,96},{96,80},{112,128},{128,112... | collective-permute-start | bytes 36872 | tf_op jit(solution)/shard_map/ppermute | solution.py:373
  30.8 7.2 %collective-permute-start.6 = (bf16[32,128]{1,0:T(8,128)(2,1)S(1)}, bf16[32,128]{1,0:T(8,128)(2,1)S(1)}, u32[]{:S(2)}, u32[]{:S(2)}) collective-permute-start(bf16[32,128]{1,0:T(8,128)(2,1)S(1)} %get-tuple-element.39), channel_id=1, source_target_pairs={{0,1},{1,0},{2,3},{3,2},{4,5},{5,4},{6,7},{7,6},{8,9},{9,8},{10,11... | collective-permute-start | bytes 24584 | tf_op jit(solution)/shard_map/ppermute | solution.py:373
  32.7 8.6 %collective-permute-start.7 = (bf16[32,128]{1,0:T(8,128)(2,1)S(1)}, bf16[32,128]{1,0:T(8,128)(2,1)S(1)}, u32[]{:S(2)}, u32[]{:S(2)}) collective-permute-start(bf16[32,128]{1,0:T(8,128)(2,1)S(1)} %get-tuple-element.40), channel_id=1, source_target_pairs={{1,2},{2,1},{3,4},{4,3},{5,6},{6,5},{7,8},{8,7},{9,10},{10,9},{11,... | collective-permute-start | bytes 24584 | tf_op jit(solution)/shard_map/ppermute | solution.py:373
  42.1 20.1 %collective-permute-start.10 = (bf16[32,128]{1,0:T(8,128)(2,1)S(1)}, bf16[32,128]{1,0:T(8,128)(2,1)S(1)}, u32[]{:S(2)}, u32[]{:S(2)}) collective-permute-start(bf16[32,128]{1,0:T(8,128)(2,1)S(1)} %get-tuple-element.46), channel_id=1, source_target_pairs={{0,1},{1,0},{2,3},{3,2},{4,5},{5,4},{6,7},{7,6},{8,9},{9,8},{10,11... | collective-permute-start | bytes 24584 | tf_op jit(solution)/shard_map/ppermute | solution.py:373
  44.1 18.2 %collective-permute-start.11 = (bf16[32,128]{1,0:T(8,128)(2,1)S(1)}, bf16[32,128]{1,0:T(8,128)(2,1)S(1)}, u32[]{:S(2)}, u32[]{:S(2)}) collective-permute-start(bf16[32,128]{1,0:T(8,128)(2,1)S(1)} %get-tuple-element.47), channel_id=1, source_target_pairs={{1,2},{2,1},{3,4},{4,3},{5,6},{6,5},{7,8},{8,7},{9,10},{10,9},{11,... | collective-permute-start | bytes 24584 | tf_op jit(solution)/shard_map/ppermute | solution.py:373
  49.4 12.8 %collective-permute-start.8 = (bf16[48,128]{1,0:T(8,128)(2,1)S(1)}, bf16[48,128]{1,0:T(8,128)(2,1)S(1)}, u32[]{:S(2)}, u32[]{:S(2)}) collective-permute-start(bf16[48,128]{1,0:T(8,128)(2,1)S(1)} %get-tuple-element.44), channel_id=1, source_target_pairs={{0,16},{16,0},{32,48},{48,32},{64,80},{80,64},{96,112},{112,96},{1... | collective-permute-start | bytes 36872 | tf_op jit(solution)/shard_map/ppermute | solution.py:373
  51.3 10.9 %collective-permute-start.9 = (bf16[48,128]{1,0:T(8,128)(2,1)S(1)}, bf16[48,128]{1,0:T(8,128)(2,1)S(1)}, u32[]{:S(2)}, u32[]{:S(2)}) collective-permute-start(bf16[48,128]{1,0:T(8,128)(2,1)S(1)} %get-tuple-element.45), channel_id=1, source_target_pairs={{16,32},{32,16},{48,64},{64,48},{80,96},{96,80},{112,128},{128,112... | collective-permute-start | bytes 36872 | tf_op jit(solution)/shard_map/ppermute | solution.py:373
  56.6 0.7 %copy-start.7 = (s32[1,1,32]{2,1,0:T(1,128)S(1)}, s32[1,1,32]{2,1,0:T(1,128)}, u32[]{:S(2)}) copy-start(s32[1,1,32]{2,1,0:T(1,128)} %param.11) | copy-start | bytes 388
  56.6 0.7 %copy-start.8 = (s32[1,1,24]{2,1,0:T(1,128)S(1)}, s32[1,1,24]{2,1,0:T(1,128)}, u32[]{:S(2)}) copy-start(s32[1,1,24]{2,1,0:T(1,128)} %param.12) | copy-start | bytes 292

commit v2 on v1

v2 whole, which is shorter than its diff:
```python
import jax
import jax.numpy as jnp
from jax import lax
from jax.experimental import pallas as pl
from jax.experimental.pallas import tpu as pltpu
from jax.sharding import PartitionSpec as P

EX, EY, NE, NRHS = 4, 8, 32, 6
F32, BF16 = jnp.float32, jnp.bfloat16
VMEM = pl.BlockSpec(memory_space=pltpu.VMEM)
SMEM = pl.BlockSpec(memory_space=pltpu.SMEM)
ANY = pl.BlockSpec(memory_space=pl.ANY)
NT = (((1,), (1,)), ((), ()))
NN = (((1,), (0,)), ((), ()))

XA, XB = 0, 2048
XC = 4096
XD = 5120
XG = 5888
XR = 6656
XT = 7424
XLEN = 7936
YA, YB = 0, 2048
YF = 4096
YC = 5120
YD = 5632
YG = 6400
YR = 7168
YT = 7552
YLEN = 8064

EXT, SPAN = 160, 960


def dot(a, b, dims=NN):
    return lax.dot_general(a, b, dims, preferred_element_type=F32)


def iota(shape, dim):
    return lax.broadcasted_iota(jnp.int32, shape, dim)


def onehot(mask):
    return mask.astype(F32).astype(BF16)


def split(x):
    hi = x.astype(BF16)
    return hi, (x - hi.astype(F32)).astype(BF16)


def halves(x):
    lanes = x.shape[1] // 2
    return jnp.concatenate([x[:, :lanes], x[:, lanes:]], 0)


def over(a, b):
    return jnp.concatenate([a, b], 0)


def parity(axis):
    return lax.axis_index(axis) % 2


def with_traces(v):
    q, lane = iota((64, 128), 0), iota((64, 128), 1)
    t = lane % 16
    f = lane // 16 - 4
    along_y = 16 * (t // 4) + t % 4
    source = jnp.where(f == 0, 48 + t, jnp.where(f == 1, t, jnp.where(f == 2, along_y + 12, along_y)))
    pick = onehot(q == jnp.where(f < 0, lane, source))
    hi, lo = split(v)
    return dot(hi, pick) + dot(lo, pick)


def pack_lanes(v):
    hi, lo = split(v)
    q, lane = iota((64, 128), 0), iota((64, 128), 1)
    both = dot(hi, onehot(q == lane)) + dot(lo, onehot(q == lane - 64))
    return jnp.concatenate([both[n * NE : (n + 1) * NE] for n in range(NRHS)], 1)


def pack_x_kernel(blocks, faces, tent, guess, rhs, even, odd, guess_packed, rhs_packed):
    g = pack_lanes(guess[...].reshape(NRHS * NE, 64))
    r = pack_lanes(rhs[...].reshape(NRHS * NE, 64))
    guess_packed[...] = g.astype(BF16)
    rhs_packed[...] = r.astype(BF16)
    first = parity("bx") == 0

    def put(start, lanes, make):
        low, high = make(0), make(1)
        even[:, start : start + lanes] = jnp.where(first, high, low).astype(BF16)
        odd[:, start : start + lanes] = jnp.where(first, low, high).astype(BF16)

    def rows(k, side):
        return 8 * k if side == 0 else 24 - 8 * k

    def of(ref, k, side, start, lanes):
        row = rows(k, side)
        base = row // 16 * 16
        return ref[base : base + 16, start : start + lanes].astype(F32)[row - base : row - base + 8]

    def packed(value, k, side):
        return value[rows(k, side) : rows(k, side) + 8]

    def face_traces(side):
        return jnp.concatenate([of(faces, 1, side, f * 1024 + 768 * side, 256) for f in range(4)], 1)

    for h in range(2):
        put(XA + h * 1024, 1024, lambda s: over(of(blocks, 0, s, h * 1024, 1024), of(blocks, 0, s, h * 1024 + 2048, 1024)))
        put(XB + h * 1024, 1024, lambda s: over(of(faces, 0, s, h * 1024, 1024), of(faces, 0, s, h * 1024 + 2048, 1024)))
    put(XC, 1024, lambda s: over(of(blocks, 1, s, 3072 * s, 1024), face_traces(s)))
    put(XD, 768, lambda s: over(packed(g, 0, s), packed(g, 1, s)))
    put(XG, 768, lambda s: over(packed(g, 2, s), packed(r, 0, s)))
    put(XR, 768, lambda s: over(packed(r, 1, s), jnp.zeros((8, 768), F32)))
    put(XT, 512, lambda s: halves(of(tent, 0, s, 3072 * s, 1024)))


def pack_y_kernel(blocks, faces, tent, guess_packed, rhs_packed, x_even, x_odd, even, odd, low, high):
    first = parity("bx") == 0
    for start in range(0, XLEN, 256):
        a = x_even[:, start : start + 256].astype(F32)
        b = x_odd[:, start : start + 256].astype(F32)
        low[:, start : start + 256] = jnp.where(first, b, a).astype(BF16)
        high[:, start : start + 256] = jnp.where(first, a, b).astype(BF16)
    py = parity("by")
    is_first = py == 0

    def select(k, near=None, far=None, columns=64):
        r, j = iota((16, columns), 0), iota((16, columns), 1)
        high_side = jnp.where(r < 8, py, 1 - py) == 0
        iy = jnp.where(high_side, 7 - k, k)
        row = r % 8 - 2
        source = jnp.where((row >= 0) & (row < 4), row * 8 + iy, -1)
        if near is not None:
            source = jnp.where(row == -1, 32 + near + iy, jnp.where(row == 4, 48 + near + iy, source))
        if far is not None:
            source = jnp.where(row == -2, 32 + far + iy, jnp.where(row == 5, 48 + far + iy, source))
        return onehot(j == source)

    def put(start, value):
        even[:, start : start + value[0].shape[1]] = value[0].astype(BF16)
        odd[:, start : start + value[1].shape[1]] = value[1].astype(BF16)

    def both(make, picked):
        return make(picked[:8]), make(picked[8:])

    for ref, start, part in ((blocks, YA, XA), (faces, YB, XB)):
        cut = []
        for h in range(2):
            source = jnp.concatenate(
                [ref[:, h * 2048 : h * 2048 + 2048], low[:, part : part + 2048], high[:, part : part + 2048]], 0
            )
            cut.append(dot(select(0, 8 * h), source))
        put(start, (over(cut[0][:8], cut[1][:8]), over(cut[0][8:], cut[1][8:])))

    def by_side(minus, plus):
        up = jnp.where(is_first, plus[:8], minus[:8])
        down = jnp.where(is_first, minus[8:], plus[8:])
        return halves(up), halves(down)

    own1, own0 = select(1, columns=32), select(0, columns=32)

    def lanes(ref, pieces, width):
        return jnp.concatenate([ref[:, p : p + width] for p in pieces], 1)

    minus, plus = [i * 1024 for i in range(4)], [i * 1024 + 768 for i in range(4)]
    put(YC, by_side(dot(own1, lanes(blocks, minus, 256)), dot(own1, lanes(blocks, plus, 256))))
    put(YT, by_side(dot(own0, lanes(tent, minus, 256)), dot(own0, lanes(tent, plus, 256))))
    minus = [f * 1024 + i * 256 for f in range(4) for i in range(4)]
    plus = [p + 128 for p in minus]
    put(YF, by_side(dot(own1, lanes(faces, minus, 128)), dot(own1, lanes(faces, plus, 128))))
    own = guess_packed[...]
    rows = jnp.concatenate([own, low[:, XD : XD + 768], high[:, XD : XD + 768]], 0)
    g0, g1, g2 = dot(select(0, 0, 8), rows), dot(select(1, 0), rows), dot(select(2, columns=32), own)
    rows = jnp.concatenate([rhs_packed[...], low[:, XG : XG + 768], high[:, XG : XG + 768]], 0)
    r0, r1 = dot(select(0, 8), rows), dot(own1, rhs_packed[...])
    put(YD, (over(g0[:8], g1[:8]), over(g0[8:], g1[8:])))
    put(YG, (over(g2[:8], r0[:8]), over(g2[8:], r0[8:])))
    put(YR, both(halves, r1))


def prolong_kernel(tent, t16, plus_y, minus_y, stage, t32):
    lane = iota((256, 128), 1)
    for k in range(4):
        for ph in range(8):
            chunk = tent[:, (ph * 4 + k) * 128 : (ph * 4 + k + 1) * 128].astype(F32)
            stage[k, pl.ds(ph, NE, stride=8), :] = chunk
    for k in range(4):
        both = stage[k]
        other = pltpu.roll(both, 64, 1)
        t32[pl.ds(2 * k, 256, stride=8), :] = jnp.where(lane < 64, both, other)
        t32[pl.ds(2 * k + 1, 256, stride=8), :] = jnp.where(lane < 64, other, both)
    t16[...] = t32[...].astype(BF16)
    sub = iota((8, 128), 0)
    for e in range(NE):
        plus, minus = [], []
        for h in range(2):
            base = e * 64 + 32 * h
            a, b = t32[base + 8 : base + 16, :], t32[base + 24 : base + 32, :]
            plus.append(jnp.where(sub < 4, pltpu.roll(a, 4, 0), b))
            a, b = t32[base : base + 8, :], t32[base + 16 : base + 24, :]
            minus.append(jnp.where(sub < 4, a, pltpu.roll(b, 4, 0)))
        plus_y[e * 16 : e * 16 + 16, :] = jnp.concatenate(plus, 0).astype(BF16)
        minus_y[e * 16 : e * 16 + 16, :] = jnp.concatenate(minus, 0).astype(BF16)


def operators(block_chunk, face_chunk, w, inverse, stage, fstage, w32):
    lane = iota((256, 128), 1)
    lane_e = iota((NE, 128), 1)
    diag = jnp.zeros((NE, 128), F32)
    for k in range(4):
        for ph in range(8):
            c = ph * 4 + k
            chunk = block_chunk(c)
            diag = diag + jnp.where((lane_e == 2 * c) | (lane_e == 65 + 2 * c), chunk, 0.0)
            stage[k, pl.ds(ph, NE, stride=8), :] = chunk
    diag = (diag + pltpu.roll(diag, 64, 1))[:, :64]
    inverse[...] = 1.0 / jnp.where(diag == 0.0, 1.0, diag)
    for f in range(4):
        for ph in range(8):
            fstage[f, pl.ds(ph, NE, stride=8), :] = face_chunk(f * 8 + ph)
    folded = jnp.concatenate([fstage[f].astype(BF16) for f in range(4)], 1)
    row, col = iota((512, 128), 0), iota((512, 128), 1)
    lo_of = (row // 16) % 8
    target = 64 + row // 128 * 16 + row % 16
    for k in range(4):
        both = stage[k]
        other = pltpu.roll(both, 64, 1)
        for s, part in enumerate((both, other)):
            p_lo = 2 * k + s
            coupled = dot(folded, onehot((col == target) & (lo_of == p_lo)))
            w32[pl.ds(p_lo, 256, stride=8), :] = jnp.where(lane < 64, part, coupled)
    w[...] = w32[...].astype(BF16)


def own_kernel(blocks, faces, w, inverse, *scratch):
    chunk = lambda ref: lambda c: ref[:, c * 128 : (c + 1) * 128].astype(F32)
    operators(chunk(blocks), chunk(faces), w, inverse, *scratch)


NOTHING = (8, 128)


def part(ref, start, c, half):
    row = 8 * (c // half)
    lane = start + (c % half) * 128
    return ref[:, lane : lane + 128].astype(F32)[row : row + 8]


def halo_x_kernel(low, high, w, inverse, *scratch):
    zero = jnp.zeros(NOTHING, F32)

    def block(c):
        far_low = part(low, XC, c - 24, 8) if c >= 24 else zero
        far_high = part(high, XC, c, 8) if c < 8 else zero
        return jnp.concatenate([part(low, XA, c, 16), far_low, part(high, XA, c, 16), far_high], 0)

    def face(c):
        f, ph = c // 8, c % 8
        far_low = part(low, XC, 8 + f * 2 + ph - 6, 8) if ph >= 6 else zero
        far_high = part(high, XC, 8 + f * 2 + ph, 8) if ph < 2 else zero
        return jnp.concatenate([part(low, XB, c, 16), far_low, part(high, XB, c, 16), far_high], 0)

    operators(block, face, w, inverse, *scratch)


def halo_y_kernel(even, odd, w, inverse, low, high, *scratch):
    first = parity("by") == 0
    for start in range(0, YLEN, 128):
        a = even[:, start : start + 128].astype(F32)
        b = odd[:, start : start + 128].astype(F32)
        low[:, start : start + 128] = jnp.where(first, b, a).astype(BF16)
        high[:, start : start + 128] = jnp.where(first, a, b).astype(BF16)
    zero = jnp.zeros(NOTHING, F32)

    def block(c):
        i, d = c // 8, c % 8
        far_low = part(low, YC, i * 2 + d - 6, 4) if d >= 6 else zero
        far_high = part(high, YC, i * 2 + d, 4) if d < 2 else zero
        return jnp.concatenate([part(low, YA, c, 16), far_low, part(high, YA, c, 16), far_high], 0)

    def face(c):
        f, ph = c // 8, c % 8
        i = ph // 2
        far_low = part(low, YF, f * 4 + i, 8) if ph % 2 == 1 else zero
        far_high = part(high, YF, f * 4 + i, 8) if ph % 2 == 0 else zero
        return jnp.concatenate([part(low, YB, c, 16), far_low, part(high, YB, c, 16), far_high], 0)

    operators(block, face, w, inverse, *scratch)


def factors(bounds):
    low, high = bounds[0:1, 0:1], bounds[0:1, 1:2]
    centre = 0.5 * (high + low)
    half_width = 0.5 * (high - low)
    spread = centre / half_width
    first = 1.0 / spread
    second = 1.0 / (2.0 * spread - first)
    third = 1.0 / (2.0 * spread - second)
    return centre, half_width, first, second, third


OWN = [((ix + 3) * 16 + iy, 0, ix * 8 + iy) for ix in range(EX) for iy in range(EY)]


def beside_x(k):
    return [((7 + k if s else 2 - k) * 16 + iy, 1, s * 16 + k * 8 + iy) for s in range(2) for iy in range(EY)]


def beside_y(k, rows):
    return [((r + 1) * 16 + (8 + k if s else 15 - k), 2, s * 16 + k * 8 + r) for s in range(2) for r in rows]


LEVELS = (
    (1, 9, OWN + beside_x(0) + beside_x(1) + beside_y(0, range(1, 7)) + beside_y(1, range(2, 6))),
    (2, 8, OWN + beside_x(0) + beside_y(0, range(2, 6))),
    (3, 7, OWN),
)


def smooth_kernel(guess, rhs, w, wx, wy, inv, inv_x, inv_y, bounds, x_low, x_high, y_low, y_high, smoothed,
                  g_ref, r_ref, i_ref, t_ref, x_ref, a_ref):
    def joined(value):
        return value + pltpu.roll(value, 64, 1)

    def fill(ref, own, x_parts, y_parts):
        ref[...] = jnp.zeros((SPAN, 128), F32)
        for n in range(NRHS):
            for ix in range(EX):
                row = n * EXT + (ix + 3) * 16
                ref[row : row + 8, 0:64] = own[n, ix * 8 : ix * 8 + 8, :]
            for side, message in enumerate((x_low, x_high)):
                for k, (start, top) in enumerate(x_parts):
                    row = n * EXT + (7 + k if side else 2 - k) * 16
                    value = message[:, start + n * 128 : start + n * 128 + 128].astype(F32)
                    ref[row : row + 8, :] = joined(value[8 * top : 8 * top + 8])
            for side, message in enumerate((y_low, y_high)):
                for k, (start, top, half) in enumerate(y_parts):
                    value = part(message, start, n, half) if half else (
                        message[:, start + n * 128 : start + n * 128 + 128].astype(F32)[8 * top : 8 * top + 8]
                    )
                    ref[pl.ds(n * EXT + 16 + (8 + k if side else 15 - k), 8, stride=16), :] = joined(value)

    fill(g_ref, guess, ((XD, 0), (XD, 1), (XG, 0)), ((YD, 0, 0), (YD, 1, 0), (YG, 0, 0)))
    fill(r_ref, rhs, ((XG, 1), (XR, 0)), ((YG, 1, 0), (YR, 0, 3)))
    i_ref[...] = jnp.ones((EXT, 128), F32)
    wide = lambda value: jnp.concatenate([value, value], 1)
    for ix in range(EX):
        i_ref[(ix + 3) * 16 : (ix + 3) * 16 + 8, 0:64] = inv[ix * 8 : ix * 8 + 8, :]
    for s in range(2):
        for k in range(2):
            base = s * 16 + k * 8
            row = (7 + k if s else 2 - k) * 16
            i_ref[row : row + 8, 0:64] = inv_x[base : base + 8, :]
            i_ref[pl.ds(16 + (8 + k if s else 15 - k), 8, stride=16), :] = wide(inv_y[base : base + 8, :])
    x_ref[...] = jnp.zeros((8 * EXT, 128), F32)
    a_ref[...] = jnp.zeros((8 * EXT, 128), F32)
    lane = iota((16, 128), 1)
    tables = (w, wx, wy)

    def apply(level, v):
        first, last, elements = LEVELS[level]
        t_ref[...] = with_traces(v)
        for n in range(NRHS):
            for ri in range(first, last):
                row = n * EXT + ri * 16
                own = t_ref[row : row + 16, :]
                sides = jnp.where(
                    lane < 80,
                    t_ref[row - 16 : row, :],
                    jnp.where(
                        lane < 96,
                        t_ref[row + 16 : row + 32, :],
                        jnp.where(lane < 112, pltpu.roll(own, 1, 0), pltpu.roll(own, 15, 0)),
                    ),
                )
                x_ref[row : row + 16, :] = jnp.where(lane < 64, own, sides)
        for row, table, e in elements:
            hi, lo = split(x_ref[pl.ds(row, 8, stride=EXT), :])
            out = dot(over(hi, lo), tables[table][e * 64 : e * 64 + 64, :], NT)
            a_ref[pl.ds(row, 8, stride=EXT), 0:64] = out[:8] + out[8:]
        return a_ref[:SPAN, 0:64]

    centre, half_width, first, second, third = factors(bounds)
    inverse = jnp.concatenate([i_ref[:, 0:64]] * NRHS, 0)
    v = g_ref[:, 0:64]
    r = r_ref[:, 0:64] - apply(0, v)
    u = inverse * r / centre
    x = v + u
    for level, factor, new in ((1, first, second), (2, second, third)):
        r = r - apply(level, u)
        u = new * factor * u + (2.0 * new / half_width) * inverse * r
        x = x + u
    for n in range(NRHS):
        for ix in range(EX):
            row = n * EXT + (ix + 3) * 16
            smoothed[n, ix * 8 : ix * 8 + 8, :] = x[row : row + 8]


def ghost_rows(message, start, out):
    lane = iota((8, 128), 1)
    for j in range(8):
        both = part(message, start, j, 4)
        other = pltpu.roll(both, 64, 1)
        out[pl.ds(2 * j, 8, stride=16), :] = jnp.where(lane < 64, both, other)
        out[pl.ds(2 * j + 1, 8, stride=16), :] = jnp.where(lane < 64, other, both)


def label_masks(masks):
    lane = iota((16, 256), 1)
    for b in range(4):
        masks[b * 16 : b * 16 + 16, :] = onehot(lane // 64 == b)


def masked(masks, piece, label):
    mask = masks[pl.ds(pl.multiple_of(label * 16, 16), 16), :]
    return jnp.concatenate([piece, piece], 1) * jnp.concatenate([mask] * 4, 0)


def none(count):
    return jnp.zeros((count, 128), BF16)


def face_column(f, rows):
    return jnp.concatenate([none(64 + 16 * f), rows] + ([none(48 - 16 * f)] if f < 3 else []), 0)


def galerkin_kernel(labels, side_labels, t16, plus_y, minus_y, w, x_low, x_high, local, ghost, edge_columns,
                    tt, xlow, xhigh, masks, big):
    ghost_rows(x_low, XT, xlow)
    ghost_rows(x_high, XT, xhigh)
    label_masks(masks)
    lane128 = iota((64, 128), 1)
    for pair in range(NE // 2):
        turned = t16[pair * 128 : pair * 128 + 128, :].astype(F32).T[:64]
        first, second = labels[2 * pair], labels[2 * pair + 1]
        for a in range(4):
            keep = jnp.where(
                lane128 < 64,
                jnp.where(first == a, 1.0, 0.0),
                jnp.where(second == a, 1.0, 0.0),
            )
            tt[a * 64 : a * 64 + 64, pair * 128 : pair * 128 + 128] = (turned * keep).astype(BF16)
    for f in range(2):
        for ix in range(EX):
            start = (4 * ix + 3 * f) * 128
            edge_columns[f, :, ix * 128 : ix * 128 + 128] = tt[:, start : start + 128]

    def row_of_elements(ix, carry):
        for iy in range(EY):
            e = ix * EY + iy
            own = pl.ds(pl.multiple_of(e * 64, 64), 64)
            before = pl.multiple_of(jnp.maximum(e - 8, 0) * 64, 64)
            after = pl.multiple_of(jnp.minimum(e + 8, 31) * 64, 64)
            rows = [
                jnp.where(ix == 0, xlow[iy * 16 : iy * 16 + 16, :], t16[pl.ds(before + 48, 16), :].astype(F32)).astype(BF16),
                jnp.where(ix == 3, xhigh[iy * 16 : iy * 16 + 16, :], t16[pl.ds(after, 16), :].astype(F32)).astype(BF16),
            ]
            if iy > 0:
                rows.append(plus_y[pl.ds(pl.multiple_of((e - 1) * 16, 16), 16), :])
            else:
                rows.append(none(16))
            if iy < 7:
                rows.append(minus_y[pl.ds(pl.multiple_of((e + 1) * 16, 16), 16), :])
            columns = [jnp.concatenate([t16[own, :], none(64)], 0)]
            columns += [face_column(f, value) for f, value in enumerate(rows)]
            pieces = dot(w[own, :], jnp.concatenate(columns, 1)).astype(BF16)
            piece = lambda s: pieces[:, s * 128 : s * 128 + 128]
            label0 = jnp.where(ix == 0, side_labels[iy], labels[jnp.maximum(e - 8, 0)])
            label1 = jnp.where(ix == 3, side_labels[8 + iy], labels[jnp.minimum(e + 8, 31)])
            big[0, own, :] = masked(masks, piece(0), labels[e])
            big[1, own, :] = masked(masks, piece(1), label0)
            big[2, own, :] = masked(masks, piece(2), label1)
            nothing = jnp.zeros((64, 256), BF16)
            big[3, own, :] = masked(masks, piece(3), labels[e - 1]) if iy > 0 else nothing
            big[4, own, :] = masked(masks, piece(4), labels[e + 1]) if iy < 7 else nothing
        return carry

    lax.fori_loop(0, EX, row_of_elements, 0)
    local[...] = (
        dot(tt[...], big[0])
        + dot(tt[:, 512:], big[1, 512:, :])
        + dot(tt[:, :1536], big[2, :1536, :])
        + dot(tt[...], big[3])
        + dot(tt[...], big[4])
    )
    ghost[0] = dot(tt[:, :512], big[1, :512, :])
    ghost[1] = dot(tt[:, 1536:], big[2, 1536:, :])
    ghost[2] = jnp.zeros((256, 256), F32)
    ghost[3] = jnp.zeros((256, 256), F32)


def ghost_y_kernel(side_labels, w, edge_columns, y_low, y_high, ghost_in, ghost, rows, masks, side, result, sems):
    label_masks(masks)
    copies = []
    for f, message in enumerate((y_low, y_high)):
        ghost_rows(message, YT, rows)
        side[...] = jnp.zeros((512, 256), BF16)
        for ix in range(EX):
            e = ix * EY + 7 * f
            near = rows[(ix + 2) * 16 : (ix + 2) * 16 + 16, :].astype(BF16)
            piece = dot(w[e * 64 : e * 64 + 64, :], face_column(2 + f, near)).astype(BF16)
            start = ix * 128 + 64 * f
            side[start : start + 64, :] = masked(masks, piece, side_labels[16 + 4 * f + ix])
        result[f] = dot(edge_columns[f], side[...])
        copies.append(pltpu.make_async_copy(result.at[f], ghost.at[2 + f], sems.at[f]))
        copies[-1].start()
    for copy in copies:
        copy.wait()


def call(kernel, outs, scratch, operands, flops, moved, in_specs=None, out_specs=None, aliases=None):
    return pl.pallas_call(
        kernel,
        out_shape=outs,
        in_specs=in_specs or [VMEM] * len(operands),
        out_specs=out_specs or [VMEM] * len(outs),
        scratch_shapes=scratch,
        input_output_aliases=aliases or {},
        cost_estimate=pl.CostEstimate(flops=flops, bytes_accessed=moved, transcendentals=0),
        compiler_params=pltpu.CompilerParams(vmem_limit_bytes=48 * 1024 * 1024),
    )(*operands)


def exchange(messages, axis):
    out = []
    for first, message in enumerate(messages):
        pairs = []
        for i in range(first, lax.axis_size(axis) - 1, 2):
            pairs += [(i, i + 1), (i + 1, i)]
        out.append(lax.ppermute(message, axis, pairs))
    return out


def shaped(*shape, dtype=BF16):
    return jax.ShapeDtypeStruct(shape, dtype)


STAGES = [pltpu.VMEM((4, 256, 128), F32), pltpu.VMEM((4, 256, 128), F32), pltpu.VMEM((2048, 128), F32)]


def on_device(blocks, faces, tentative, aggregate, ghost_labels, rhs, guess, bounds):
    blocks, faces, tentative = [a.reshape(NE, 4096) for a in (blocks, faces, tentative)]
    rhs = jnp.swapaxes(rhs[0, 0], 1, 2)
    guess = jnp.swapaxes(guess[0, 0], 1, 2)
    labels, side_labels = aggregate.reshape(NE), ghost_labels.reshape(24)
    packed = shaped(NE, 768)
    even, odd, guess_packed, rhs_packed = call(
        pack_x_kernel, [shaped(16, XLEN)] * 2 + [packed] * 2, [],
        (blocks, faces, tentative, guess, rhs), 10**6, 2**20,
    )
    even, odd = exchange((even, odd), "bx")
    w, inverse = call(
        own_kernel, [shaped(2048, 128), shaped(NE, 64, dtype=F32)], STAGES, (blocks, faces), 10**9, 2**20
    )
    t16, plus_y, minus_y = call(
        prolong_kernel, [shaped(2048, 128), shaped(512, 128), shaped(512, 128)],
        [STAGES[0], STAGES[2]], (tentative,), 5 * 10**8, 2**20,
    )
    even, odd, x_low, x_high = call(
        pack_y_kernel, [shaped(16, YLEN)] * 2 + [shaped(16, XLEN)] * 2, [],
        (blocks, faces, tentative, guess_packed, rhs_packed, even, odd), 10**8, 2**20,
    )
    even, odd = exchange((even, odd), "by")
    wx, inverse_x = call(
        halo_x_kernel, [shaped(2048, 128), shaped(NE, 64, dtype=F32)], STAGES, (x_low, x_high), 10**9, 2**20
    )
    local, ghost, edge_columns = call(
        galerkin_kernel,
        [shaped(256, 256, dtype=F32), shaped(4, 256, 256, dtype=F32), shaped(2, 256, 512)],
        [
            pltpu.VMEM((256, 2048), BF16),
            pltpu.VMEM((128, 128), F32),
            pltpu.VMEM((128, 128), F32),
            pltpu.VMEM((64, 256), BF16),
            pltpu.VMEM((5, 2048, 256), BF16),
        ],
        (labels, side_labels, t16, plus_y, minus_y, w, x_low, x_high),
        4 * 10**9, 4 * 2**20,
        [SMEM, SMEM] + [VMEM] * 6,
    )
    wy, inverse_y, y_low, y_high = call(
        halo_y_kernel, [shaped(2048, 128), shaped(NE, 64, dtype=F32)] + [shaped(16, YLEN)] * 2, STAGES,
        (even, odd), 10**9, 2**20,
    )
    (smoothed,) = call(
        smooth_kernel, [shaped(NRHS, NE, 64, dtype=F32)],
        [pltpu.VMEM((SPAN, 128), F32)] * 2
        + [pltpu.VMEM((EXT, 128), F32), pltpu.VMEM((SPAN, 128), F32)]
        + [pltpu.VMEM((8 * EXT, 128), F32)] * 2,
        (guess, rhs, w, wx, wy, inverse, inverse_x, inverse_y, bounds.reshape(1, 2), x_low, x_high, y_low, y_high),
        10**9, 2**20,
    )
    (ghost,) = call(
        ghost_y_kernel, [shaped(4, 256, 256, dtype=F32)],
        [
            pltpu.VMEM((128, 128), F32),
            pltpu.VMEM((64, 256), BF16),
            pltpu.VMEM((512, 256), BF16),
            pltpu.VMEM((2, 256, 256), F32),
            pltpu.SemaphoreType.DMA((2,)),
        ],
        (side_labels, w, edge_columns, y_low, y_high, ghost), 10**9, 2**20,
        [SMEM] + [VMEM] * 4 + [ANY], [ANY], {5: 0},
    )
    return jnp.swapaxes(smoothed, 1, 2)[None, None], local[None, None], ghost[None, None]


def solution(mesh):
    b = lambda extra: P("bx", "by", *([None] * extra))
    return jax.shard_map(
        on_device,
        mesh=mesh,
        in_specs=(b(2), b(2), b(2), b(1), b(1), b(3), b(3), P()),
        out_specs=(b(3), b(2), b(3)),
        check_vma=False,
    )
```

time: 64 us -> 43.4 us (0.68)
  the two profiles are of different devices: /device:TPU:102 before, /device:TPU:134 now
where the time goes in v2:
time: 43.4 us; the launch traced here: 43 us
  starting transfers between devices  15.1 us (35%)
  Pallas kernels  14.5 us (33%)
  waiting for transfers between devices  6.64 us (15%)
  local copies, waits for them, and re-layouts  5.95 us (14%)
  between operations  0.83 us (2%)
    ppermute x4, starting transfers between devices, exchange(): out.append(lax.ppermute(message, axis, pairs))  15.1 us
    pallas_call x9, Pallas kernels, call(): pl.pallas_call(kernel, out_shape=outs, in_specs=in_specs or [VMEM] * len(...  14.5 us
    ppermute x4, waiting for transfers between devices, exchange(): out.append(lax.ppermute(message, axis, pairs))  6.64 us
    unnamed x26, local copies, waits for them, and re-layouts  5.95 us
  transfers between devices with their start and end apart: 4, of which 1 were waited for; matrix products, arithmetic and copies ran while one was open for 0% of the time, Pallas kernels for 16%

profile of v2, /device:TPU:134, one launch (start us, length us, event | category | flops | bytes accessed | tf_op | source)
XLA Modules:
  0.0 43.0 jit_solution(5082020707148430013)
XLA Ops:
  0.6 0.0 copy-start
  0.6 0.9 %copy-done = bf16[1,1,32,4096]{3,2,1,0:T(8,128)(2,1)S(1)} copy-done((bf16[1,1,32,4096]{3,2,1,0:T(8,128)(2,1)S(1)}, bf16[1,1,32,4096]{3,2,1,0:T(8,128)(2,1)}, u32[]{:S(2)}) %copy-start) | copy-done | bytes 262168
  1.6 0.0 copy-start.2
  1.6 0.9 %copy-done.2 = bf16[1,1,32,4096]{3,2,1,0:T(8,128)(2,1)S(1)} copy-done((bf16[1,1,32,4096]{3,2,1,0:T(8,128)(2,1)S(1)}, bf16[1,1,32,4096]{3,2,1,0:T(8,128)(2,1)}, u32[]{:S(2)}) %copy-start.2) | copy-done | bytes 262168
  2.5 0.0 copy-start.4
  2.5 0.9 %copy-done.4 = bf16[1,1,32,4096]{3,2,1,0:T(8,128)(2,1)S(1)} copy-done((bf16[1,1,32,4096]{3,2,1,0:T(8,128)(2,1)S(1)}, bf16[1,1,32,4096]{3,2,1,0:T(8,128)(2,1)}, u32[]{:S(2)}) %copy-start.4) | copy-done | bytes 262168
  3.5 0.0 copy-start.6
  3.5 0.9 %copy-done.6 = f32[1,1,6,64,32]{3,4,2,1,0:T(8,128)S(1)} copy-done((f32[1,1,6,64,32]{3,4,2,1,0:T(8,128)S(1)}, f32[1,1,6,64,32]{3,4,2,1,0:T(8,128)}, u32[]{:S(2)}) %copy-start.6) | copy-done | bytes 49176
  4.4 0.0 copy-start.8
  4.4 0.9 %copy-done.8 = f32[1,1,6,64,32]{3,4,2,1,0:T(8,128)S(1)} copy-done((f32[1,1,6,64,32]{3,4,2,1,0:T(8,128)S(1)}, f32[1,1,6,64,32]{3,4,2,1,0:T(8,128)}, u32[]{:S(2)}) %copy-start.8) | copy-done | bytes 49176
  5.3 0.0 copy-start.5
  5.3 0.2 shard_map.104
  5.5 2.7 %collective-permute-start = (bf16[16,7936]{1,0:T(8,128)(2,1)S(1)}, bf16[16,7936]{1,0:T(8,128)(2,1)S(1)}, u32[]{:S(2)}, u32[]{:S(2)}) collective-permute-start(bf16[16,7936]{1,0:T(8,128)(2,1)S(1)} %get-tuple-element.28), channel_id=1, source_target_pairs={{0,16},{16,0},{32,48},{48,32},{64,80},{80,64},{96,112},{112,96},{1... | collective-permute-start | bytes 761864 | tf_op jit(solution)/shard_map/ppermute | solution.py:532
  8.2 0.0 copy-start.1
  8.2 0.0 copy-start.3
  8.2 4.6 %collective-permute-start.1 = (bf16[16,7936]{1,0:T(8,128)(2,1)S(1)}, bf16[16,7936]{1,0:T(8,128)(2,1)S(1)}, u32[]{:S(2)}, u32[]{:S(2)}) collective-permute-start(bf16[16,7936]{1,0:T(8,128)(2,1)S(1)} %get-tuple-element.29), channel_id=1, source_target_pairs={{16,32},{32,16},{48,64},{64,48},{80,96},{96,80},{112,128},{128,112... | collective-permute-start | bytes 761864 | tf_op jit(solution)/shard_map/ppermute | solution.py:532
  12.8 0.0 copy-done.5
  12.8 0.3 shard_map.109
  13.2 0.0 copy-done.1
  13.2 0.0 copy-done.3
  13.2 0.8 %shard_map.103 = (bf16[2048,128]{1,0:T(8,128)(2,1)S(1)}, f32[32,64]{1,0:T(8,128)S(1)}) custom-call(bf16[32,4096]{1,0:T(8,128)(2,1)S(1)} %bitcast.18, bf16[32,4096]{1,0:T(8,128)(2,1)S(1)} %bitcast.21), custom_call_target="tpu_custom_call" | custom-call | flops 1000000000 | bytes 1048576 | tf_op jit(solution)/shard_map/pallas_call | solution.py:514
  14.0 6.6 %collective-permute-done.x_even = bf16[16,7936]{1,0:T(8,128)(2,1)S(1)} collective-permute-done((bf16[16,7936]{1,0:T(8,128)(2,1)S(1)}, bf16[16,7936]{1,0:T(8,128)(2,1)S(1)}, u32[]{:S(2)}, u32[]{:S(2)}) %collective-permute-start) | collective-permute-done | bytes 253984 | tf_op jit(solution)/shard_map/ppermute | solution.py:532
  20.7 0.0 collective-permute-done.1.x_odd
  20.7 0.4 %shard_map.105 = (bf16[16,8064]{1,0:T(8,128)(2,1)S(1)}, bf16[16,8064]{1,0:T(8,128)(2,1)S(1)}, bf16[16,7936]{1,0:T(8,128)(2,1)S(1)}, bf16[16,7936]{1,0:T(8,128)(2,1)S(1)}) custom-call(bf16[32,4096]{1,0:T(8,128)(2,1)S(1)} %bitcast.19, bf16[32,4096]{1,0:T(8,128)(2,1)S(1)} %bitcast.22, bf16[32,4096]{1,0:T(8,128)(2,1)S(1)} %bitcast.25, ...), custom_call_target="tpu_custom_call" | custom-call | flops 100000000 | bytes 1048576 | tf_op jit(solution)/shard_map/pallas_call | solution.py:514
  21.1 1.9 %collective-permute-start.2 = (bf16[16,8064]{1,0:T(8,128)(2,1)S(1)}, bf16[16,8064]{1,0:T(8,128)(2,1)S(1)}, u32[]{:S(2)}, u32[]{:S(2)}) collective-permute-start(bf16[16,8064]{1,0:T(8,128)(2,1)S(1)} %get-tuple-element.33), channel_id=1, source_target_pairs={{0,1},{1,0},{2,3},{3,2},{4,5},{5,4},{6,7},{7,6},{8,9},{9,8},{10,11... | collective-permute-start | bytes 774152 | tf_op jit(solution)/shard_map/ppermute | solution.py:532
  23.1 5.9 %collective-permute-start.3 = (bf16[16,8064]{1,0:T(8,128)(2,1)S(1)}, bf16[16,8064]{1,0:T(8,128)(2,1)S(1)}, u32[]{:S(2)}, u32[]{:S(2)}) collective-permute-start(bf16[16,8064]{1,0:T(8,128)(2,1)S(1)} %get-tuple-element.34), channel_id=1, source_target_pairs={{1,2},{2,1},{3,4},{4,3},{5,6},{6,5},{7,8},{8,7},{9,10},{10,9},{11,... | collective-permute-start | bytes 774152 | tf_op jit(solution)/shard_map/ppermute | solution.py:532
  28.9 0.8 %shard_map.106 = (bf16[2048,128]{1,0:T(8,128)(2,1)S(1)}, f32[32,64]{1,0:T(8,128)S(1)}) custom-call(bf16[16,7936]{1,0:T(8,128)(2,1)S(1)} %get-tuple-element.30.low.x_low, bf16[16,7936]{1,0:T(8,128)(2,1)S(1)} %get-tuple-element.31.high.x_high), custom_call_target="tpu_custom_call" | custom-call | flops 1000000000 | bytes 1048576 | tf_op jit(solution)/shard_map/pallas_call | solution.py:514
  29.8 0.0 copy-start.10
  29.8 0.0 copy-start.11
  29.8 0.6 %copy-done.10 = s32[1,1,32]{2,1,0:T(1,128)S(1)} copy-done((s32[1,1,32]{2,1,0:T(1,128)S(1)}, s32[1,1,32]{2,1,0:T(1,128)}, u32[]{:S(2)}) %copy-start.10) | copy-done | bytes 152
  30.4 0.0 copy-done.11
  30.5 4.9 %shard_map.110 = (f32[256,256]{1,0:T(8,128)}, f32[4,256,256]{2,1,0:T(8,128)}, bf16[2,256,512]{2,1,0:T(8,128)(2,1)S(1)}) custom-call(s32[32]{0:T(128)S(1)} %bitcast.30, s32[24]{0:T(128)S(1)} %bitcast.31, bf16[2048,128]{1,0:T(8,128)(2,1)S(1)} %get-tuple-element.41.t16, bf16[512,128]{1,0:T(8,128)(2,1)S(1)} %get-tuple-element.42.plus_y, ...), custom_call_target="tpu_custom_call" | custom-call | flops 4000000000 | bytes 4194304 | tf_op jit(solution)/shard_map/pallas_call | solution.py:514
  35.4 0.0 collective-permute-done.2.even
  35.4 0.0 collective-permute-done.3.odd
  35.4 1.0 %shard_map.107 = (bf16[2048,128]{1,0:T(8,128)(2,1)S(1)}, f32[32,64]{1,0:T(8,128)S(1)}, bf16[16,8064]{1,0:T(8,128)(2,1)S(1)}, bf16[16,8064]{1,0:T(8,128)(2,1)S(1)}) custom-call(bf16[16,8064]{1,0:T(8,128)(2,1)S(1)} %collective-permute-done.2.even, bf16[16,8064]{1,0:T(8,128)(2,1)S(1)} %collective-permute-done.3.odd), custom_call_target="tpu_custom_call" | custom-call | flops 1000000000 | bytes 1048576 | tf_op jit(solution)/shard_map/pallas_call | solution.py:514
  36.4 0.0 copy-start.7
  36.4 0.0 copy-start.9
  36.4 1.9 %shard_map.111 = f32[4,256,256]{2,1,0:T(8,128)} custom-call(s32[24]{0:T(128)S(1)} %bitcast.32, bf16[2048,128]{1,0:T(8,128)(2,1)S(1)} %get-tuple-element.25.w, bf16[2,256,512]{2,1,0:T(8,128)(2,1)S(1)} %get-tuple-element.45.edge_columns, bf16[16,8064]{1,0:T(8,128)(2,1)S(1)} %get-tuple-element.39.y_low, ...), custom_call_target="tpu_custom_call", output_to_operand_aliasing={{}: (5, {})} | custom-call | flops 1000000000 | bytes 1048576 | tf_op jit(solution)/shard_map/pallas_call | solution.py:514
  38.3 0.0 copy-start.12
  38.3 0.0 copy-done.7
  38.3 0.0 copy-done.9
  38.3 0.6 %copy-done.12 = f32[2]{0:T(128)S(1)} copy-done((f32[2]{0:T(128)S(1)}, f32[2]{0:T(128)}, u32[]{:S(2)}) %copy-start.12) | copy-done | bytes 32
  38.9 4.1 %shard_map.108 = f32[6,32,64]{2,1,0:T(8,128)} custom-call(f32[6,32,64]{2,1,0:T(8,128)S(1)} %bitcast.27, f32[6,32,64]{2,1,0:T(8,128)S(1)} %bitcast.29, bf16[2048,128]{1,0:T(8,128)(2,1)S(1)} %get-tuple-element.25.w, bf16[2048,128]{1,0:T(8,128)(2,1)S(1)} %get-tuple-element.32.wx, bf16[2048,128]{1,0:T(8,128)(2,1)S(1)} %get-tuple-element.35.wy, ...), custom_call_target="tpu_custom_call" | custom-call | flops 1000000000 | bytes 1048576 | tf_op jit(solution)/shard_map/pallas_call | solution.py:514
Async XLA Ops:
  0.6 1.0 %copy-start = (bf16[1,1,32,4096]{3,2,1,0:T(8,128)(2,1)S(1)}, bf16[1,1,32,4096]{3,2,1,0:T(8,128)(2,1)}, u32[]{:S(2)}) copy-start(bf16[1,1,32,4096]{3,2,1,0:T(8,128)(2,1)} %param.8) | copy-start | bytes 786436
  1.6 0.9 %copy-start.2 = (bf16[1,1,32,4096]{3,2,1,0:T(8,128)(2,1)S(1)}, bf16[1,1,32,4096]{3,2,1,0:T(8,128)(2,1)}, u32[]{:S(2)}) copy-start(bf16[1,1,32,4096]{3,2,1,0:T(8,128)(2,1)} %param.9) | copy-start | bytes 786436
  2.5 0.9 %copy-start.4 = (bf16[1,1,32,4096]{3,2,1,0:T(8,128)(2,1)S(1)}, bf16[1,1,32,4096]{3,2,1,0:T(8,128)(2,1)}, u32[]{:S(2)}) copy-start(bf16[1,1,32,4096]{3,2,1,0:T(8,128)(2,1)} %param.10) | copy-start | bytes 786436
  3.5 0.9 %copy-start.6 = (f32[1,1,6,64,32]{3,4,2,1,0:T(8,128)S(1)}, f32[1,1,6,64,32]{3,4,2,1,0:T(8,128)}, u32[]{:S(2)}) copy-start(f32[1,1,6,64,32]{3,4,2,1,0:T(8,128)} %param.14) | copy-start | bytes 147460
  4.4 0.9 %copy-start.8 = (f32[1,1,6,64,32]{3,4,2,1,0:T(8,128)S(1)}, f32[1,1,6,64,32]{3,4,2,1,0:T(8,128)}, u32[]{:S(2)}) copy-start(f32[1,1,6,64,32]{3,4,2,1,0:T(8,128)} %param.13) | copy-start | bytes 147460
  5.3 7.6 %copy-start.5 = (bf16[1,1,32,4096]{3,2,1,0:T(8,128)(2,1)S(1)}, bf16[1,1,32,4096]{3,2,1,0:T(8,128)(2,1)}, u32[]{:S(2)}) copy-start(bf16[1,1,32,4096]{3,2,1,0:T(8,128)(2,1)} %param.10) | copy-start | bytes 786436
  5.5 15.2 %collective-permute-start = (bf16[16,7936]{1,0:T(8,128)(2,1)S(1)}, bf16[16,7936]{1,0:T(8,128)(2,1)S(1)}, u32[]{:S(2)}, u32[]{:S(2)}) collective-permute-start(bf16[16,7936]{1,0:T(8,128)(2,1)S(1)} %get-tuple-element.28), channel_id=1, source_target_pairs={{0,16},{16,0},{32,48},{48,32},{64,80},{80,64},{96,112},{112,96},{1... | collective-permute-start | bytes 761864 | tf_op jit(solution)/shard_map/ppermute | solution.py:532
  8.2 5.0 %copy-start.1 = (bf16[1,1,32,4096]{3,2,1,0:T(8,128)(2,1)S(1)}, bf16[1,1,32,4096]{3,2,1,0:T(8,128)(2,1)}, u32[]{:S(2)}) copy-start(bf16[1,1,32,4096]{3,2,1,0:T(8,128)(2,1)} %param.8) | copy-start | bytes 786436
  8.2 5.0 %copy-start.3 = (bf16[1,1,32,4096]{3,2,1,0:T(8,128)(2,1)S(1)}, bf16[1,1,32,4096]{3,2,1,0:T(8,128)(2,1)}, u32[]{:S(2)}) copy-start(bf16[1,1,32,4096]{3,2,1,0:T(8,128)(2,1)} %param.9) | copy-start | bytes 786436
  8.2 12.4 %collective-permute-start.1 = (bf16[16,7936]{1,0:T(8,128)(2,1)S(1)}, bf16[16,7936]{1,0:T(8,128)(2,1)S(1)}, u32[]{:S(2)}, u32[]{:S(2)}) collective-permute-start(bf16[16,7936]{1,0:T(8,128)(2,1)S(1)} %get-tuple-element.29), channel_id=1, source_target_pairs={{16,32},{32,16},{48,64},{64,48},{80,96},{96,80},{112,128},{128,112... | collective-permute-start | bytes 761864 | tf_op jit(solution)/shard_map/ppermute | solution.py:532
  21.1 14.2 %collective-permute-start.2 = (bf16[16,8064]{1,0:T(8,128)(2,1)S(1)}, bf16[16,8064]{1,0:T(8,128)(2,1)S(1)}, u32[]{:S(2)}, u32[]{:S(2)}) collective-permute-start(bf16[16,8064]{1,0:T(8,128)(2,1)S(1)} %get-tuple-element.33), channel_id=1, source_target_pairs={{0,1},{1,0},{2,3},{3,2},{4,5},{5,4},{6,7},{7,6},{8,9},{9,8},{10,11... | collective-permute-start | bytes 774152 | tf_op jit(solution)/shard_map/ppermute | solution.py:532
  23.1 12.3 %collective-permute-start.3 = (bf16[16,8064]{1,0:T(8,128)(2,1)S(1)}, bf16[16,8064]{1,0:T(8,128)(2,1)S(1)}, u32[]{:S(2)}, u32[]{:S(2)}) collective-permute-start(bf16[16,8064]{1,0:T(8,128)(2,1)S(1)} %get-tuple-element.34), channel_id=1, source_target_pairs={{1,2},{2,1},{3,4},{4,3},{5,6},{6,5},{7,8},{8,7},{9,10},{10,9},{11,... | collective-permute-start | bytes 774152 | tf_op jit(solution)/shard_map/ppermute | solution.py:532
  29.8 0.7 %copy-start.10 = (s32[1,1,32]{2,1,0:T(1,128)S(1)}, s32[1,1,32]{2,1,0:T(1,128)}, u32[]{:S(2)}) copy-start(s32[1,1,32]{2,1,0:T(1,128)} %param.11) | copy-start | bytes 388
  29.8 0.7 %copy-start.11 = (s32[1,1,24]{2,1,0:T(1,128)S(1)}, s32[1,1,24]{2,1,0:T(1,128)}, u32[]{:S(2)}) copy-start(s32[1,1,24]{2,1,0:T(1,128)} %param.12) | copy-start | bytes 292
  36.4 1.9 %copy-start.7 = (f32[1,1,6,64,32]{3,4,2,1,0:T(8,128)S(1)}, f32[1,1,6,64,32]{3,4,2,1,0:T(8,128)}, u32[]{:S(2)}) copy-start(f32[1,1,6,64,32]{3,4,2,1,0:T(8,128)} %param.14) | copy-start | bytes 147460
  36.4 1.9 %copy-start.9 = (f32[1,1,6,64,32]{3,4,2,1,0:T(8,128)S(1)}, f32[1,1,6,64,32]{3,4,2,1,0:T(8,128)}, u32[]{:S(2)}) copy-start(f32[1,1,6,64,32]{3,4,2,1,0:T(8,128)} %param.13) | copy-start | bytes 147460
  38.3 0.7 %copy-start.12 = (f32[2]{0:T(128)S(1)}, f32[2]{0:T(128)}, u32[]{:S(2)}) copy-start(f32[2]{0:T(128)} %param.15) | copy-start | bytes 28

commit v3 on v2

--- a/solution.py
+++ b/solution.py
@@ -9,17 +9,17 @@
 F32, BF16 = jnp.float32, jnp.bfloat16
 VMEM = pl.BlockSpec(memory_space=pltpu.VMEM)
 SMEM = pl.BlockSpec(memory_space=pltpu.SMEM)
-ANY = pl.BlockSpec(memory_space=pl.ANY)
+HBM = pl.BlockSpec(memory_space=pltpu.HBM)
 NT = (((1,), (1,)), ((), ()))
 NN = (((1,), (0,)), ((), ()))
 
 XA, XB = 0, 2048
 XC = 4096
 XD = 5120
-XG = 5888
-XR = 6656
-XT = 7424
-XLEN = 7936
+XH = 5888
+XK = 6272
+XT = 6528
+XLEN = 7040
 YA, YB = 0, 2048
 YF = 4096
 YC = 5120
@@ -80,7 +80,24 @@
     return jnp.concatenate([both[n * NE : (n + 1) * NE] for n in range(NRHS)], 1)
 
 
-def pack_x_kernel(blocks, faces, tent, guess, rhs, even, odd, guess_packed, rhs_packed):
+def trace_lanes(side):
+    row, lane = iota((768, 256), 0), iota((768, 256), 1)
+    source = lane // 32 * 128 + lane // 16 % 2 * 64 + lane % 16 + 48 * side
+    return onehot((row == source) & (lane < 192))
+
+
+def pack_x_kernel(blocks_in, faces_in, tent_in, guess_in, rhs_in, bounds_in, even, odd, guess_packed, rhs_packed,
+                  blocks, faces, tent, guess, rhs, bounds, sems):
+    copies = [
+        pltpu.make_async_copy(source, target, sems.at[i])
+        for i, (source, target) in enumerate((
+            (guess_in, guess), (rhs_in, rhs), (blocks_in, blocks), (faces_in, faces), (tent_in, tent), (bounds_in, bounds),
+        ))
+    ]
+    for copy in copies:
+        copy.start()
+    for copy in copies:
+        copy.wait()
     g = pack_lanes(guess[...].reshape(NRHS * NE, 64))
     r = pack_lanes(rhs[...].reshape(NRHS * NE, 64))
     guess_packed[...] = g.astype(BF16)
@@ -111,18 +128,18 @@
         put(XB + h * 1024, 1024, lambda s: over(of(faces, 0, s, h * 1024, 1024), of(faces, 0, s, h * 1024 + 2048, 1024)))
     put(XC, 1024, lambda s: over(of(blocks, 1, s, 3072 * s, 1024), face_traces(s)))
     put(XD, 768, lambda s: over(packed(g, 0, s), packed(g, 1, s)))
-    put(XG, 768, lambda s: over(packed(g, 2, s), packed(r, 0, s)))
-    put(XR, 768, lambda s: over(packed(r, 1, s), jnp.zeros((8, 768), F32)))
+    put(XH, 384, lambda s: halves(packed(r, 0, s)))
+    put(XK, 256, lambda s: dot(over(packed(g, 2, s), packed(r, 1, s)).astype(BF16), trace_lanes(s)))
     put(XT, 512, lambda s: halves(of(tent, 0, s, 3072 * s, 1024)))
 
 
 def pack_y_kernel(blocks, faces, tent, guess_packed, rhs_packed, x_even, x_odd, even, odd, low, high):
     first = parity("bx") == 0
-    for start in range(0, XLEN, 256):
-        a = x_even[:, start : start + 256].astype(F32)
-        b = x_odd[:, start : start + 256].astype(F32)
-        low[:, start : start + 256] = jnp.where(first, b, a).astype(BF16)
-        high[:, start : start + 256] = jnp.where(first, a, b).astype(BF16)
+    for start in range(0, XLEN, 128):
+        a = x_even[:, start : start + 128].astype(F32)
+        b = x_odd[:, start : start + 128].astype(F32)
+        low[:, start : start + 128] = jnp.where(first, b, a).astype(BF16)
+        high[:, start : start + 128] = jnp.where(first, a, b).astype(BF16)
     py = parity("by")
     is_first = py == 0
 
@@ -173,8 +190,11 @@
     own = guess_packed[...]
     rows = jnp.concatenate([own, low[:, XD : XD + 768], high[:, XD : XD + 768]], 0)
     g0, g1, g2 = dot(select(0, 0, 8), rows), dot(select(1, 0), rows), dot(select(2, columns=32), own)
-    rows = jnp.concatenate([rhs_packed[...], low[:, XG : XG + 768], high[:, XG : XG + 768]], 0)
-    r0, r1 = dot(select(0, 8), rows), dot(own1, rhs_packed[...])
+    cut = []
+    for h in range(2):
+        rows = [rhs_packed[:, h * 384 : h * 384 + 384], low[:, XH : XH + 384], high[:, XH : XH + 384]]
+        cut.append(dot(select(0, 8 * h), jnp.concatenate(rows, 0)))
+    r0, r1 = jnp.concatenate(cut, 1), dot(own1, rhs_packed[...])
     put(YD, (over(g0[:8], g1[:8]), over(g0[8:], g1[8:])))
     put(YG, (over(g2[:8], r0[:8]), over(g2[8:], r0[8:])))
     put(YR, both(halves, r1))
@@ -248,7 +268,7 @@
     return ref[:, lane : lane + 128].astype(F32)[row : row + 8]
 
 
-def halo_x_kernel(low, high, w, inverse, *scratch):
+def halo_x(low, high, w, inverse, *scratch):
     zero = jnp.zeros(NOTHING, F32)
 
     def block(c):
@@ -265,7 +285,7 @@
     operators(block, face, w, inverse, *scratch)
 
 
-def halo_y_kernel(even, odd, w, inverse, low, high, *scratch):
+def halo_y(even, odd, w, inverse, low, high, *scratch):
     first = parity("by") == 0
     for start in range(0, YLEN, 128):
         a = even[:, start : start + 128].astype(F32)
@@ -319,22 +339,21 @@
 )
 
 
-def smooth_kernel(guess, rhs, w, wx, wy, inv, inv_x, inv_y, bounds, x_low, x_high, y_low, y_high, smoothed,
-                  g_ref, r_ref, i_ref, t_ref, x_ref, a_ref):
+def smooth(guess, rhs, w, wx, wy, inv, inv_x, inv_y, bounds, x_low, x_high, y_low, y_high, smoothed,
+           g_ref, r_ref, i_ref, t_ref, x_ref, a_ref):
     def joined(value):
         return value + pltpu.roll(value, 64, 1)
 
-    def fill(ref, own, x_parts, y_parts):
+    def fill(ref, own, x_value, x_count, y_parts):
         ref[...] = jnp.zeros((SPAN, 128), F32)
         for n in range(NRHS):
             for ix in range(EX):
                 row = n * EXT + (ix + 3) * 16
                 ref[row : row + 8, 0:64] = own[n, ix * 8 : ix * 8 + 8, :]
-            for side, message in enumerate((x_low, x_high)):
-                for k, (start, top) in enumerate(x_parts):
+            for side in range(2):
+                for k in range(x_count):
                     row = n * EXT + (7 + k if side else 2 - k) * 16
-                    value = message[:, start + n * 128 : start + n * 128 + 128].astype(F32)
-                    ref[row : row + 8, :] = joined(value[8 * top : 8 * top + 8])
+                    ref[row : row + 8, :] = joined(x_value(side, k, n))
             for side, message in enumerate((y_low, y_high)):
                 for k, (start, top, half) in enumerate(y_parts):
                     value = part(message, start, n, half) if half else (
@@ -342,8 +361,23 @@
                     )
                     ref[pl.ds(n * EXT + 16 + (8 + k if side else 15 - k), 8, stride=16), :] = joined(value)
 
-    fill(g_ref, guess, ((XD, 0), (XD, 1), (XG, 0)), ((YD, 0, 0), (YD, 1, 0), (YG, 0, 0)))
-    fill(r_ref, rhs, ((XG, 1), (XR, 0)), ((YG, 1, 0), (YR, 0, 3)))
+    x_messages = (x_low, x_high)
+    spread = [lax.dot_general(m[:, XK : XK + 256], trace_lanes(1 - s), NT, preferred_element_type=F32)
+              for s, m in enumerate(x_messages)]
+
+    def whole(side, start, n):
+        return x_messages[side][:, start + n * 128 : start + n * 128 + 128].astype(F32)
+
+    def x_guess(side, k, n):
+        if k == 2:
+            return spread[side][0:8, n * 128 : n * 128 + 128]
+        return whole(side, XD, n)[8 * k : 8 * k + 8]
+
+    def x_rhs(side, k, n):
+        return spread[side][8:16, n * 128 : n * 128 + 128] if k else part(x_messages[side], XH, n, 3)
+
+    fill(g_ref, guess, x_guess, 3, ((YD, 0, 0), (YD, 1, 0), (YG, 0, 0)))
+    fill(r_ref, rhs, x_rhs, 2, ((YG, 1, 0), (YR, 0, 3)))
     i_ref[...] = jnp.ones((EXT, 128), F32)
     wide = lambda value: jnp.concatenate([value, value], 1)
     for ix in range(EX):
@@ -426,10 +460,7 @@
     return jnp.concatenate([none(64 + 16 * f), rows] + ([none(48 - 16 * f)] if f < 3 else []), 0)
 
 
-def galerkin_kernel(labels, side_labels, t16, plus_y, minus_y, w, x_low, x_high, local, ghost, edge_columns,
-                    tt, xlow, xhigh, masks, big):
-    ghost_rows(x_low, XT, xlow)
-    ghost_rows(x_high, XT, xhigh)
+def galerkin_kernel(labels, t16, plus_y, minus_y, w, local, edge_columns, tt, masks, big):
     label_masks(masks)
     lane128 = iota((64, 128), 1)
     for pair in range(NE // 2):
@@ -442,10 +473,12 @@
                 jnp.where(second == a, 1.0, 0.0),
             )
             tt[a * 64 : a * 64 + 64, pair * 128 : pair * 128 + 128] = (turned * keep).astype(BF16)
+    edge_columns[0] = tt[:, :512]
+    edge_columns[1] = tt[:, 1536:]
     for f in range(2):
         for ix in range(EX):
             start = (4 * ix + 3 * f) * 128
-            edge_columns[f, :, ix * 128 : ix * 128 + 128] = tt[:, start : start + 128]
+            edge_columns[2 + f, :, ix * 128 : ix * 128 + 128] = tt[:, start : start + 128]
 
     def row_of_elements(ix, carry):
         for iy in range(EY):
@@ -454,8 +487,8 @@
             before = pl.multiple_of(jnp.maximum(e - 8, 0) * 64, 64)
             after = pl.multiple_of(jnp.minimum(e + 8, 31) * 64, 64)
             rows = [
-                jnp.where(ix == 0, xlow[iy * 16 : iy * 16 + 16, :], t16[pl.ds(before + 48, 16), :].astype(F32)).astype(BF16),
-                jnp.where(ix == 3, xhigh[iy * 16 : iy * 16 + 16, :], t16[pl.ds(after, 16), :].astype(F32)).astype(BF16),
+                t16[pl.ds(before + 48, 16), :],
+                t16[pl.ds(after, 16), :],
             ]
             if iy > 0:
                 rows.append(plus_y[pl.ds(pl.multiple_of((e - 1) * 16, 16), 16), :])
@@ -467,11 +500,9 @@
             columns += [face_column(f, value) for f, value in enumerate(rows)]
             pieces = dot(w[own, :], jnp.concatenate(columns, 1)).astype(BF16)
             piece = lambda s: pieces[:, s * 128 : s * 128 + 128]
-            label0 = jnp.where(ix == 0, side_labels[iy], labels[jnp.maximum(e - 8, 0)])
-            label1 = jnp.where(ix == 3, side_labels[8 + iy], labels[jnp.minimum(e + 8, 31)])
             big[0, own, :] = masked(masks, piece(0), labels[e])
-            big[1, own, :] = masked(masks, piece(1), label0)
-            big[2, own, :] = masked(masks, piece(2), label1)
+            big[1, own, :] = masked(masks, piece(1), labels[jnp.maximum(e - 8, 0)])
+            big[2, own, :] = masked(masks, piece(2), labels[jnp.minimum(e + 8, 31)])
             nothing = jnp.zeros((64, 256), BF16)
             big[3, own, :] = masked(masks, piece(3), labels[e - 1]) if iy > 0 else nothing
             big[4, own, :] = masked(masks, piece(4), labels[e + 1]) if iy < 7 else nothing
@@ -485,27 +516,46 @@
         + dot(tt[...], big[3])
         + dot(tt[...], big[4])
     )
-    ghost[0] = dot(tt[:, :512], big[1, :512, :])
-    ghost[1] = dot(tt[:, 1536:], big[2, 1536:, :])
-    ghost[2] = jnp.zeros((256, 256), F32)
-    ghost[3] = jnp.zeros((256, 256), F32)
-
-
-def ghost_y_kernel(side_labels, w, edge_columns, y_low, y_high, ghost_in, ghost, rows, masks, side, result, sems):
+
+
+def ghost_block(face, message, start, first_row, elements, side_labels, label_start, w, columns, rows, masks, side, result):
+    ghost_rows(message, start, rows)
+    for i, (e, place) in enumerate(elements):
+        near = rows[(i + first_row) * 16 : (i + first_row) * 16 + 16, :].astype(BF16)
+        piece = dot(w[e * 64 : e * 64 + 64, :], face_column(face, near)).astype(BF16)
+        side[place : place + 64, :] = masked(masks, piece, side_labels[label_start + i])
+    result[...] = dot(columns, side[...])
+
+
+def middle_kernel(side_labels, w, edge_columns, x_low, x_high, wx, inverse_x, ghost,
+                  stage, fstage, w32, rows, masks, side, result, sems):
+    label_masks(masks)
+    copies = []
+    for f, message in enumerate((x_low, x_high)):
+        elements = [(24 * f + iy, iy * 64) for iy in range(EY)]
+        ghost_block(f, message, XT, 0, elements, side_labels, 8 * f, w, edge_columns[f], rows, masks, side, result.at[f])
+        copies.append(pltpu.make_async_copy(result.at[f], ghost.at[f], sems.at[f]))
+        copies[-1].start()
+    halo_x(x_low, x_high, wx, inverse_x, stage, fstage, w32)
+    for copy in copies:
+        copy.wait()
+
+
+def finish_kernel(side_labels, guess, rhs, w, wx, inv, inv_x, bounds, x_low, x_high, y_even, y_odd, edge_columns, ghost_in,
+                  smoothed, ghost, wy, inv_y, y_low, y_high, stage, fstage, w32, g_ref, r_ref, i_ref, t_ref, x_ref, a_ref,
+                  rows, masks, side, result, sems):
+    halo_y(y_even, y_odd, wy, inv_y, y_low, y_high, stage, fstage, w32)
     label_masks(masks)
     copies = []
     for f, message in enumerate((y_low, y_high)):
-        ghost_rows(message, YT, rows)
         side[...] = jnp.zeros((512, 256), BF16)
-        for ix in range(EX):
-            e = ix * EY + 7 * f
-            near = rows[(ix + 2) * 16 : (ix + 2) * 16 + 16, :].astype(BF16)
-            piece = dot(w[e * 64 : e * 64 + 64, :], face_column(2 + f, near)).astype(BF16)
-            start = ix * 128 + 64 * f
-            side[start : start + 64, :] = masked(masks, piece, side_labels[16 + 4 * f + ix])
-        result[f] = dot(edge_columns[f], side[...])
+        elements = [(8 * ix + 7 * f, ix * 128 + 64 * f) for ix in range(EX)]
+        ghost_block(2 + f, message, YT, 2, elements, side_labels, 16 + 4 * f, w, edge_columns[2 + f], rows, masks, side,
+                    result.at[f])
         copies.append(pltpu.make_async_copy(result.at[f], ghost.at[2 + f], sems.at[f]))
         copies[-1].start()
+    smooth(guess, rhs, w, wx, wy, inv, inv_x, inv_y, bounds, x_low, x_high, y_low, y_high, smoothed,
+           g_ref, r_ref, i_ref, t_ref, x_ref, a_ref)
     for copy in copies:
         copy.wait()
 
@@ -540,69 +590,61 @@
 STAGES = [pltpu.VMEM((4, 256, 128), F32), pltpu.VMEM((4, 256, 128), F32), pltpu.VMEM((2048, 128), F32)]
 
 
+GHOST = [
+    pltpu.VMEM((128, 128), F32),
+    pltpu.VMEM((64, 256), BF16),
+    pltpu.VMEM((512, 256), BF16),
+    pltpu.VMEM((2, 256, 256), F32),
+    pltpu.SemaphoreType.DMA((2,)),
+]
+
+
 def on_device(blocks, faces, tentative, aggregate, ghost_labels, rhs, guess, bounds):
-    blocks, faces, tentative = [a.reshape(NE, 4096) for a in (blocks, faces, tentative)]
+    wide = lambda *shape: shaped(*shape, dtype=F32)
     rhs = jnp.swapaxes(rhs[0, 0], 1, 2)
     guess = jnp.swapaxes(guess[0, 0], 1, 2)
     labels, side_labels = aggregate.reshape(NE), ghost_labels.reshape(24)
-    packed = shaped(NE, 768)
-    even, odd, guess_packed, rhs_packed = call(
-        pack_x_kernel, [shaped(16, XLEN)] * 2 + [packed] * 2, [],
-        (blocks, faces, tentative, guess, rhs), 10**6, 2**20,
+    even, odd, guess_packed, rhs_packed, blocks, faces, tentative, guess, rhs, bounds = call(
+        pack_x_kernel,
+        [shaped(16, XLEN)] * 2 + [shaped(NE, 768)] * 2 + [shaped(NE, 4096)] * 3
+        + [wide(NRHS, NE, 64)] * 2 + [wide(1, 2)],
+        [pltpu.SemaphoreType.DMA((6,))],
+        [a.reshape(NE, 4096) for a in (blocks, faces, tentative)] + [guess, rhs, bounds.reshape(1, 2)],
+        10**6, 2**20, [HBM] * 6,
     )
     even, odd = exchange((even, odd), "bx")
-    w, inverse = call(
-        own_kernel, [shaped(2048, 128), shaped(NE, 64, dtype=F32)], STAGES, (blocks, faces), 10**9, 2**20
-    )
+    w, inverse = call(own_kernel, [shaped(2048, 128), wide(NE, 64)], STAGES, (blocks, faces), 10**9, 2**20)
     t16, plus_y, minus_y = call(
         prolong_kernel, [shaped(2048, 128), shaped(512, 128), shaped(512, 128)],
         [STAGES[0], STAGES[2]], (tentative,), 5 * 10**8, 2**20,
     )
+    local, edge_columns = call(
+        galerkin_kernel,
+        [wide(256, 256), shaped(4, 256, 512)],
+        [pltpu.VMEM((256, 2048), BF16), GHOST[1], pltpu.VMEM((5, 2048, 256), BF16)],
+        (labels, t16, plus_y, minus_y, w),
+        4 * 10**9, 4 * 2**20, [SMEM] + [VMEM] * 4,
+    )
     even, odd, x_low, x_high = call(
         pack_y_kernel, [shaped(16, YLEN)] * 2 + [shaped(16, XLEN)] * 2, [],
         (blocks, faces, tentative, guess_packed, rhs_packed, even, odd), 10**8, 2**20,
     )
     even, odd = exchange((even, odd), "by")
-    wx, inverse_x = call(
-        halo_x_kernel, [shaped(2048, 128), shaped(NE, 64, dtype=F32)], STAGES, (x_low, x_high), 10**9, 2**20
-    )
-    local, ghost, edge_columns = call(
-        galerkin_kernel,
-        [shaped(256, 256, dtype=F32), shaped(4, 256, 256, dtype=F32), shaped(2, 256, 512)],
-        [
-            pltpu.VMEM((256, 2048), BF16),
-            pltpu.VMEM((128, 128), F32),
-            pltpu.VMEM((128, 128), F32),
-            pltpu.VMEM((64, 256), BF16),
-            pltpu.VMEM((5, 2048, 256), BF16),
-        ],
-        (labels, side_labels, t16, plus_y, minus_y, w, x_low, x_high),
-        4 * 10**9, 4 * 2**20,
-        [SMEM, SMEM] + [VMEM] * 6,
-    )
-    wy, inverse_y, y_low, y_high = call(
-        halo_y_kernel, [shaped(2048, 128), shaped(NE, 64, dtype=F32)] + [shaped(16, YLEN)] * 2, STAGES,
-        (even, odd), 10**9, 2**20,
-    )
-    (smoothed,) = call(
-        smooth_kernel, [shaped(NRHS, NE, 64, dtype=F32)],
-        [pltpu.VMEM((SPAN, 128), F32)] * 2
+    wx, inverse_x, ghost = call(
+        middle_kernel, [shaped(2048, 128), wide(NE, 64), wide(4, 256, 256)], STAGES + GHOST,
+        (side_labels, w, edge_columns, x_low, x_high), 10**9, 2**20,
+        [SMEM] + [VMEM] * 4, [VMEM, VMEM, HBM],
+    )
+    smoothed, ghost = call(
+        finish_kernel, [wide(NRHS, NE, 64), wide(4, 256, 256)],
+        [pltpu.VMEM((2048, 128), BF16), pltpu.VMEM((NE, 64), F32)] + [pltpu.VMEM((16, YLEN), BF16)] * 2
+        + STAGES
+        + [pltpu.VMEM((SPAN, 128), F32)] * 2
         + [pltpu.VMEM((EXT, 128), F32), pltpu.VMEM((SPAN, 128), F32)]
-        + [pltpu.VMEM((8 * EXT, 128), F32)] * 2,
-        (guess, rhs, w, wx, wy, inverse, inverse_x, inverse_y, bounds.reshape(1, 2), x_low, x_high, y_low, y_high),
-        10**9, 2**20,
-    )
-    (ghost,) = call(
-        ghost_y_kernel, [shaped(4, 256, 256, dtype=F32)],
-        [
-            pltpu.VMEM((128, 128), F32),
-            pltpu.VMEM((64, 256), BF16),
-            pltpu.VMEM((512, 256), BF16),
-            pltpu.VMEM((2, 256, 256), F32),
-            pltpu.SemaphoreType.DMA((2,)),
-        ],
-        (side_labels, w, edge_columns, y_low, y_high, ghost), 10**9, 2**20,
-        [SMEM] + [VMEM] * 4 + [ANY], [ANY], {5: 0},
+        + [pltpu.VMEM((8 * EXT, 128), F32)] * 2
+        + GHOST,
+        (side_labels, guess, rhs, w, wx, inverse, inverse_x, bounds, x_low, x_high, even, odd, edge_columns, ghost),
+        10**9, 2**20, [SMEM] + [VMEM] * 12 + [HBM], [VMEM, HBM], {13: 1},
     )
     return jnp.swapaxes(smoothed, 1, 2)[None, None], local[None, None], ghost[None, None]
 

time: 43.4 us -> 43.3 us (level)
  the two profiles are of different devices: /device:TPU:134 before, /device:TPU:6 now
where the time goes in v3:
time: 43.3 us; the launch traced here: 43 us
  Pallas kernels  15.1 us (35%)
  starting transfers between devices  15 us (35%)
  local copies, waits for them, and re-layouts  6.59 us (15%)
  waiting for transfers between devices  5.6 us (13%)
  between operations  0.74 us (2%)
    pallas_call x7, Pallas kernels, call(): pl.pallas_call(kernel, out_shape=outs, in_specs=in_specs or [VMEM] * len(...  15.1 us
    ppermute x4, starting transfers between devices, exchange(): out.append(lax.ppermute(message, axis, pairs))  15 us
    unnamed x16, local copies, waits for them, and re-layouts  6.59 us
    ppermute x4, waiting for transfers between devices, exchange(): out.append(lax.ppermute(message, axis, pairs))  5.6 us
  transfers between devices with their start and end apart: 4, of which 1 were waited for; matrix products, arithmetic and copies ran while one was open for 0% of the time, Pallas kernels for 18%

profile of v3, /device:TPU:6, one launch (start us, length us, event | category | flops | bytes accessed | tf_op | source)
XLA Modules:
  0.0 43.0 jit_solution(2027160550059743708)
XLA Ops:
  0.6 0.0 copy-start.5
  0.6 0.6 %copy-done.5 = f32[2]{0:T(128)S(1)} copy-done((f32[2]{0:T(128)S(1)}, f32[2]{0:T(128)}, u32[]{:S(2)}) %copy-start.5) | copy-done | bytes 32
  1.3 0.0 copy-start
  1.3 0.9 %copy-done = bf16[1,1,32,4096]{3,2,1,0:T(8,128)(2,1)S(1)} copy-done((bf16[1,1,32,4096]{3,2,1,0:T(8,128)(2,1)S(1)}, bf16[1,1,32,4096]{3,2,1,0:T(8,128)(2,1)}, u32[]{:S(2)}) %copy-start) | copy-done | bytes 262168
  2.2 0.0 copy-start.1
  2.2 0.9 %copy-done.1 = bf16[1,1,32,4096]{3,2,1,0:T(8,128)(2,1)S(1)} copy-done((bf16[1,1,32,4096]{3,2,1,0:T(8,128)(2,1)S(1)}, bf16[1,1,32,4096]{3,2,1,0:T(8,128)(2,1)}, u32[]{:S(2)}) %copy-start.1) | copy-done | bytes 262168
  3.2 0.0 copy-start.2
  3.2 0.9 %copy-done.2 = bf16[1,1,32,4096]{3,2,1,0:T(8,128)(2,1)S(1)} copy-done((bf16[1,1,32,4096]{3,2,1,0:T(8,128)(2,1)S(1)}, bf16[1,1,32,4096]{3,2,1,0:T(8,128)(2,1)}, u32[]{:S(2)}) %copy-start.2) | copy-done | bytes 262168
  4.1 0.0 copy-start.3
  4.1 0.9 %copy-done.3 = f32[1,1,6,64,32]{3,4,2,1,0:T(8,128)S(1)} copy-done((f32[1,1,6,64,32]{3,4,2,1,0:T(8,128)S(1)}, f32[1,1,6,64,32]{3,4,2,1,0:T(8,128)}, u32[]{:S(2)}) %copy-start.3) | copy-done | bytes 49176
  5.0 0.0 copy-start.4
  5.0 0.9 %copy-done.4 = f32[1,1,6,64,32]{3,4,2,1,0:T(8,128)S(1)} copy-done((f32[1,1,6,64,32]{3,4,2,1,0:T(8,128)S(1)}, f32[1,1,6,64,32]{3,4,2,1,0:T(8,128)}, u32[]{:S(2)}) %copy-start.4) | copy-done | bytes 49176
  5.9 0.8 %shard_map.103 = (bf16[16,7040]{1,0:T(8,128)(2,1)S(1)}, bf16[16,7040]{1,0:T(8,128)(2,1)S(1)}, bf16[32,768]{1,0:T(8,128)(2,1)S(1)}, bf16[32,768]{1,0:T(8,128)(2,1...) custom-call(bf16[32,4096]{1,0:T(8,128)(2,1)S(1)} %bitcast.17, ...), custom_call_target="tpu_custom_call" | custom-call | flops 1000000 | bytes 1048576 | tf_op jit(solution)/shard_map/pallas_call | solution.py:564
  6.7 2.7 %collective-permute-start = (bf16[16,7040]{1,0:T(8,128)(2,1)S(1)}, bf16[16,7040]{1,0:T(8,128)(2,1)S(1)}, u32[]{:S(2)}, u32[]{:S(2)}) collective-permute-start(bf16[16,7040]{1,0:T(8,128)(2,1)S(1)} %get-tuple-element.41), channel_id=1, source_target_pairs={{0,16},{16,0},{32,48},{48,32},{64,80},{80,64},{96,112},{112,96},{1... | collective-permute-start | bytes 675848 | tf_op jit(solution)/shard_map/ppermute | solution.py:582
  9.5 4.5 %collective-permute-start.1 = (bf16[16,7040]{1,0:T(8,128)(2,1)S(1)}, bf16[16,7040]{1,0:T(8,128)(2,1)S(1)}, u32[]{:S(2)}, u32[]{:S(2)}) collective-permute-start(bf16[16,7040]{1,0:T(8,128)(2,1)S(1)} %get-tuple-element.42), channel_id=1, source_target_pairs={{16,32},{32,16},{48,64},{64,48},{80,96},{96,80},{112,128},{128,112... | collective-permute-start | bytes 675848 | tf_op jit(solution)/shard_map/ppermute | solution.py:582
  14.0 0.3 shard_map.105
  14.3 0.8 %shard_map.104 = (bf16[2048,128]{1,0:T(8,128)(2,1)S(1)}, f32[32,64]{1,0:T(8,128)S(1)}) custom-call(bf16[32,4096]{1,0:T(8,128)(2,1)S(1)} %get-tuple-element.31.blocks, bf16[32,4096]{1,0:T(8,128)(2,1)S(1)} %get-tuple-element.32.faces), custom_call_target="tpu_custom_call" | custom-call | flops 1000000000 | bytes 1048576 | tf_op jit(solution)/shard_map/pallas_call | solution.py:564
  15.1 5.6 %collective-permute-done.x_even = bf16[16,7040]{1,0:T(8,128)(2,1)S(1)} collective-permute-done((bf16[16,7040]{1,0:T(8,128)(2,1)S(1)}, bf16[16,7040]{1,0:T(8,128)(2,1)S(1)}, u32[]{:S(2)}, u32[]{:S(2)}) %collective-permute-start) | collective-permute-done | bytes 225312 | tf_op jit(solution)/shard_map/ppermute | solution.py:582
  20.7 0.0 collective-permute-done.1.x_odd
  20.7 0.5 %shard_map.107 = (bf16[16,8064]{1,0:T(8,128)(2,1)S(1)}, bf16[16,8064]{1,0:T(8,128)(2,1)S(1)}, bf16[16,7040]{1,0:T(8,128)(2,1)S(1)}, bf16[16,7040]{1,0:T(8,128)(2,1)S(1)}) custom-call(bf16[32,4096]{1,0:T(8,128)(2,1)S(1)} %get-tuple-element.31.blocks, bf16[32,4096]{1,0:T(8,128)(2,1)S(1)} %get-tuple-element.32.faces, ...), custom_call_target="tpu_custom_call" | custom-call | flops 100000000 | bytes 1048576 | tf_op jit(solution)/shard_map/pallas_call | solution.py:564
  21.2 1.9 %collective-permute-start.2 = (bf16[16,8064]{1,0:T(8,128)(2,1)S(1)}, bf16[16,8064]{1,0:T(8,128)(2,1)S(1)}, u32[]{:S(2)}, u32[]{:S(2)}) collective-permute-start(bf16[16,8064]{1,0:T(8,128)(2,1)S(1)} %get-tuple-element.49), channel_id=1, source_target_pairs={{0,1},{1,0},{2,3},{3,2},{4,5},{5,4},{6,7},{7,6},{8,9},{9,8},{10,11... | collective-permute-start | bytes 774152 | tf_op jit(solution)/shard_map/ppermute | solution.py:582
  23.1 5.9 %collective-permute-start.3 = (bf16[16,8064]{1,0:T(8,128)(2,1)S(1)}, bf16[16,8064]{1,0:T(8,128)(2,1)S(1)}, u32[]{:S(2)}, u32[]{:S(2)}) collective-permute-start(bf16[16,8064]{1,0:T(8,128)(2,1)S(1)} %get-tuple-element.50), channel_id=1, source_target_pairs={{1,2},{2,1},{3,4},{4,3},{5,6},{6,5},{7,8},{8,7},{9,10},{10,9},{11,... | collective-permute-start | bytes 774152 | tf_op jit(solution)/shard_map/ppermute | solution.py:582
  29.0 0.0 copy-start.7
  29.0 0.6 %copy-done.7 = s32[1,1,32]{2,1,0:T(1,128)S(1)} copy-done((s32[1,1,32]{2,1,0:T(1,128)S(1)}, s32[1,1,32]{2,1,0:T(1,128)}, u32[]{:S(2)}) %copy-start.7) | copy-done | bytes 152
  29.6 4.4 %shard_map.106 = (f32[256,256]{1,0:T(8,128)}, bf16[4,256,512]{2,1,0:T(8,128)(2,1)S(1)}) custom-call(s32[32]{0:T(128)S(1)} %bitcast.25, bf16[2048,128]{1,0:T(8,128)(2,1)S(1)} %get-tuple-element.35.t16, bf16[512,128]{1,0:T(8,128)(2,1)S(1)} %get-tuple-element.36.plus_y, bf16[512,128]{1,0:T(8,128)(2,1)S(1)} %get-tuple-element.37.minus_y, ...), custom_call_target="tpu_custom_call" | custom-call | flops 4000000000 | bytes 4194304 | tf_op jit(solution)/shard_map/pallas_call | solution.py:564
  34.1 0.0 copy-start.6
  34.1 0.7 %copy-done.6 = s32[1,1,24]{2,1,0:T(1,128)S(1)} copy-done((s32[1,1,24]{2,1,0:T(1,128)S(1)}, s32[1,1,24]{2,1,0:T(1,128)}, u32[]{:S(2)}) %copy-start.6) | copy-done | bytes 120
  34.7 2.3 %shard_map.108 = (bf16[2048,128]{1,0:T(8,128)(2,1)S(1)}, f32[32,64]{1,0:T(8,128)S(1)}, f32[4,256,256]{2,1,0:T(8,128)}) custom-call(s32[24]{0:T(128)S(1)} %bitcast.23, bf16[2048,128]{1,0:T(8,128)(2,1)S(1)} %get-tuple-element.33.w, bf16[4,256,512]{2,1,0:T(8,128)(2,1)S(1)} %get-tuple-element.38.edge_columns, bf16[16,7040]{1,0:T(8,128)(2,1)S(1)} %get-tuple-element.43.x_low, ...), custom_call_target="tpu_custom_call" | custom-call | flops 1000000000 | bytes 1048576 | tf_op jit(solution)/shard_map/pallas_call | solution.py:564
  37.0 0.0 collective-permute-done.2.y_even
  37.0 0.0 collective-permute-done.3.y_odd
  37.0 5.9 %shard_map.109 = (f32[6,32,64]{2,1,0:T(8,128)}, f32[4,256,256]{2,1,0:T(8,128)}) custom-call(s32[24]{0:T(128)S(1)} %bitcast.24, f32[6,32,64]{2,1,0:T(8,128)S(1)} %get-tuple-element.29.guess, f32[6,32,64]{2,1,0:T(8,128)S(1)} %get-tuple-element.30.rhs, bf16[2048,128]{1,0:T(8,128)(2,1)S(1)} %get-tuple-element.33.w, ...), custom_call_target="tpu_custom_call", output_to_operand_aliasing={{1}: (13, {})} | custom-call | flops 1000000000 | bytes 1048576 | tf_op jit(solution)/shard_map/pallas_call | solution.py:564
Async XLA Ops:
  0.6 0.7 %copy-start.5 = (f32[2]{0:T(128)S(1)}, f32[2]{0:T(128)}, u32[]{:S(2)}) copy-start(f32[2]{0:T(128)} %param.15) | copy-start | bytes 28
  1.3 0.9 %copy-start = (bf16[1,1,32,4096]{3,2,1,0:T(8,128)(2,1)S(1)}, bf16[1,1,32,4096]{3,2,1,0:T(8,128)(2,1)}, u32[]{:S(2)}) copy-start(bf16[1,1,32,4096]{3,2,1,0:T(8,128)(2,1)} %param.8) | copy-start | bytes 786436
  2.2 0.9 %copy-start.1 = (bf16[1,1,32,4096]{3,2,1,0:T(8,128)(2,1)S(1)}, bf16[1,1,32,4096]{3,2,1,0:T(8,128)(2,1)}, u32[]{:S(2)}) copy-start(bf16[1,1,32,4096]{3,2,1,0:T(8,128)(2,1)} %param.9) | copy-start | bytes 786436
  3.2 0.9 %copy-start.2 = (bf16[1,1,32,4096]{3,2,1,0:T(8,128)(2,1)S(1)}, bf16[1,1,32,4096]{3,2,1,0:T(8,128)(2,1)}, u32[]{:S(2)}) copy-start(bf16[1,1,32,4096]{3,2,1,0:T(8,128)(2,1)} %param.10) | copy-start | bytes 786436
  4.1 0.9 %copy-start.3 = (f32[1,1,6,64,32]{3,4,2,1,0:T(8,128)S(1)}, f32[1,1,6,64,32]{3,4,2,1,0:T(8,128)}, u32[]{:S(2)}) copy-start(f32[1,1,6,64,32]{3,4,2,1,0:T(8,128)} %param.14) | copy-start | bytes 147460
  5.0 0.9 %copy-start.4 = (f32[1,1,6,64,32]{3,4,2,1,0:T(8,128)S(1)}, f32[1,1,6,64,32]{3,4,2,1,0:T(8,128)}, u32[]{:S(2)}) copy-start(f32[1,1,6,64,32]{3,4,2,1,0:T(8,128)} %param.13) | copy-start | bytes 147460
  6.7 14.0 %collective-permute-start = (bf16[16,7040]{1,0:T(8,128)(2,1)S(1)}, bf16[16,7040]{1,0:T(8,128)(2,1)S(1)}, u32[]{:S(2)}, u32[]{:S(2)}) collective-permute-start(bf16[16,7040]{1,0:T(8,128)(2,1)S(1)} %get-tuple-element.41), channel_id=1, source_target_pairs={{0,16},{16,0},{32,48},{48,32},{64,80},{80,64},{96,112},{112,96},{1... | collective-permute-start | bytes 675848 | tf_op jit(solution)/shard_map/ppermute | solution.py:582
  9.5 11.2 %collective-permute-start.1 = (bf16[16,7040]{1,0:T(8,128)(2,1)S(1)}, bf16[16,7040]{1,0:T(8,128)(2,1)S(1)}, u32[]{:S(2)}, u32[]{:S(2)}) collective-permute-start(bf16[16,7040]{1,0:T(8,128)(2,1)S(1)} %get-tuple-element.42), channel_id=1, source_target_pairs={{16,32},{32,16},{48,64},{64,48},{80,96},{96,80},{112,128},{128,112... | collective-permute-start | bytes 675848 | tf_op jit(solution)/shard_map/ppermute | solution.py:582
  21.2 15.8 %collective-permute-start.2 = (bf16[16,8064]{1,0:T(8,128)(2,1)S(1)}, bf16[16,8064]{1,0:T(8,128)(2,1)S(1)}, u32[]{:S(2)}, u32[]{:S(2)}) collective-permute-start(bf16[16,8064]{1,0:T(8,128)(2,1)S(1)} %get-tuple-element.49), channel_id=1, source_target_pairs={{0,1},{1,0},{2,3},{3,2},{4,5},{5,4},{6,7},{7,6},{8,9},{9,8},{10,11... | collective-permute-start | bytes 774152 | tf_op jit(solution)/shard_map/ppermute | solution.py:582
  23.1 13.9 %collective-permute-start.3 = (bf16[16,8064]{1,0:T(8,128)(2,1)S(1)}, bf16[16,8064]{1,0:T(8,128)(2,1)S(1)}, u32[]{:S(2)}, u32[]{:S(2)}) collective-permute-start(bf16[16,8064]{1,0:T(8,128)(2,1)S(1)} %get-tuple-element.50), channel_id=1, source_target_pairs={{1,2},{2,1},{3,4},{4,3},{5,6},{6,5},{7,8},{8,7},{9,10},{10,9},{11,... | collective-permute-start | bytes 774152 | tf_op jit(solution)/shard_map/ppermute | solution.py:582
  29.0 0.7 %copy-start.7 = (s32[1,1,32]{2,1,0:T(1,128)S(1)}, s32[1,1,32]{2,1,0:T(1,128)}, u32[]{:S(2)}) copy-start(s32[1,1,32]{2,1,0:T(1,128)} %param.11) | copy-start | bytes 388
  34.1 0.7 %copy-start.6 = (s32[1,1,24]{2,1,0:T(1,128)S(1)}, s32[1,1,24]{2,1,0:T(1,128)}, u32[]{:S(2)}) copy-start(s32[1,1,24]{2,1,0:T(1,128)} %param.12) | copy-start | bytes 292

commit v4 on v3

--- a/solution.py
+++ b/solution.py
@@ -86,13 +86,13 @@
     return onehot((row == source) & (lane < 192))
 
 
-def pack_x_kernel(blocks_in, faces_in, tent_in, guess_in, rhs_in, bounds_in, even, odd, guess_packed, rhs_packed,
-                  blocks, faces, tent, guess, rhs, bounds, sems):
+def pack_x_kernel(blocks_in, faces_in, tent_in, guess_in, rhs_in, even, odd, guess_packed, rhs_packed,
+                  blocks, faces, tent, guess, rhs, sems):
     copies = [
         pltpu.make_async_copy(source, target, sems.at[i])
-        for i, (source, target) in enumerate((
-            (guess_in, guess), (rhs_in, rhs), (blocks_in, blocks), (faces_in, faces), (tent_in, tent), (bounds_in, bounds),
-        ))
+        for i, (source, target) in enumerate(
+            ((guess_in, guess), (rhs_in, rhs), (blocks_in, blocks), (faces_in, faces), (tent_in, tent))
+        )
     ]
     for copy in copies:
         copy.start()
@@ -133,7 +133,7 @@
     put(XT, 512, lambda s: halves(of(tent, 0, s, 3072 * s, 1024)))
 
 
-def pack_y_kernel(blocks, faces, tent, guess_packed, rhs_packed, x_even, x_odd, even, odd, low, high):
+def pack_y_kernel(blocks, faces, tent, guess_packed, rhs_packed, x_even, x_odd, _, even, odd, low, high):
     first = parity("bx") == 0
     for start in range(0, XLEN, 128):
         a = x_even[:, start : start + 128].astype(F32)
@@ -254,7 +254,8 @@
     w[...] = w32[...].astype(BF16)
 
 
-def own_kernel(blocks, faces, w, inverse, *scratch):
+def own_kernel(blocks, faces, bounds, w, inverse, coefficients, *scratch):
+    coefficients[...] = jnp.concatenate([jnp.broadcast_to(c, (1, 128)) for c in factors(bounds)] + [jnp.zeros((3, 128), F32)], 0)
     chunk = lambda ref: lambda c: ref[:, c * 128 : (c + 1) * 128].astype(F32)
     operators(chunk(blocks), chunk(faces), w, inverse, *scratch)
 
@@ -339,7 +340,7 @@
 )
 
 
-def smooth(guess, rhs, w, wx, wy, inv, inv_x, inv_y, bounds, x_low, x_high, y_low, y_high, smoothed,
+def smooth(guess, rhs, w, wx, wy, inv, inv_x, inv_y, coefficients, x_low, x_high, y_low, y_high, smoothed,
            g_ref, r_ref, i_ref, t_ref, x_ref, a_ref):
     def joined(value):
         return value + pltpu.roll(value, 64, 1)
@@ -416,7 +417,7 @@
             a_ref[pl.ds(row, 8, stride=EXT), 0:64] = out[:8] + out[8:]
         return a_ref[:SPAN, 0:64]
 
-    centre, half_width, first, second, third = factors(bounds)
+    centre, half_width, first, second, third = [coefficients[i : i + 1, 0:64] for i in range(5)]
     inverse = jnp.concatenate([i_ref[:, 0:64]] * NRHS, 0)
     v = g_ref[:, 0:64]
     r = r_ref[:, 0:64] - apply(0, v)
@@ -541,7 +542,7 @@
         copy.wait()
 
 
-def finish_kernel(side_labels, guess, rhs, w, wx, inv, inv_x, bounds, x_low, x_high, y_even, y_odd, edge_columns, ghost_in,
+def finish_kernel(side_labels, guess, rhs, w, wx, inv, inv_x, coefficients, x_low, x_high, y_even, y_odd, edge_columns, ghost_in,
                   smoothed, ghost, wy, inv_y, y_low, y_high, stage, fstage, w32, g_ref, r_ref, i_ref, t_ref, x_ref, a_ref,
                   rows, masks, side, result, sems):
     halo_y(y_even, y_odd, wy, inv_y, y_low, y_high, stage, fstage, w32)
@@ -554,13 +555,13 @@
                     result.at[f])
         copies.append(pltpu.make_async_copy(result.at[f], ghost.at[2 + f], sems.at[f]))
         copies[-1].start()
-    smooth(guess, rhs, w, wx, wy, inv, inv_x, inv_y, bounds, x_low, x_high, y_low, y_high, smoothed,
+    smooth(guess, rhs, w, wx, wy, inv, inv_x, inv_y, coefficients, x_low, x_high, y_low, y_high, smoothed,
            g_ref, r_ref, i_ref, t_ref, x_ref, a_ref)
     for copy in copies:
         copy.wait()
 
 
-def call(kernel, outs, scratch, operands, flops, moved, in_specs=None, out_specs=None, aliases=None):
+def call(kernel, outs, scratch, operands, flops, moved, in_specs=None, out_specs=None, aliases=None, room=48):
     return pl.pallas_call(
         kernel,
         out_shape=outs,
@@ -569,7 +570,7 @@
         scratch_shapes=scratch,
         input_output_aliases=aliases or {},
         cost_estimate=pl.CostEstimate(flops=flops, bytes_accessed=moved, transcendentals=0),
-        compiler_params=pltpu.CompilerParams(vmem_limit_bytes=48 * 1024 * 1024),
+        compiler_params=pltpu.CompilerParams(vmem_limit_bytes=room * 1024 * 1024),
     )(*operands)
 
 
@@ -604,16 +605,17 @@
     rhs = jnp.swapaxes(rhs[0, 0], 1, 2)
     guess = jnp.swapaxes(guess[0, 0], 1, 2)
     labels, side_labels = aggregate.reshape(NE), ghost_labels.reshape(24)
-    even, odd, guess_packed, rhs_packed, blocks, faces, tentative, guess, rhs, bounds = call(
-        pack_x_kernel,
-        [shaped(16, XLEN)] * 2 + [shaped(NE, 768)] * 2 + [shaped(NE, 4096)] * 3
-        + [wide(NRHS, NE, 64)] * 2 + [wide(1, 2)],
-        [pltpu.SemaphoreType.DMA((6,))],
-        [a.reshape(NE, 4096) for a in (blocks, faces, tentative)] + [guess, rhs, bounds.reshape(1, 2)],
-        10**6, 2**20, [HBM] * 6,
+    blocks, faces, tentative = [a.reshape(NE, 4096) for a in (blocks, faces, tentative)]
+    even, odd, guess_packed, rhs_packed = call(
+        pack_x_kernel, [shaped(16, XLEN)] * 2 + [shaped(NE, 768)] * 2,
+        [pltpu.VMEM((NE, 4096), BF16)] * 3 + [pltpu.VMEM((NRHS, NE, 64), F32)] * 2 + [pltpu.SemaphoreType.DMA((5,))],
+        (blocks, faces, tentative, guess, rhs), 10**6, 2**20, [HBM] * 5, room=62,
     )
     even, odd = exchange((even, odd), "bx")
-    w, inverse = call(own_kernel, [shaped(2048, 128), wide(NE, 64)], STAGES, (blocks, faces), 10**9, 2**20)
+    w, inverse, coefficients = call(
+        own_kernel, [shaped(2048, 128), wide(NE, 64), wide(8, 128)], STAGES,
+        (blocks, faces, bounds.reshape(1, 2)), 10**9, 2**20,
+    )
     t16, plus_y, minus_y = call(
         prolong_kernel, [shaped(2048, 128), shaped(512, 128), shaped(512, 128)],
         [STAGES[0], STAGES[2]], (tentative,), 5 * 10**8, 2**20,
@@ -627,7 +629,8 @@
     )
     even, odd, x_low, x_high = call(
         pack_y_kernel, [shaped(16, YLEN)] * 2 + [shaped(16, XLEN)] * 2, [],
-        (blocks, faces, tentative, guess_packed, rhs_packed, even, odd), 10**8, 2**20,
+        (blocks, faces, tentative, guess_packed, rhs_packed, even, odd, edge_columns), 10**8, 2**20,
+        [VMEM] * 7 + [pl.BlockSpec(memory_space=pl.ANY)],
     )
     even, odd = exchange((even, odd), "by")
     wx, inverse_x, ghost = call(
@@ -643,7 +646,7 @@
         + [pltpu.VMEM((EXT, 128), F32), pltpu.VMEM((SPAN, 128), F32)]
         + [pltpu.VMEM((8 * EXT, 128), F32)] * 2
         + GHOST,
-        (side_labels, guess, rhs, w, wx, inverse, inverse_x, bounds, x_low, x_high, even, odd, edge_columns, ghost),
+        (side_labels, guess, rhs, w, wx, inverse, inverse_x, coefficients, x_low, x_high, even, odd, edge_columns, ghost),
         10**9, 2**20, [SMEM] + [VMEM] * 12 + [HBM], [VMEM, HBM], {13: 1},
     )
     return jnp.swapaxes(smoothed, 1, 2)[None, None], local[None, None], ghost[None, None]

time: 43.3 us -> 39.2 us (0.905)
  the two profiles are of different devices: /device:TPU:6 before, /device:TPU:123 now
where the time goes in v4:
time: 39.2 us; the launch traced here: 38.9 us
  Pallas kernels  16.7 us (43%)
  starting transfers between devices  14.4 us (37%)
  waiting for transfers between devices  4.98 us (13%)
  local copies, waits for them, and re-layouts  1.96 us (5%)
  between operations  0.79 us (2%)
    pallas_call x7, Pallas kernels, call(): pl.pallas_call(kernel, out_shape=outs, in_specs=in_specs or [VMEM] * len(...  16.7 us
    ppermute x4, starting transfers between devices, exchange(): out.append(lax.ppermute(message, axis, pairs))  14.4 us
    ppermute x4, waiting for transfers between devices, exchange(): out.append(lax.ppermute(message, axis, pairs))  4.98 us
    unnamed x20, local copies, waits for them, and re-layouts  1.96 us
  transfers between devices with their start and end apart: 4, of which 1 were waited for; matrix products, arithmetic and copies ran while one was open for 0% of the time, Pallas kernels for 20%

profile of v4, /device:TPU:123, one launch (start us, length us, event | category | flops | bytes accessed | tf_op | source)
XLA Modules:
  0.0 38.9 jit_solution(6367719020475547541)
XLA Ops:
  0.6 0.0 copy-start.2
  0.6 2.5 %shard_map.106 = (bf16[16,7040]{1,0:T(8,128)(2,1)}, bf16[16,7040]{1,0:T(8,128)(2,1)}, bf16[32,768]{1,0:T(8,128)(2,1)}, bf16[32,768]{1,0:T(8,128)(2,1)}) custom-call(bf16[32,4096]{1,0:T(8,128)(2,1)} %bitcast.17, bf16[32,4096]{1,0:T(8,128)(2,1)} %bitcast.20, bf16[32,4096]{1,0:T(8,128)(2,1)} %bitcast.23, f32[6,32,64]{2,1,0:T(8,128)} %bitcast.26, ...), custom_call_target="tpu_custom_call" | custom-call | flops 1000000 | bytes 1048576 | tf_op jit(solution)/shard_map/pallas_call | solution.py:565
  3.1 2.2 %collective-permute-start = (bf16[16,7040]{1,0:T(8,128)(2,1)}, bf16[16,7040]{1,0:T(8,128)(2,1)S(1)}, u32[]{:S(2)}, u32[]{:S(2)}) collective-permute-start(bf16[16,7040]{1,0:T(8,128)(2,1)} %get-tuple-element.31), channel_id=1, source_target_pairs={{0,16},{16,0},{32,48},{48,32},{64,80},{80,64},{96,112},{112,96},{1... | collective-permute-start | bytes 675848 | tf_op jit(solution)/shard_map/ppermute | solution.py:583
  5.3 0.0 copy-start
  5.3 0.0 copy-start.1
  5.3 5.8 %collective-permute-start.1 = (bf16[16,7040]{1,0:T(8,128)(2,1)}, bf16[16,7040]{1,0:T(8,128)(2,1)S(1)}, u32[]{:S(2)}, u32[]{:S(2)}) collective-permute-start(bf16[16,7040]{1,0:T(8,128)(2,1)} %get-tuple-element.32), channel_id=1, source_target_pairs={{16,32},{32,16},{48,64},{64,48},{80,96},{96,80},{112,128},{128,112... | collective-permute-start | bytes 675848 | tf_op jit(solution)/shard_map/ppermute | solution.py:583
  11.1 0.0 copy-done.2
  11.1 0.3 shard_map.104
  11.5 0.0 copy-start.8
  11.5 0.0 copy-done
  11.5 0.0 copy-done.1
  11.5 0.6 %copy-done.8 = f32[2]{0:T(128)S(1)} copy-done((f32[2]{0:T(128)S(1)}, f32[2]{0:T(128)}, u32[]{:S(2)}) %copy-start.8) | copy-done | bytes 32
  12.1 0.9 %shard_map.103 = (bf16[2048,128]{1,0:T(8,128)(2,1)S(1)}, f32[32,64]{1,0:T(8,128)S(1)}, f32[8,128]{1,0:T(8,128)S(1)}) custom-call(bf16[32,4096]{1,0:T(8,128)(2,1)S(1)} %bitcast.18, bf16[32,4096]{1,0:T(8,128)(2,1)S(1)} %bitcast.21, f32[1,2]{1,0:T(1,128)S(1)} %bitcast.32), custom_call_target="tpu_custom_call" | custom-call | flops 1000000000 | bytes 1048576 | tf_op jit(solution)/shard_map/pallas_call | solution.py:565
  13.0 0.0 copy-start.9
  13.0 0.6 %copy-done.9 = s32[1,1,32]{2,1,0:T(1,128)S(1)} copy-done((s32[1,1,32]{2,1,0:T(1,128)S(1)}, s32[1,1,32]{2,1,0:T(1,128)}, u32[]{:S(2)}) %copy-start.9) | copy-done | bytes 152
  13.7 0.0 copy-start.5
  13.7 0.0 copy-start.6
  13.7 4.4 %shard_map.105 = (f32[256,256]{1,0:T(8,128)}, bf16[4,256,512]{2,1,0:T(8,128)(2,1)S(1)}) custom-call(s32[32]{0:T(128)S(1)} %bitcast.33, bf16[2048,128]{1,0:T(8,128)(2,1)S(1)} %get-tuple-element.25.t16, bf16[512,128]{1,0:T(8,128)(2,1)S(1)} %get-tuple-element.26.plus_y, bf16[512,128]{1,0:T(8,128)(2,1)S(1)} %get-tuple-element.27.minus_y, ...), custom_call_target="tpu_custom_call" | custom-call | flops 4000000000 | bytes 4194304 | tf_op jit(solution)/shard_map/pallas_call | solution.py:565
  18.1 0.0 collective-permute-done.x_even
  18.1 0.0 collective-permute-done.1.x_odd
  18.1 0.0 copy-done.5
  18.1 0.0 copy-done.6
  18.1 0.5 %shard_map.107 = (bf16[16,8064]{1,0:T(8,128)(2,1)S(1)}, bf16[16,8064]{1,0:T(8,128)(2,1)S(1)}, bf16[16,7040]{1,0:T(8,128)(2,1)S(1)}, bf16[16,7040]{1,0:T(8,128)(2,1)S(1)}) custom-call(bf16[32,4096]{1,0:T(8,128)(2,1)S(1)} %bitcast.19, bf16[32,4096]{1,0:T(8,128)(2,1)S(1)} %bitcast.22, bf16[32,4096]{1,0:T(8,128)(2,1)S(1)} %bitcast.25, ...), custom_call_target="tpu_custom_call" | custom-call | flops 100000000 | bytes 1048576 | tf_op jit(solution)/shard_map/pallas_call | solution.py:565
  18.6 3.2 %collective-permute-start.2 = (bf16[16,8064]{1,0:T(8,128)(2,1)S(1)}, bf16[16,8064]{1,0:T(8,128)(2,1)S(1)}, u32[]{:S(2)}, u32[]{:S(2)}) collective-permute-start(bf16[16,8064]{1,0:T(8,128)(2,1)S(1)} %get-tuple-element.39), channel_id=1, source_target_pairs={{0,1},{1,0},{2,3},{3,2},{4,5},{5,4},{6,7},{7,6},{8,9},{9,8},{10,11... | collective-permute-start | bytes 774152 | tf_op jit(solution)/shard_map/ppermute | solution.py:583
  21.7 3.3 %collective-permute-start.3 = (bf16[16,8064]{1,0:T(8,128)(2,1)S(1)}, bf16[16,8064]{1,0:T(8,128)(2,1)S(1)}, u32[]{:S(2)}, u32[]{:S(2)}) collective-permute-start(bf16[16,8064]{1,0:T(8,128)(2,1)S(1)} %get-tuple-element.40), channel_id=1, source_target_pairs={{1,2},{2,1},{3,4},{4,3},{5,6},{6,5},{7,8},{8,7},{9,10},{10,9},{11,... | collective-permute-start | bytes 774152 | tf_op jit(solution)/shard_map/ppermute | solution.py:583
  25.0 0.0 copy-start.7
  25.0 0.6 %copy-done.7 = s32[1,1,24]{2,1,0:T(1,128)S(1)} copy-done((s32[1,1,24]{2,1,0:T(1,128)S(1)}, s32[1,1,24]{2,1,0:T(1,128)}, u32[]{:S(2)}) %copy-start.7) | copy-done | bytes 120
  25.7 0.0 copy-start.3
  25.7 0.0 copy-start.4
  25.7 2.3 %shard_map.108 = (bf16[2048,128]{1,0:T(8,128)(2,1)S(1)}, f32[32,64]{1,0:T(8,128)S(1)}, f32[4,256,256]{2,1,0:T(8,128)}) custom-call(s32[24]{0:T(128)S(1)} %bitcast.30, bf16[2048,128]{1,0:T(8,128)(2,1)S(1)} %get-tuple-element.24.w, bf16[4,256,512]{2,1,0:T(8,128)(2,1)S(1)} %get-tuple-element.28._.edge_columns, bf16[16,7040]{1,0:T(8,128)(2,1)S(1)} %get-tuple-element.33.x_low, ...), custom_call_target="tpu_custom_call" | custom-call | flops 1000000000 | bytes 1048576 | tf_op jit(solution)/shard_map/pallas_call | solution.py:565
  28.0 0.0 collective-permute-done.2.y_even
  28.0 5.0 %collective-permute-done.3.y_odd = bf16[16,8064]{1,0:T(8,128)(2,1)S(1)} collective-permute-done((bf16[16,8064]{1,0:T(8,128)(2,1)S(1)}, bf16[16,8064]{1,0:T(8,128)(2,1)S(1)}, u32[]{:S(2)}, u32[]{:S(2)}) %collective-permute-start.3) | collective-permute-done | bytes 258080 | tf_op jit(solution)/shard_map/ppermute | solution.py:583
  33.0 0.0 copy-done.3
  33.0 0.0 copy-done.4
  33.0 5.9 %shard_map.109 = (f32[6,32,64]{2,1,0:T(8,128)}, f32[4,256,256]{2,1,0:T(8,128)}) custom-call(s32[24]{0:T(128)S(1)} %bitcast.31, f32[6,32,64]{2,1,0:T(8,128)S(1)} %bitcast.27, f32[6,32,64]{2,1,0:T(8,128)S(1)} %bitcast.29, bf16[2048,128]{1,0:T(8,128)(2,1)S(1)} %get-tuple-element.24.w, ...), custom_call_target="tpu_custom_call", output_to_operand_aliasing={{1}: (13, {})} | custom-call | flops 1000000000 | bytes 1048576 | tf_op jit(solution)/shard_map/pallas_call | solution.py:565
Async XLA Ops:
  0.6 10.5 %copy-start.2 = (bf16[1,1,32,4096]{3,2,1,0:T(8,128)(2,1)S(1)}, bf16[1,1,32,4096]{3,2,1,0:T(8,128)(2,1)}, u32[]{:S(2)}) copy-start(bf16[1,1,32,4096]{3,2,1,0:T(8,128)(2,1)} %param.10) | copy-start | bytes 786436
  3.1 15.0 %collective-permute-start = (bf16[16,7040]{1,0:T(8,128)(2,1)}, bf16[16,7040]{1,0:T(8,128)(2,1)S(1)}, u32[]{:S(2)}, u32[]{:S(2)}) collective-permute-start(bf16[16,7040]{1,0:T(8,128)(2,1)} %get-tuple-element.31), channel_id=1, source_target_pairs={{0,16},{16,0},{32,48},{48,32},{64,80},{80,64},{96,112},{112,96},{1... | collective-permute-start | bytes 675848 | tf_op jit(solution)/shard_map/ppermute | solution.py:583
  5.3 6.2 %copy-start = (bf16[1,1,32,4096]{3,2,1,0:T(8,128)(2,1)S(1)}, bf16[1,1,32,4096]{3,2,1,0:T(8,128)(2,1)}, u32[]{:S(2)}) copy-start(bf16[1,1,32,4096]{3,2,1,0:T(8,128)(2,1)} %param.8) | copy-start | bytes 786436
  5.3 6.2 %copy-start.1 = (bf16[1,1,32,4096]{3,2,1,0:T(8,128)(2,1)S(1)}, bf16[1,1,32,4096]{3,2,1,0:T(8,128)(2,1)}, u32[]{:S(2)}) copy-start(bf16[1,1,32,4096]{3,2,1,0:T(8,128)(2,1)} %param.9) | copy-start | bytes 786436
  5.3 12.8 %collective-permute-start.1 = (bf16[16,7040]{1,0:T(8,128)(2,1)}, bf16[16,7040]{1,0:T(8,128)(2,1)S(1)}, u32[]{:S(2)}, u32[]{:S(2)}) collective-permute-start(bf16[16,7040]{1,0:T(8,128)(2,1)} %get-tuple-element.32), channel_id=1, source_target_pairs={{16,32},{32,16},{48,64},{64,48},{80,96},{96,80},{112,128},{128,112... | collective-permute-start | bytes 675848 | tf_op jit(solution)/shard_map/ppermute | solution.py:583
  11.5 0.7 %copy-start.8 = (f32[2]{0:T(128)S(1)}, f32[2]{0:T(128)}, u32[]{:S(2)}) copy-start(f32[2]{0:T(128)} %param.15) | copy-start | bytes 28
  13.0 0.7 %copy-start.9 = (s32[1,1,32]{2,1,0:T(1,128)S(1)}, s32[1,1,32]{2,1,0:T(1,128)}, u32[]{:S(2)}) copy-start(s32[1,1,32]{2,1,0:T(1,128)} %param.11) | copy-start | bytes 388
  13.7 4.4 %copy-start.5 = (bf16[32,768]{1,0:T(8,128)(2,1)S(1)}, bf16[32,768]{1,0:T(8,128)(2,1)}, u32[]{:S(2)}) copy-start(bf16[32,768]{1,0:T(8,128)(2,1)} %get-tuple-element.29.guess_packed) | copy-start | bytes 147460
  13.7 4.4 %copy-start.6 = (bf16[32,768]{1,0:T(8,128)(2,1)S(1)}, bf16[32,768]{1,0:T(8,128)(2,1)}, u32[]{:S(2)}) copy-start(bf16[32,768]{1,0:T(8,128)(2,1)} %get-tuple-element.30.rhs_packed) | copy-start | bytes 147460
  18.6 9.4 %collective-permute-start.2 = (bf16[16,8064]{1,0:T(8,128)(2,1)S(1)}, bf16[16,8064]{1,0:T(8,128)(2,1)S(1)}, u32[]{:S(2)}, u32[]{:S(2)}) collective-permute-start(bf16[16,8064]{1,0:T(8,128)(2,1)S(1)} %get-tuple-element.39), channel_id=1, source_target_pairs={{0,1},{1,0},{2,3},{3,2},{4,5},{5,4},{6,7},{7,6},{8,9},{9,8},{10,11... | collective-permute-start | bytes 774152 | tf_op jit(solution)/shard_map/ppermute | solution.py:583
  21.7 11.3 %collective-permute-start.3 = (bf16[16,8064]{1,0:T(8,128)(2,1)S(1)}, bf16[16,8064]{1,0:T(8,128)(2,1)S(1)}, u32[]{:S(2)}, u32[]{:S(2)}) collective-permute-start(bf16[16,8064]{1,0:T(8,128)(2,1)S(1)} %get-tuple-element.40), channel_id=1, source_target_pairs={{1,2},{2,1},{3,4},{4,3},{5,6},{6,5},{7,8},{8,7},{9,10},{10,9},{11,... | collective-permute-start | bytes 774152 | tf_op jit(solution)/shard_map/ppermute | solution.py:583
  25.0 0.7 %copy-start.7 = (s32[1,1,24]{2,1,0:T(1,128)S(1)}, s32[1,1,24]{2,1,0:T(1,128)}, u32[]{:S(2)}) copy-start(s32[1,1,24]{2,1,0:T(1,128)} %param.12) | copy-start | bytes 292
  25.7 7.3 %copy-start.3 = (f32[1,1,6,64,32]{3,4,2,1,0:T(8,128)S(1)}, f32[1,1,6,64,32]{3,4,2,1,0:T(8,128)}, u32[]{:S(2)}) copy-start(f32[1,1,6,64,32]{3,4,2,1,0:T(8,128)} %param.14) | copy-start | bytes 147460
  25.7 7.3 %copy-start.4 = (f32[1,1,6,64,32]{3,4,2,1,0:T(8,128)S(1)}, f32[1,1,6,64,32]{3,4,2,1,0:T(8,128)}, u32[]{:S(2)}) copy-start(f32[1,1,6,64,32]{3,4,2,1,0:T(8,128)} %param.13) | copy-start | bytes 147460

commit v5 on v4

v5 whole, which is shorter than its diff:
```python
import jax
import jax.numpy as jnp
from jax import lax
from jax.experimental import pallas as pl
from jax.experimental.pallas import tpu as pltpu
from jax.sharding import PartitionSpec as P

EX, EY, NE, NRHS = 4, 8, 32, 6
F32, BF16 = jnp.float32, jnp.bfloat16
VMEM = pl.BlockSpec(memory_space=pltpu.VMEM)
SMEM = pl.BlockSpec(memory_space=pltpu.SMEM)
HBM = pl.BlockSpec(memory_space=pltpu.HBM)
ANY = pl.BlockSpec(memory_space=pl.ANY)
NT = (((1,), (1,)), ((), ()))
NN = (((1,), (0,)), ((), ()))

XA = 0
XB = 512
XC = 2560
XD = 3072
XH = 3840
XK = 4224
XT = 4480
XE = 4992
XLEN = 5120
YA, YB = 0, 512
YF = 2560
YD = 3584
YG = 4352
YR = 5120
YT = 5504
YE = 6016
YLEN = 6144

EXT, SPAN = 160, 960


def dot(a, b, dims=NN):
    return lax.dot_general(a, b, dims, preferred_element_type=F32)


def iota(shape, dim):
    return lax.broadcasted_iota(jnp.int32, shape, dim)


def onehot(mask):
    return mask.astype(F32).astype(BF16)


def split(x):
    hi = x.astype(BF16)
    return hi, (x - hi.astype(F32)).astype(BF16)


def halves(x):
    lanes = x.shape[1] // 2
    return jnp.concatenate([x[:, :lanes], x[:, lanes:]], 0)


def over(a, b):
    return jnp.concatenate([a, b], 0)


def parity(axis):
    return lax.axis_index(axis) % 2


def with_traces(v):
    q, lane = iota((64, 128), 0), iota((64, 128), 1)
    t = lane % 16
    f = lane // 16 - 4
    along_y = 16 * (t // 4) + t % 4
    source = jnp.where(f == 0, 48 + t, jnp.where(f == 1, t, jnp.where(f == 2, along_y + 12, along_y)))
    pick = onehot(q == jnp.where(f < 0, lane, source))
    hi, lo = split(v)
    return dot(hi, pick) + dot(lo, pick)


def by_element(rows):
    return jnp.concatenate([rows[n * NE : (n + 1) * NE] for n in range(NRHS)], 1)


def pack_lanes(v):
    hi, lo = split(v)
    q, lane = iota((64, 128), 0), iota((64, 128), 1)
    return by_element(dot(hi, onehot(q == lane)) + dot(lo, onehot(q == lane - 64)))


def pack_traces(traces):
    hi, lo = split(traces)
    lane = iota(traces.shape, 1)
    return by_element(jnp.where(lane >= 64, hi.astype(F32), pltpu.roll(lo.astype(F32), 64, 1)))


def squeeze(value, offset):
    lane = iota((8, 128), 1) % 64
    keep = (lane >= offset) & (lane < offset + 16)
    tiles = []
    for first in (0, 4):
        total = jnp.zeros((8, 128), F32)
        for j, n in enumerate(range(first, min(first + 4, NRHS))):
            one = jnp.where(keep, value[:, n * 128 : n * 128 + 128], 0.0)
            total = total + pltpu.roll(one, (16 * j - offset) % 128, 1)
        tiles.append(total)
    return jnp.concatenate(tiles, 1)


def unsqueeze(tiles, n, offset):
    lane = iota((8, 128), 1) % 64
    tile = tiles[:, n // 4 * 128 : n // 4 * 128 + 128]
    moved = pltpu.roll(tile, (offset - 16 * (n % 4)) % 128, 1)
    return jnp.where((lane >= offset) & (lane < offset + 16), moved, 0.0)


TRACE_OFFSET, VALUE_OFFSET = (16, 0), (0, 48)


def pack_x_kernel(blocks_in, faces_in, tent_in, guess_in, rhs_in, even, odd, traces_packed, b_packed, b_out, diagonal,
                  blocks, faces, tent, guess, rhs, stage, w32, w16, x_ref, a_ref, sems):
    copies = [
        pltpu.make_async_copy(source, target, sems.at[i])
        for i, (source, target) in enumerate(
            ((guess_in, guess), (blocks_in, blocks), (rhs_in, rhs), (faces_in, faces), (tent_in, tent))
        )
    ]
    for copy in copies:
        copy.start()
    copies[0].wait()
    v = guess[...].reshape(NRHS * NE, 64)
    traces = with_traces(v)
    t = pack_traces(traces)
    traces_packed[...] = t.astype(BF16)
    x_ref[0:192, :] = traces
    x_ref[192:256, :] = jnp.zeros((64, 128), F32)
    copies[1].wait()
    diag = stage_blocks(lambda c: blocks[:, c * 128 : (c + 1) * 128].astype(F32), stage)
    diag = diag + pltpu.roll(diag, 64, 1)
    diagonal[...] = diag.astype(BF16)
    for k in range(4):
        both = stage[k]
        w32[pl.ds(2 * k, 256, stride=8), :] = both
        w32[pl.ds(2 * k + 1, 256, stride=8), :] = pltpu.roll(both, 64, 1)
    w16[...] = w32[...].astype(BF16)
    lane8 = iota((8, 128), 1)
    for e in range(NE):
        hi, lo = split(jnp.where(lane8 < 64, x_ref[pl.ds(e, 8, stride=NE), :], 0.0))
        out = dot(over(hi, lo), w16[e * 64 : e * 64 + 64, :], NT)
        a_ref[pl.ds(e, 8, stride=NE), 0:64] = out[:8] + out[8:]
    for copy in copies[2:]:
        copy.wait()
    b = rhs[...].reshape(NRHS * NE, 64) - a_ref[0:192, 0:64]
    b_out[...] = b
    r = pack_lanes(b)
    b_packed[...] = r.astype(BF16)
    first = parity("bx") == 0

    def put(start, lanes, make):
        low, high = make(0), make(1)
        even[:, start : start + lanes] = jnp.where(first, high, low).astype(BF16)
        odd[:, start : start + lanes] = jnp.where(first, low, high).astype(BF16)

    def rows(k, side):
        return 8 * k if side == 0 else 24 - 8 * k

    def of(ref, k, side, start, lanes):
        row = rows(k, side)
        base = row // 16 * 16
        return ref[base : base + 16, start : start + lanes].astype(F32)[row - base : row - base + 8]

    def packed(value, k, side):
        return value[rows(k, side) : rows(k, side) + 8]

    def face_traces(side):
        return jnp.concatenate([of(faces, 1, side, f * 1024 + 768 * side, 256) for f in range(4)], 1)

    put(XA, 512, lambda s: halves(of(blocks, 0, s, 3072 * s, 1024)))
    for h in range(2):
        put(XB + h * 1024, 1024, lambda s: over(of(faces, 0, s, h * 1024, 1024), of(faces, 0, s, h * 1024 + 2048, 1024)))
    put(XC, 512, lambda s: halves(face_traces(s)))
    put(XD, 768, lambda s: over(packed(t, 0, s), packed(t, 1, s)))
    put(XH, 384, lambda s: halves(packed(r, 0, s)))
    put(XK, 256, lambda s: over(squeeze(packed(t, 2, s), TRACE_OFFSET[s]), squeeze(packed(r, 1, s), VALUE_OFFSET[s])))
    put(XT, 512, lambda s: halves(of(tent, 0, s, 3072 * s, 1024)))
    put(XE, 128, lambda s: over(packed(diag, 0, s), packed(diag, 1, s)))


def pack_y_kernel(blocks, faces, tent, traces_packed, b_packed, diagonal, x_even, x_odd, _, even, odd, low, high):
    first = parity("bx") == 0
    for start in range(0, XLEN, 128):
        a = x_even[:, start : start + 128].astype(F32)
        b = x_odd[:, start : start + 128].astype(F32)
        low[:, start : start + 128] = jnp.where(first, b, a).astype(BF16)
        high[:, start : start + 128] = jnp.where(first, a, b).astype(BF16)
    py = parity("by")
    is_first = py == 0

    def select(k, near=None, far=None, columns=64):
        r, j = iota((16, columns), 0), iota((16, columns), 1)
        high_side = jnp.where(r < 8, py, 1 - py) == 0
        iy = jnp.where(high_side, 7 - k, k)
        row = r % 8 - 2
        source = jnp.where((row >= 0) & (row < 4), row * 8 + iy, -1)
        if near is not None:
            source = jnp.where(row == -1, 32 + near + iy, jnp.where(row == 4, 48 + near + iy, source))
        if far is not None:
            source = jnp.where(row == -2, 32 + far + iy, jnp.where(row == 5, 48 + far + iy, source))
        return onehot(j == source)

    def put(start, value):
        even[:, start : start + value[0].shape[1]] = value[0].astype(BF16)
        odd[:, start : start + value[1].shape[1]] = value[1].astype(BF16)

    def both(make, picked):
        return make(picked[:8]), make(picked[8:])

    cut = []
    for h in range(2):
        source = [faces[:, h * 2048 : h * 2048 + 2048], low[:, XB : XB + 2048], high[:, XB : XB + 2048]]
        cut.append(dot(select(0, 8 * h), jnp.concatenate(source, 0)))
    put(YB, (over(cut[0][:8], cut[1][:8]), over(cut[0][8:], cut[1][8:])))

    def by_side(minus, plus):
        up = jnp.where(is_first, plus[:8], minus[:8])
        down = jnp.where(is_first, minus[8:], plus[8:])
        return halves(up), halves(down)

    own1, own0 = select(1, columns=32), select(0, columns=32)

    def lanes(ref, pieces, width):
        return jnp.concatenate([ref[:, p : p + width] for p in pieces], 1)

    minus, plus = [i * 1024 for i in range(4)], [i * 1024 + 768 for i in range(4)]
    put(YA, by_side(dot(own0, lanes(blocks, minus, 256)), dot(own0, lanes(blocks, plus, 256))))
    put(YT, by_side(dot(own0, lanes(tent, minus, 256)), dot(own0, lanes(tent, plus, 256))))
    minus = [f * 1024 + i * 256 for f in range(4) for i in range(4)]
    plus = [p + 128 for p in minus]
    put(YF, by_side(dot(own1, lanes(faces, minus, 128)), dot(own1, lanes(faces, plus, 128))))
    own = traces_packed[...]
    rows = jnp.concatenate([own, low[:, XD : XD + 768], high[:, XD : XD + 768]], 0)
    g0, g1, g2 = dot(select(0, 0, 8), rows), dot(select(1, 0), rows), dot(select(2, columns=32), own)
    cut = []
    for h in range(2):
        rows = [b_packed[:, h * 384 : h * 384 + 384], low[:, XH : XH + 384], high[:, XH : XH + 384]]
        cut.append(dot(select(0, 8 * h), jnp.concatenate(rows, 0)))
    r0, r1 = jnp.concatenate(cut, 1), dot(own1, b_packed[...])
    put(YD, (over(g0[:8], g1[:8]), over(g0[8:], g1[8:])))
    put(YG, (over(g2[:8], r0[:8]), over(g2[8:], r0[8:])))
    put(YR, both(halves, r1))
    own = diagonal[...]
    d0 = dot(select(0, 0), jnp.concatenate([own, low[:, XE : XE + 128], high[:, XE : XE + 128]], 0))
    d1 = dot(own1, own)
    put(YE, (over(d0[:8], d1[:8]), over(d0[8:], d1[8:])))


def prolong_kernel(tent, t16, plus_y, minus_y, stage, t32):
    lane = iota((256, 128), 1)
    for k in range(4):
        for ph in range(8):
            chunk = tent[:, (ph * 4 + k) * 128 : (ph * 4 + k + 1) * 128].astype(F32)
            stage[k, pl.ds(ph, NE, stride=8), :] = chunk
    for k in range(4):
        both = stage[k]
        other = pltpu.roll(both, 64, 1)
        t32[pl.ds(2 * k, 256, stride=8), :] = jnp.where(lane < 64, both, other)
        t32[pl.ds(2 * k + 1, 256, stride=8), :] = jnp.where(lane < 64, other, both)
    t16[...] = t32[...].astype(BF16)
    sub = iota((8, 128), 0)
    for e in range(NE):
        plus, minus = [], []
        for h in range(2):
            base = e * 64 + 32 * h
            a, b = t32[base + 8 : base + 16, :], t32[base + 24 : base + 32, :]
            plus.append(jnp.where(sub < 4, pltpu.roll(a, 4, 0), b))
            a, b = t32[base : base + 8, :], t32[base + 16 : base + 24, :]
            minus.append(jnp.where(sub < 4, a, pltpu.roll(b, 4, 0)))
        plus_y[e * 16 : e * 16 + 16, :] = jnp.concatenate(plus, 0).astype(BF16)
        minus_y[e * 16 : e * 16 + 16, :] = jnp.concatenate(minus, 0).astype(BF16)


def stage_blocks(block_chunk, stage):
    lane = iota((NE, 128), 1)
    diag = jnp.zeros((NE, 128), F32)
    for k in range(4):
        for ph in range(8):
            c = ph * 4 + k
            chunk = block_chunk(c)
            diag = diag + jnp.where((lane == 2 * c) | (lane == 65 + 2 * c), chunk, 0.0)
            stage[k, pl.ds(ph, NE, stride=8), :] = chunk
    return diag


def reciprocal(diagonal):
    return 1.0 / jnp.where(diagonal == 0.0, 1.0, diagonal)


def operators(block_chunk, face_chunk, w, stage, fstage, w32):
    lane = iota((256, 128), 1)
    diag = stage_blocks(block_chunk, stage)
    for f in range(4):
        for ph in range(8):
            fstage[f, pl.ds(ph, NE, stride=8), :] = face_chunk(f * 8 + ph)
    folded = jnp.concatenate([fstage[f].astype(BF16) for f in range(4)], 1)
    row, col = iota((512, 128), 0), iota((512, 128), 1)
    lo_of = (row // 16) % 8
    target = 64 + row // 128 * 16 + row % 16
    for k in range(4):
        both = stage[k]
        other = pltpu.roll(both, 64, 1)
        for s, part in enumerate((both, other)):
            p_lo = 2 * k + s
            coupled = dot(folded, onehot((col == target) & (lo_of == p_lo)))
            w32[pl.ds(p_lo, 256, stride=8), :] = jnp.where(lane < 64, part, coupled)
    w[...] = w32[...].astype(BF16)
    return (diag + pltpu.roll(diag, 64, 1))[:, :64]


def own_kernel(blocks, faces, bounds, w, inverse, coefficients, *scratch):
    coefficients[...] = jnp.concatenate([jnp.broadcast_to(c, (1, 128)) for c in factors(bounds)] + [jnp.zeros((3, 128), F32)], 0)
    chunk = lambda ref: lambda c: ref[:, c * 128 : (c + 1) * 128].astype(F32)
    inverse[...] = 1.0 / operators(chunk(blocks), chunk(faces), w, *scratch)


NOTHING = (8, 128)


def part(ref, start, c, half):
    row = 8 * (c // half)
    lane = start + (c % half) * 128
    return ref[:, lane : lane + 128].astype(F32)[row : row + 8]


def halo_x(low, high, w, *scratch):
    zero = jnp.zeros(NOTHING, F32)

    def block(c):
        near_low = part(low, XA, c - 24, 4) if c >= 24 else zero
        near_high = part(high, XA, c, 4) if c < 8 else zero
        return jnp.concatenate([near_low, zero, near_high, zero], 0)

    def face(c):
        f, ph = c // 8, c % 8
        far_low = part(low, XC, f * 2 + ph - 6, 4) if ph >= 6 else zero
        far_high = part(high, XC, f * 2 + ph, 4) if ph < 2 else zero
        return jnp.concatenate([part(low, XB, c, 16), far_low, part(high, XB, c, 16), far_high], 0)

    operators(block, face, w, *scratch)


def halo_y(even, odd, w, low, high, *scratch):
    first = parity("by") == 0
    for start in range(0, YLEN, 128):
        a = even[:, start : start + 128].astype(F32)
        b = odd[:, start : start + 128].astype(F32)
        low[:, start : start + 128] = jnp.where(first, b, a).astype(BF16)
        high[:, start : start + 128] = jnp.where(first, a, b).astype(BF16)
    zero = jnp.zeros(NOTHING, F32)

    def block(c):
        i, d = c // 8, c % 8
        near_low = part(low, YA, i * 2 + d - 6, 4) if d >= 6 else zero
        near_high = part(high, YA, i * 2 + d, 4) if d < 2 else zero
        return jnp.concatenate([near_low, zero, near_high, zero], 0)

    def face(c):
        f, ph = c // 8, c % 8
        i = ph // 2
        far_low = part(low, YF, f * 4 + i, 8) if ph % 2 == 1 else zero
        far_high = part(high, YF, f * 4 + i, 8) if ph % 2 == 0 else zero
        return jnp.concatenate([part(low, YB, c, 16), far_low, part(high, YB, c, 16), far_high], 0)

    operators(block, face, w, *scratch)


def factors(bounds):
    low, high = bounds[0:1, 0:1], bounds[0:1, 1:2]
    centre = 0.5 * (high + low)
    half_width = 0.5 * (high - low)
    spread = centre / half_width
    first = 1.0 / spread
    second = 1.0 / (2.0 * spread - first)
    third = 1.0 / (2.0 * spread - second)
    return centre, half_width, first, second, third


def beside_own(columns):
    return [((ix + 3) * 16 + iy, 0, ix * 8 + iy) for ix in range(EX) for iy in columns]


def beside_x(k, columns):
    return [((7 + k if s else 2 - k) * 16 + iy, 1, s * 16 + k * 8 + iy) for s in range(2) for iy in columns]


def beside_y(k, rows):
    return [((r + 1) * 16 + (8 + k if s else 15 - k), 2, s * 16 + k * 8 + r) for s in range(2) for r in rows]


INNER, OUTER = range(1, 7), (0, 7)
EARLY = (1, 9, beside_own(INNER) + beside_x(0, INNER) + beside_x(1, INNER))
LATE = (1, 9, beside_own(OUTER) + beside_x(0, OUTER) + beside_x(1, OUTER) + beside_y(0, range(1, 7)) + beside_y(1, range(2, 6)))
SECOND = (2, 8, beside_own(range(EY)) + beside_x(0, range(EY)) + beside_y(0, range(2, 6)))
THIRD = (3, 7, beside_own(range(EY)))


def joined(value):
    return value + pltpu.roll(value, 64, 1)


def apply(plan, values, tables, t_ref, x_ref, a_ref):
    first, last, elements = plan
    lane = iota((16, 128), 1)
    x_ref[SPAN:, :] = jnp.zeros((8 * EXT - SPAN, 128), F32)
    for n in range(NRHS):
        for ri in range(first, last):
            row = n * EXT + ri * 16
            own = t_ref[row : row + 16, :]
            sides = jnp.where(
                lane < 80,
                t_ref[row - 16 : row, :],
                jnp.where(
                    lane < 96,
                    t_ref[row + 16 : row + 32, :],
                    jnp.where(lane < 112, pltpu.roll(own, 1, 0), pltpu.roll(own, 15, 0)),
                ),
            )
            x_ref[row : row + 16, :] = jnp.where(lane < 64, own if values else 0.0, sides)
    for row, table, e in elements:
        hi, lo = split(x_ref[pl.ds(row, 8, stride=EXT), :])
        out = dot(over(hi, lo), tables[table][e * 64 : e * 64 + 64, :], NT)
        a_ref[pl.ds(row, 8, stride=EXT), 0:64] = out[:8] + out[8:]


def start_smoothing(guess, b, inverse, w, wx, x_low, x_high, t_ref, r_ref, i_ref, x_ref, a_ref):
    t_ref[...] = jnp.zeros((SPAN, 128), F32)
    r_ref[...] = jnp.zeros((SPAN, 128), F32)
    i_ref[...] = jnp.ones((EXT, 128), F32)
    a_ref[...] = jnp.zeros((8 * EXT, 128), F32)
    traces = with_traces(guess[...].reshape(NRHS * NE, 64))
    for ix in range(EX):
        row = (ix + 3) * 16
        i_ref[row : row + 8, 0:64] = inverse[ix * 8 : ix * 8 + 8, :]
        for n in range(NRHS):
            source = n * NE + ix * 8
            t_ref[n * EXT + row : n * EXT + row + 8, :] = traces[source : source + 8]
            r_ref[n * EXT + row : n * EXT + row + 8, 0:64] = b[source : source + 8, :]
    for side, message in enumerate((x_low, x_high)):
        at = [(7 + k if side else 2 - k) * 16 for k in range(3)]
        near = message[:, XD : XD + 768].astype(F32)
        far = message[:, XK : XK + 256].astype(F32)
        diagonal = reciprocal(message[:, XE : XE + 128].astype(F32))
        for k in range(2):
            i_ref[at[k] : at[k] + 8, :] = diagonal[8 * k : 8 * k + 8]
        for n in range(NRHS):
            base = n * EXT
            for k in range(2):
                t_ref[base + at[k] : base + at[k] + 8, :] = joined(near[8 * k : 8 * k + 8, n * 128 : n * 128 + 128])
            t_ref[base + at[2] : base + at[2] + 8, :] = joined(unsqueeze(far[:8], n, TRACE_OFFSET[1 - side]))
            r_ref[base + at[0] : base + at[0] + 8, :] = joined(part(message, XH, n, 3))
            r_ref[base + at[1] : base + at[1] + 8, :] = joined(unsqueeze(far[8:], n, VALUE_OFFSET[1 - side]))
    apply(EARLY, False, (w, wx), t_ref, x_ref, a_ref)
    r_ref[...] = r_ref[...] - a_ref[:SPAN, :]


def smooth(guess, w, wx, wy, coefficients, y_low, y_high, t_in, r_in, i_in, smoothed, t_ref, r_ref, i_ref, x_ref, a_ref):
    t_ref[...] = t_in[...]
    r_ref[...] = r_in[...]
    i_ref[...] = i_in[...]
    a_ref[...] = jnp.zeros((8 * EXT, 128), F32)
    for side, message in enumerate((y_low, y_high)):
        column = [16 + (8 + k if side else 15 - k) for k in range(3)]
        diagonal = reciprocal(message[:, YE : YE + 128].astype(F32))
        near = message[:, YD : YD + 768].astype(F32)
        far = message[:, YG : YG + 768].astype(F32)
        for k in range(2):
            i_ref[pl.ds(column[k], 8, stride=16), :] = diagonal[8 * k : 8 * k + 8]
        for n in range(NRHS):
            lanes = slice(n * 128, n * 128 + 128)
            for k, value in enumerate((near[:8, lanes], near[8:, lanes], far[:8, lanes])):
                t_ref[pl.ds(n * EXT + column[k], 8, stride=16), :] = joined(value)
            for k, value in enumerate((far[8:, lanes], part(message, YR, n, 3))):
                r_ref[pl.ds(n * EXT + column[k], 8, stride=16), :] = joined(value)
    tables = (w, wx, wy)
    centre, half_width, first, second, third = [coefficients[i : i + 1, 0:64] for i in range(5)]
    inverse = jnp.concatenate([i_ref[:, 0:64]] * NRHS, 0)
    apply(LATE, False, tables, t_ref, x_ref, a_ref)
    r = r_ref[:, 0:64] - a_ref[:SPAN, 0:64]
    u = inverse * r / centre
    x = u
    for plan, factor, new in ((SECOND, first, second), (THIRD, second, third)):
        t_ref[...] = with_traces(u)
        apply(plan, True, tables, t_ref, x_ref, a_ref)
        r = r - a_ref[:SPAN, 0:64]
        u = new * factor * u + (2.0 * new / half_width) * inverse * r
        x = x + u
    for n in range(NRHS):
        for ix in range(EX):
            row = n * EXT + (ix + 3) * 16
            smoothed[n, ix * 8 : ix * 8 + 8, :] = guess[n, ix * 8 : ix * 8 + 8, :] + x[row : row + 8]


def ghost_rows(message, start, out):
    lane = iota((8, 128), 1)
    for j in range(8):
        both = part(message, start, j, 4)
        other = pltpu.roll(both, 64, 1)
        out[pl.ds(2 * j, 8, stride=16), :] = jnp.where(lane < 64, both, other)
        out[pl.ds(2 * j + 1, 8, stride=16), :] = jnp.where(lane < 64, other, both)


def label_masks(masks):
    lane = iota((16, 256), 1)
    for b in range(4):
        masks[b * 16 : b * 16 + 16, :] = onehot(lane // 64 == b)


def masked(masks, piece, label):
    mask = masks[pl.ds(pl.multiple_of(label * 16, 16), 16), :]
    return jnp.concatenate([piece, piece], 1) * jnp.concatenate([mask] * 4, 0)


def none(count):
    return jnp.zeros((count, 128), BF16)


def face_column(f, rows):
    return jnp.concatenate([none(64 + 16 * f), rows] + ([none(48 - 16 * f)] if f < 3 else []), 0)


def galerkin_kernel(half, labels, t16, plus_y, minus_y, w, *refs):
    (before_local, _), refs = (refs[:2], refs[2:]) if half else ((None, None), refs)
    local, edge_column, edge_columns, tt, masks, big = refs
    label_masks(masks)
    lane128 = iota((64, 128), 1)
    for pair in range(8):
        e = 16 * half + 2 * pair
        turned = t16[e * 64 : e * 64 + 128, :].astype(F32).T[:64]
        first, second = labels[e], labels[e + 1]
        for a in range(4):
            keep = jnp.where(
                lane128 < 64,
                jnp.where(first == a, 1.0, 0.0),
                jnp.where(second == a, 1.0, 0.0),
            )
            tt[a * 64 : a * 64 + 64, pair * 128 : pair * 128 + 128] = (turned * keep).astype(BF16)
    edge_column[...] = tt[:, 512 * half : 512 * half + 512]
    for f in range(2):
        for i in range(2):
            start = (4 * i + 3 * f) * 128
            edge_columns[f, :, i * 128 : i * 128 + 128] = tt[:, start : start + 128]

    def row_of_elements(ix, carry):
        for iy in range(EY):
            e = ix * EY + iy
            own = pl.ds(pl.multiple_of(e * 64, 64), 64)
            here = pl.ds(pl.multiple_of((e - 16 * half) * 64, 64), 64)
            before = pl.multiple_of(jnp.maximum(e - 8, 0) * 64, 64)
            after = pl.multiple_of(jnp.minimum(e + 8, 31) * 64, 64)
            rows = [
                t16[pl.ds(before + 48, 16), :],
                t16[pl.ds(after, 16), :],
            ]
            if iy > 0:
                rows.append(plus_y[pl.ds(pl.multiple_of((e - 1) * 16, 16), 16), :])
            else:
                rows.append(none(16))
            if iy < 7:
                rows.append(minus_y[pl.ds(pl.multiple_of((e + 1) * 16, 16), 16), :])
            columns = [jnp.concatenate([t16[own, :], none(64)], 0)]
            columns += [face_column(f, value) for f, value in enumerate(rows)]
            pieces = dot(w[own, :], jnp.concatenate(columns, 1)).astype(BF16)
            piece = lambda s: pieces[:, s * 128 : s * 128 + 128]
            big[0, here, :] = masked(masks, piece(0), labels[e])
            big[1, here, :] = masked(masks, piece(1), labels[jnp.maximum(e - 8, 0)])
            big[2, here, :] = masked(masks, piece(2), labels[jnp.minimum(e + 8, 31)])
            nothing = jnp.zeros((64, 256), BF16)
            big[3, here, :] = masked(masks, piece(3), labels[e - 1]) if iy > 0 else nothing
            big[4, here, :] = masked(masks, piece(4), labels[e + 1]) if iy < 7 else nothing
        return carry

    lax.fori_loop(2 * half, 2 * half + 2, row_of_elements, 0)
    total = dot(tt[...], big[0]) + dot(tt[...], big[3]) + dot(tt[...], big[4])
    if half:
        total = before_local[...] + total + dot(tt[...], big[1]) + dot(tt[:, :512], big[2, :512, :])
    else:
        total = total + dot(tt[:, 512:], big[1, 512:, :]) + dot(tt[...], big[2])
    local[...] = total


def ghost_block(face, message, start, first_row, elements, side_labels, label_start, w, columns, rows, masks, side, result):
    ghost_rows(message, start, rows)
    for i, (e, place) in enumerate(elements):
        near = rows[(i + first_row) * 16 : (i + first_row) * 16 + 16, :].astype(BF16)
        piece = dot(w[e * 64 : e * 64 + 64, :], face_column(face, near)).astype(BF16)
        side[place : place + 64, :] = masked(masks, piece, side_labels[label_start + i])
    width = 512 // len(columns)
    result[...] = sum(dot(c[...], side[i * width : (i + 1) * width, :]) for i, c in enumerate(columns))


def middle_kernel(side_labels, w, column0, column1, x_low, x_high, guess, b, inverse, wx, t_ref, r_ref, i_ref, ghost,
                  stage, fstage, w32, x_ref, a_ref, rows, masks, side, result, sems):
    label_masks(masks)
    copies = []
    for f, (message, column) in enumerate(((x_low, column0), (x_high, column1))):
        elements = [(24 * f + iy, iy * 64) for iy in range(EY)]
        ghost_block(f, message, XT, 0, elements, side_labels, 8 * f, w, (column,), rows, masks, side, result.at[f])
        copies.append(pltpu.make_async_copy(result.at[f], ghost.at[f], sems.at[f]))
        copies[-1].start()
    halo_x(x_low, x_high, wx, stage, fstage, w32)
    start_smoothing(guess, b, inverse, w, wx, x_low, x_high, t_ref, r_ref, i_ref, x_ref, a_ref)
    for copy in copies:
        copy.wait()


def finish_kernel(side_labels, guess, w, wx, coefficients, y_even, y_odd, columns0, columns1, t_in, r_in, i_in, ghost_in,
                  smoothed, ghost, wy, y_low, y_high, stage, fstage, w32, t_ref, r_ref, i_ref, x_ref, a_ref,
                  rows, masks, side, result, sems):
    halo_y(y_even, y_odd, wy, y_low, y_high, stage, fstage, w32)
    label_masks(masks)
    copies = []
    for f, message in enumerate((y_low, y_high)):
        side[...] = jnp.zeros((512, 256), BF16)
        elements = [(8 * ix + 7 * f, ix * 128 + 64 * f) for ix in range(EX)]
        columns = (columns0.at[f], columns1.at[f])
        ghost_block(2 + f, message, YT, 2, elements, side_labels, 16 + 4 * f, w, columns, rows, masks, side, result.at[f])
        copies.append(pltpu.make_async_copy(result.at[f], ghost.at[2 + f], sems.at[f]))
        copies[-1].start()
    smooth(guess, w, wx, wy, coefficients, y_low, y_high, t_in, r_in, i_in, smoothed, t_ref, r_ref, i_ref, x_ref, a_ref)
    for copy in copies:
        copy.wait()


def call(kernel, outs, scratch, operands, flops, moved, in_specs=None, out_specs=None, aliases=None, room=48):
    return pl.pallas_call(
        kernel,
        out_shape=outs,
        in_specs=in_specs or [VMEM] * len(operands),
        out_specs=out_specs or [VMEM] * len(outs),
        scratch_shapes=scratch,
        input_output_aliases=aliases or {},
        cost_estimate=pl.CostEstimate(flops=flops, bytes_accessed=moved, transcendentals=0),
        compiler_params=pltpu.CompilerParams(vmem_limit_bytes=room * 1024 * 1024),
    )(*operands)


def exchange(messages, axis):
    out = []
    for first, message in enumerate(messages):
        pairs = []
        for i in range(first, lax.axis_size(axis) - 1, 2):
            pairs += [(i, i + 1), (i + 1, i)]
        out.append(lax.ppermute(message, axis, pairs))
    return out


def shaped(*shape, dtype=BF16):
    return jax.ShapeDtypeStruct(shape, dtype)


STAGES = [pltpu.VMEM((4, 256, 128), F32), pltpu.VMEM((4, 256, 128), F32), pltpu.VMEM((2048, 128), F32)]


GHOST = [
    pltpu.VMEM((128, 128), F32),
    pltpu.VMEM((64, 256), BF16),
    pltpu.VMEM((512, 256), BF16),
    pltpu.VMEM((2, 256, 256), F32),
    pltpu.SemaphoreType.DMA((2,)),
]


def on_device(blocks, faces, tentative, aggregate, ghost_labels, rhs, guess, bounds):
    wide = lambda *shape: shaped(*shape, dtype=F32)
    rhs = jnp.swapaxes(rhs[0, 0], 1, 2)
    guess = jnp.swapaxes(guess[0, 0], 1, 2)
    labels, side_labels = aggregate.reshape(NE), ghost_labels.reshape(24)
    blocks, faces, tentative = [a.reshape(NE, 4096) for a in (blocks, faces, tentative)]
    even, odd, traces_packed, b_packed, b, diagonal = call(
        pack_x_kernel,
        [shaped(16, XLEN)] * 2 + [shaped(NE, 768)] * 2 + [wide(NRHS * NE, 64), shaped(NE, 128)],
        [pltpu.VMEM((NE, 4096), BF16)] * 3 + [pltpu.VMEM((NRHS, NE, 64), F32)] * 2
        + [STAGES[0], STAGES[2], pltpu.VMEM((2048, 128), BF16)] + [pltpu.VMEM((256, 128), F32)] * 2
        + [pltpu.SemaphoreType.DMA((5,))],
        (blocks, faces, tentative, guess, rhs), 10**6, 2**20, [HBM] * 5, room=62,
    )
    even, odd = exchange((even, odd), "bx")
    w, inverse, coefficients = call(
        own_kernel, [shaped(2048, 128), wide(NE, 64), wide(8, 128)], STAGES,
        (blocks, faces, bounds.reshape(1, 2)), 10**9, 2**20,
    )
    t16, plus_y, minus_y = call(
        prolong_kernel, [shaped(2048, 128), shaped(512, 128), shaped(512, 128)],
        [STAGES[0], STAGES[2]], (tentative,), 5 * 10**8, 2**20,
    )

    def galerkin(half, *more):
        return call(
            lambda *refs: galerkin_kernel(half, *refs),
            [wide(256, 256), shaped(256, 512), shaped(2, 256, 256)],
            [pltpu.VMEM((256, 1024), BF16), GHOST[1], pltpu.VMEM((5, 1024, 256), BF16)],
            (labels, t16, plus_y, minus_y, w, *more),
            2 * 10**9, 2 * 2**20, [SMEM] + [VMEM] * 4 + [VMEM, ANY][: len(more)],
        )

    local, column0, columns0 = galerkin(0)
    even, odd, x_low, x_high = call(
        pack_y_kernel, [shaped(16, YLEN)] * 2 + [shaped(16, XLEN)] * 2, [],
        (blocks, faces, tentative, traces_packed, b_packed, diagonal, even, odd, column0), 10**8, 2**20,
        [VMEM] * 8 + [ANY],
    )
    even, odd = exchange((even, odd), "by")
    local, column1, columns1 = galerkin(1, local, x_low)
    extended = [wide(SPAN, 128)] * 2 + [wide(EXT, 128)]
    fields = [pltpu.VMEM(a.shape, F32) for a in extended]
    pads = [pltpu.VMEM((8 * EXT, 128), F32)] * 2
    wx, traces, residue, inverses, ghost = call(
        middle_kernel, [shaped(2048, 128)] + extended + [wide(4, 256, 256)], STAGES + pads + GHOST,
        (side_labels, w, column0, column1, x_low, x_high, guess, b, inverse), 10**9, 2**20,
        [SMEM] + [VMEM] * 8, [VMEM] * 4 + [HBM],
    )
    smoothed, ghost = call(
        finish_kernel, [wide(NRHS, NE, 64), wide(4, 256, 256)],
        [pltpu.VMEM((2048, 128), BF16)] + [pltpu.VMEM((16, YLEN), BF16)] * 2 + STAGES + fields + pads + GHOST,
        (side_labels, guess, w, wx, coefficients, even, odd, columns0, columns1, traces, residue, inverses, ghost),
        10**9, 2**20, [SMEM] + [VMEM] * 11 + [HBM], [VMEM, HBM], {12: 1},
    )
    return jnp.swapaxes(smoothed, 1, 2)[None, None], local[None, None], ghost[None, None]


def solution(mesh):
    b = lambda extra: P("bx", "by", *([None] * extra))
    return jax.shard_map(
        on_device,
        mesh=mesh,
        in_specs=(b(2), b(2), b(2), b(1), b(1), b(3), b(3), P()),
        out_specs=(b(3), b(2), b(3)),
        check_vma=False,
    )
```

time: 39.2 us -> 36.7 us (0.936)
  the two profiles are of different devices: /device:TPU:123 before, /device:TPU:102 now
where the time goes in v5:
time: 36.7 us; the launch traced here: 36.5 us
  Pallas kernels  17.3 us (47%)
  starting transfers between devices  16.3 us (44%)
  local copies, waits for them, and re-layouts  1.97 us (5%)
  between operations  0.85 us (2%)
    pallas_call x8, Pallas kernels, call(): pl.pallas_call(kernel, out_shape=outs, in_specs=in_specs or [VMEM] * len(...  17.3 us
    ppermute x4, starting transfers between devices, exchange(): out.append(lax.ppermute(message, axis, pairs))  16.3 us
    unnamed x22, local copies, waits for them, and re-layouts  1.97 us
  transfers between devices with their start and end apart: 4, of which 0 were waited for; matrix products, arithmetic and copies ran while one was open for 0% of the time, Pallas kernels for 25%

profile of v5, /device:TPU:102, one launch (start us, length us, event | category | flops | bytes accessed | tf_op | source)
XLA Modules:
  0.0 36.5 jit_solution(7240164581947055687)
XLA Ops:
  0.6 0.0 copy-start.2
  0.6 2.8 %shard_map.106 = (bf16[16,5120]{1,0:T(8,128)(2,1)}, bf16[16,5120]{1,0:T(8,128)(2,1)}, bf16[32,768]{1,0:T(8,128)(2,1)}, bf16[32,768]{1,0:T(8,128)(2,1)}, f32[192,64]{1,0:T(8,128)}, /*index=5*/bf16[32,128]{1,0:T(8,128)(2,1)}) custom-call(bf16[32,4096]{1,0:T(8,128)(2,1)} %bitcast.17, bf16[32,4096]{1,0:T(8,128)(2,1)} %bitcast.20, bf16[32,4096]{1,0:T(8,128)(2,1)} %bitcast.23, ...), custom_call_target="tpu_custom_call" | custom-call | flops 1000000 | bytes 1048576 | tf_op jit(solution)/shard_map/pallas_call | solution.py:632
  3.5 2.7 %collective-permute-start = (bf16[16,5120]{1,0:T(8,128)(2,1)}, bf16[16,5120]{1,0:T(8,128)(2,1)S(1)}, u32[]{:S(2)}, u32[]{:S(2)}) collective-permute-start(bf16[16,5120]{1,0:T(8,128)(2,1)} %get-tuple-element.41), channel_id=1, source_target_pairs={{0,16},{16,0},{32,48},{48,32},{64,80},{80,64},{96,112},{112,96},{1... | collective-permute-start | bytes 491528 | tf_op jit(solution)/shard_map/ppermute | solution.py:650
  6.2 0.0 copy-start
  6.2 0.0 copy-start.1
  6.3 5.8 %collective-permute-start.1 = (bf16[16,5120]{1,0:T(8,128)(2,1)}, bf16[16,5120]{1,0:T(8,128)(2,1)S(1)}, u32[]{:S(2)}, u32[]{:S(2)}) collective-permute-start(bf16[16,5120]{1,0:T(8,128)(2,1)} %get-tuple-element.42), channel_id=1, source_target_pairs={{16,32},{32,16},{48,64},{64,48},{80,96},{96,80},{112,128},{128,112... | collective-permute-start | bytes 491528 | tf_op jit(solution)/shard_map/ppermute | solution.py:650
  12.1 0.0 copy-done.2
  12.1 0.3 shard_map.104
  12.4 0.0 copy-start.9
  12.4 0.0 copy-done
  12.4 0.0 copy-done.1
  12.4 0.6 %copy-done.9 = f32[2]{0:T(128)S(1)} copy-done((f32[2]{0:T(128)S(1)}, f32[2]{0:T(128)}, u32[]{:S(2)}) %copy-start.9) | copy-done | bytes 32
  13.1 0.8 %shard_map.103 = (bf16[2048,128]{1,0:T(8,128)(2,1)S(1)}, f32[32,64]{1,0:T(8,128)S(1)}, f32[8,128]{1,0:T(8,128)S(1)}) custom-call(bf16[32,4096]{1,0:T(8,128)(2,1)S(1)} %bitcast.18, bf16[32,4096]{1,0:T(8,128)(2,1)S(1)} %bitcast.21, f32[1,2]{1,0:T(1,128)S(1)} %bitcast.31), custom_call_target="tpu_custom_call" | custom-call | flops 1000000000 | bytes 1048576 | tf_op jit(solution)/shard_map/pallas_call | solution.py:632
  13.9 0.0 copy-start.10
  13.9 0.6 %copy-done.10 = s32[1,1,32]{2,1,0:T(1,128)S(1)} copy-done((s32[1,1,32]{2,1,0:T(1,128)S(1)}, s32[1,1,32]{2,1,0:T(1,128)}, u32[]{:S(2)}) %copy-start.10) | copy-done | bytes 152
  14.6 0.0 copy-start.4
  14.6 0.0 copy-start.5
  14.6 0.0 copy-start.6
  14.6 2.2 %shard_map.105 = (f32[256,256]{1,0:T(8,128)S(1)}, bf16[256,512]{1,0:T(8,128)(2,1)S(1)}, bf16[2,256,256]{2,1,0:T(8,128)(2,1)S(1)}) custom-call(s32[32]{0:T(128)S(1)} %bitcast.32, bf16[2048,128]{1,0:T(8,128)(2,1)S(1)} %get-tuple-element.33.refs_1_, bf16[512,128]{1,0:T(8,128)(2,1)S(1)} %get-tuple-element.34.refs_2_, ...), custom_call_target="tpu_custom_call" | custom-call | flops 2000000000 | bytes 2097152 | tf_op jit(solution)/shard_map/pallas_call | solution.py:632
  16.8 0.0 collective-permute-done.x_even
  16.8 0.0 collective-permute-done.1.x_odd
  16.8 0.0 copy-done.4
  16.9 0.0 copy-done.5
  16.9 0.0 copy-done.6
  16.9 0.4 %shard_map.107 = (bf16[16,6144]{1,0:T(8,128)(2,1)S(1)}, bf16[16,6144]{1,0:T(8,128)(2,1)S(1)}, bf16[16,5120]{1,0:T(8,128)(2,1)S(1)}, bf16[16,5120]{1,0:T(8,128)(2,1)S(1)}) custom-call(bf16[32,4096]{1,0:T(8,128)(2,1)S(1)} %bitcast.19, bf16[32,4096]{1,0:T(8,128)(2,1)S(1)} %bitcast.22, bf16[32,4096]{1,0:T(8,128)(2,1)S(1)} %bitcast.25, ...), custom_call_target="tpu_custom_call" | custom-call | flops 100000000 | bytes 1048576 | tf_op jit(solution)/shard_map/pallas_call | solution.py:632
  17.3 1.9 %collective-permute-start.2 = (bf16[16,6144]{1,0:T(8,128)(2,1)S(1)}, bf16[16,6144]{1,0:T(8,128)(2,1)S(1)}, u32[]{:S(2)}, u32[]{:S(2)}) collective-permute-start(bf16[16,6144]{1,0:T(8,128)(2,1)S(1)} %get-tuple-element.50), channel_id=1, source_target_pairs={{0,1},{1,0},{2,3},{3,2},{4,5},{5,4},{6,7},{7,6},{8,9},{9,8},{10,11... | collective-permute-start | bytes 589832 | tf_op jit(solution)/shard_map/ppermute | solution.py:650
  19.2 5.9 %collective-permute-start.3 = (bf16[16,6144]{1,0:T(8,128)(2,1)S(1)}, bf16[16,6144]{1,0:T(8,128)(2,1)S(1)}, u32[]{:S(2)}, u32[]{:S(2)}) collective-permute-start(bf16[16,6144]{1,0:T(8,128)(2,1)S(1)} %get-tuple-element.51), channel_id=1, source_target_pairs={{1,2},{2,1},{3,4},{4,3},{5,6},{6,5},{7,8},{8,7},{9,10},{10,9},{11,... | collective-permute-start | bytes 589832 | tf_op jit(solution)/shard_map/ppermute | solution.py:650
  25.1 0.0 copy-start.3
  25.1 0.0 copy-start.8
  25.1 3.0 %shard_map.108 = (f32[256,256]{1,0:T(8,128)}, bf16[256,512]{1,0:T(8,128)(2,1)S(1)}, bf16[2,256,256]{2,1,0:T(8,128)(2,1)S(1)}) custom-call(s32[32]{0:T(128)S(1)} %bitcast.33, bf16[2048,128]{1,0:T(8,128)(2,1)S(1)} %get-tuple-element.33.refs_1_, bf16[512,128]{1,0:T(8,128)(2,1)S(1)} %get-tuple-element.34.refs_2_, ...), custom_call_target="tpu_custom_call" | custom-call | flops 2000000000 | bytes 2097152 | tf_op jit(solution)/shard_map/pallas_call | solution.py:632
  28.1 0.0 copy-start.7
  28.1 0.0 copy-done.3
  28.1 0.0 copy-done.8
  28.1 0.6 %copy-done.7 = s32[1,1,24]{2,1,0:T(1,128)S(1)} copy-done((s32[1,1,24]{2,1,0:T(1,128)S(1)}, s32[1,1,24]{2,1,0:T(1,128)}, u32[]{:S(2)}) %copy-start.7) | copy-done | bytes 120
  28.7 2.7 %shard_map.109 = (bf16[2048,128]{1,0:T(8,128)(2,1)S(1)}, f32[960,128]{1,0:T(8,128)S(1)}, f32[960,128]{1,0:T(8,128)S(1)}, f32[160,128]{1,0:T(8,128)S(1)}, f32[4,256,256]{2,1,0:T(8,128)}) custom-call(s32[24]{0:T(128)S(1)} %bitcast.29, bf16[2048,128]{1,0:T(8,128)(2,1)S(1)} %get-tuple-element.32.refs_4_.w, bf16[256,512]{1,0:T(8,128)(2,1)S(1)} %get-tuple-element.36._.column0, ...), custom_call_target="tpu_custom_call" | custom-call | flops 1000000000 | bytes 1048576 | tf_op jit(solution)/shard_map/pallas_call | solution.py:632
  31.4 0.0 collective-permute-done.2.y_even
  31.4 0.0 collective-permute-done.3.y_odd
  31.4 5.0 %shard_map.110 = (f32[6,32,64]{2,1,0:T(8,128)}, f32[4,256,256]{2,1,0:T(8,128)}) custom-call(s32[24]{0:T(128)S(1)} %bitcast.30, f32[6,32,64]{2,1,0:T(8,128)S(1)} %bitcast.28, bf16[2048,128]{1,0:T(8,128)(2,1)S(1)} %get-tuple-element.32.refs_4_.w, bf16[2048,128]{1,0:T(8,128)(2,1)S(1)} %get-tuple-element.48.wx, ...), custom_call_target="tpu_custom_call", output_to_operand_aliasing={{1}: (12, {})} | custom-call | flops 1000000000 | bytes 1048576 | tf_op jit(solution)/shard_map/pallas_call | solution.py:632
Async XLA Ops:
  0.6 11.4 %copy-start.2 = (bf16[1,1,32,4096]{3,2,1,0:T(8,128)(2,1)S(1)}, bf16[1,1,32,4096]{3,2,1,0:T(8,128)(2,1)}, u32[]{:S(2)}) copy-start(bf16[1,1,32,4096]{3,2,1,0:T(8,128)(2,1)} %param.10) | copy-start | bytes 786436
  3.5 13.3 %collective-permute-start = (bf16[16,5120]{1,0:T(8,128)(2,1)}, bf16[16,5120]{1,0:T(8,128)(2,1)S(1)}, u32[]{:S(2)}, u32[]{:S(2)}) collective-permute-start(bf16[16,5120]{1,0:T(8,128)(2,1)} %get-tuple-element.41), channel_id=1, source_target_pairs={{0,16},{16,0},{32,48},{48,32},{64,80},{80,64},{96,112},{112,96},{1... | collective-permute-start | bytes 491528 | tf_op jit(solution)/shard_map/ppermute | solution.py:650
  6.2 6.2 %copy-start = (bf16[1,1,32,4096]{3,2,1,0:T(8,128)(2,1)S(1)}, bf16[1,1,32,4096]{3,2,1,0:T(8,128)(2,1)}, u32[]{:S(2)}) copy-start(bf16[1,1,32,4096]{3,2,1,0:T(8,128)(2,1)} %param.8) | copy-start | bytes 786436
  6.2 6.2 %copy-start.1 = (bf16[1,1,32,4096]{3,2,1,0:T(8,128)(2,1)S(1)}, bf16[1,1,32,4096]{3,2,1,0:T(8,128)(2,1)}, u32[]{:S(2)}) copy-start(bf16[1,1,32,4096]{3,2,1,0:T(8,128)(2,1)} %param.9) | copy-start | bytes 786436
  6.3 10.6 %collective-permute-start.1 = (bf16[16,5120]{1,0:T(8,128)(2,1)}, bf16[16,5120]{1,0:T(8,128)(2,1)S(1)}, u32[]{:S(2)}, u32[]{:S(2)}) collective-permute-start(bf16[16,5120]{1,0:T(8,128)(2,1)} %get-tuple-element.42), channel_id=1, source_target_pairs={{16,32},{32,16},{48,64},{64,48},{80,96},{96,80},{112,128},{128,112... | collective-permute-start | bytes 491528 | tf_op jit(solution)/shard_map/ppermute | solution.py:650
  12.4 0.7 %copy-start.9 = (f32[2]{0:T(128)S(1)}, f32[2]{0:T(128)}, u32[]{:S(2)}) copy-start(f32[2]{0:T(128)} %param.15) | copy-start | bytes 28
  13.9 0.7 %copy-start.10 = (s32[1,1,32]{2,1,0:T(1,128)S(1)}, s32[1,1,32]{2,1,0:T(1,128)}, u32[]{:S(2)}) copy-start(s32[1,1,32]{2,1,0:T(1,128)} %param.11) | copy-start | bytes 388
  14.6 2.3 %copy-start.4 = (bf16[32,768]{1,0:T(8,128)(2,1)S(1)}, bf16[32,768]{1,0:T(8,128)(2,1)}, u32[]{:S(2)}) copy-start(bf16[32,768]{1,0:T(8,128)(2,1)} %get-tuple-element.38.traces_packed) | copy-start | bytes 147460
  14.6 2.3 %copy-start.5 = (bf16[32,768]{1,0:T(8,128)(2,1)S(1)}, bf16[32,768]{1,0:T(8,128)(2,1)}, u32[]{:S(2)}) copy-start(bf16[32,768]{1,0:T(8,128)(2,1)} %get-tuple-element.39.b_packed) | copy-start | bytes 147460
  14.6 2.3 %copy-start.6 = (bf16[32,128]{1,0:T(8,128)(2,1)S(1)}, bf16[32,128]{1,0:T(8,128)(2,1)}, u32[]{:S(2)}) copy-start(bf16[32,128]{1,0:T(8,128)(2,1)} %get-tuple-element.40.diagonal) | copy-start | bytes 24580
  17.3 14.1 %collective-permute-start.2 = (bf16[16,6144]{1,0:T(8,128)(2,1)S(1)}, bf16[16,6144]{1,0:T(8,128)(2,1)S(1)}, u32[]{:S(2)}, u32[]{:S(2)}) collective-permute-start(bf16[16,6144]{1,0:T(8,128)(2,1)S(1)} %get-tuple-element.50), channel_id=1, source_target_pairs={{0,1},{1,0},{2,3},{3,2},{4,5},{5,4},{6,7},{7,6},{8,9},{9,8},{10,11... | collective-permute-start | bytes 589832 | tf_op jit(solution)/shard_map/ppermute | solution.py:650
  19.2 12.2 %collective-permute-start.3 = (bf16[16,6144]{1,0:T(8,128)(2,1)S(1)}, bf16[16,6144]{1,0:T(8,128)(2,1)S(1)}, u32[]{:S(2)}, u32[]{:S(2)}) collective-permute-start(bf16[16,6144]{1,0:T(8,128)(2,1)S(1)} %get-tuple-element.51), channel_id=1, source_target_pairs={{1,2},{2,1},{3,4},{4,3},{5,6},{6,5},{7,8},{8,7},{9,10},{10,9},{11,... | collective-permute-start | bytes 589832 | tf_op jit(solution)/shard_map/ppermute | solution.py:650
  25.1 3.0 %copy-start.3 = (f32[1,1,6,64,32]{3,4,2,1,0:T(8,128)S(1)}, f32[1,1,6,64,32]{3,4,2,1,0:T(8,128)}, u32[]{:S(2)}) copy-start(f32[1,1,6,64,32]{3,4,2,1,0:T(8,128)} %param.14) | copy-start | bytes 147460
  25.1 3.0 %copy-start.8 = (f32[192,64]{1,0:T(8,128)S(1)}, f32[192,64]{1,0:T(8,128)}, u32[]{:S(2)}) copy-start(f32[192,64]{1,0:T(8,128)} %get-tuple-element.46.b) | copy-start | bytes 147460
  28.1 0.7 %copy-start.7 = (s32[1,1,24]{2,1,0:T(1,128)S(1)}, s32[1,1,24]{2,1,0:T(1,128)}, u32[]{:S(2)}) copy-start(s32[1,1,24]{2,1,0:T(1,128)} %param.12) | copy-start | bytes 292

commit v6 on v5

--- a/solution.py
+++ b/solution.py
@@ -45,6 +45,10 @@
 
 def onehot(mask):
     return mask.astype(F32).astype(BF16)
+
+
+def none(count):
+    return jnp.zeros((count, 128), BF16)
 
 
 def split(x):
@@ -133,8 +137,9 @@
     x_ref[0:192, :] = traces
     x_ref[192:256, :] = jnp.zeros((64, 128), F32)
     copies[1].wait()
-    diag = stage_blocks(lambda c: blocks[:, c * 128 : (c + 1) * 128].astype(F32), stage)
-    diag = diag + pltpu.roll(diag, 64, 1)
+    chunk = lambda c: blocks[:, c * 128 : (c + 1) * 128].astype(F32)
+    stage_blocks(chunk, stage)
+    diag = diagonals(chunk)
     diagonal[...] = diag.astype(BF16)
     for k in range(4):
         both = stage[k]
@@ -252,7 +257,7 @@
     put(YE, (over(d0[:8], d1[:8]), over(d0[8:], d1[8:])))
 
 
-def prolong_kernel(tent, t16, plus_y, minus_y, stage, t32):
+def prolongator(tent, t16, plus_y, minus_y, stage, t32):
     lane = iota((256, 128), 1)
     for k in range(4):
         for ph in range(8):
@@ -278,15 +283,17 @@
 
 
 def stage_blocks(block_chunk, stage):
+    for k in range(4):
+        for ph in range(8):
+            stage[k, pl.ds(ph, NE, stride=8), :] = block_chunk(ph * 4 + k)
+
+
+def diagonals(block_chunk):
     lane = iota((NE, 128), 1)
     diag = jnp.zeros((NE, 128), F32)
-    for k in range(4):
-        for ph in range(8):
-            c = ph * 4 + k
-            chunk = block_chunk(c)
-            diag = diag + jnp.where((lane == 2 * c) | (lane == 65 + 2 * c), chunk, 0.0)
-            stage[k, pl.ds(ph, NE, stride=8), :] = chunk
-    return diag
+    for c in range(32):
+        diag = diag + jnp.where((lane == 2 * c) | (lane == 65 + 2 * c), block_chunk(c), 0.0)
+    return diag + pltpu.roll(diag, 64, 1)
 
 
 def reciprocal(diagonal):
@@ -295,29 +302,28 @@
 
 def operators(block_chunk, face_chunk, w, stage, fstage, w32):
     lane = iota((256, 128), 1)
-    diag = stage_blocks(block_chunk, stage)
+    stage_blocks(block_chunk, stage)
     for f in range(4):
         for ph in range(8):
             fstage[f, pl.ds(ph, NE, stride=8), :] = face_chunk(f * 8 + ph)
     folded = jnp.concatenate([fstage[f].astype(BF16) for f in range(4)], 1)
-    row, col = iota((512, 128), 0), iota((512, 128), 1)
-    lo_of = (row // 16) % 8
-    target = 64 + row // 128 * 16 + row % 16
+    t, lane16 = iota((16, 128), 0), iota((16, 128), 1)
+    moves = [onehot(lane16 == 64 + 16 * f + t) for f in range(4)]
     for k in range(4):
         both = stage[k]
         other = pltpu.roll(both, 64, 1)
         for s, part in enumerate((both, other)):
             p_lo = 2 * k + s
-            coupled = dot(folded, onehot((col == target) & (lo_of == p_lo)))
-            w32[pl.ds(p_lo, 256, stride=8), :] = jnp.where(lane < 64, part, coupled)
+            pick = jnp.concatenate([moves[f] if lo == p_lo else none(16) for f in range(4) for lo in range(8)], 0)
+            w32[pl.ds(p_lo, 256, stride=8), :] = jnp.where(lane < 64, part, dot(folded, pick))
     w[...] = w32[...].astype(BF16)
-    return (diag + pltpu.roll(diag, 64, 1))[:, :64]
-
-
-def own_kernel(blocks, faces, bounds, w, inverse, coefficients, *scratch):
+
+
+def own_operators(blocks, faces, bounds, w, inverse, coefficients, *scratch):
     coefficients[...] = jnp.concatenate([jnp.broadcast_to(c, (1, 128)) for c in factors(bounds)] + [jnp.zeros((3, 128), F32)], 0)
     chunk = lambda ref: lambda c: ref[:, c * 128 : (c + 1) * 128].astype(F32)
-    inverse[...] = 1.0 / operators(chunk(blocks), chunk(faces), w, *scratch)
+    operators(chunk(blocks), chunk(faces), w, *scratch)
+    inverse[...] = 1.0 / diagonals(chunk(blocks))[:, :64]
 
 
 NOTHING = (8, 128)
@@ -484,17 +490,20 @@
     apply(LATE, False, tables, t_ref, x_ref, a_ref)
     r = r_ref[:, 0:64] - a_ref[:SPAN, 0:64]
     u = inverse * r / centre
-    x = u
-    for plan, factor, new in ((SECOND, first, second), (THIRD, second, third)):
-        t_ref[...] = with_traces(u)
-        apply(plan, True, tables, t_ref, x_ref, a_ref)
-        r = r - a_ref[:SPAN, 0:64]
-        u = new * factor * u + (2.0 * new / half_width) * inverse * r
-        x = x + u
+    t_ref[...] = with_traces(u)
+    apply(SECOND, True, tables, t_ref, x_ref, a_ref)
+    r = r - a_ref[:SPAN, 0:64]
+    last = second * first * u + (2.0 * second / half_width) * inverse * r
+    total = u + last
+    t_ref[...] = with_traces(last)
+    apply(THIRD, True, tables, t_ref, x_ref, a_ref)
     for n in range(NRHS):
         for ix in range(EX):
             row = n * EXT + (ix + 3) * 16
-            smoothed[n, ix * 8 : ix * 8 + 8, :] = guess[n, ix * 8 : ix * 8 + 8, :] + x[row : row + 8]
+            own, place = slice(row, row + 8), slice(ix * 8, ix * 8 + 8)
+            residue = r[own] - a_ref[row : row + 8, 0:64]
+            update = third * second * last[own] + (2.0 * third / half_width) * inverse[own] * residue
+            smoothed[n, place, :] = guess[n, place, :] + total[own] + update
 
 
 def ghost_rows(message, start, out):
@@ -517,17 +526,11 @@
     return jnp.concatenate([piece, piece], 1) * jnp.concatenate([mask] * 4, 0)
 
 
-def none(count):
-    return jnp.zeros((count, 128), BF16)
-
-
 def face_column(f, rows):
     return jnp.concatenate([none(64 + 16 * f), rows] + ([none(48 - 16 * f)] if f < 3 else []), 0)
 
 
-def galerkin_kernel(half, labels, t16, plus_y, minus_y, w, *refs):
-    (before_local, _), refs = (refs[:2], refs[2:]) if half else ((None, None), refs)
-    local, edge_column, edge_columns, tt, masks, big = refs
+def galerkin(half, before_local, labels, t16, plus_y, minus_y, w, local, edge_column, edge_columns, tt, masks, big):
     label_masks(masks)
     lane128 = iota((64, 128), 1)
     for pair in range(8):
@@ -595,9 +598,17 @@
     result[...] = sum(dot(c[...], side[i * width : (i + 1) * width, :]) for i, c in enumerate(columns))
 
 
-def middle_kernel(side_labels, w, column0, column1, x_low, x_high, guess, b, inverse, wx, t_ref, r_ref, i_ref, ghost,
-                  stage, fstage, w32, x_ref, a_ref, rows, masks, side, result, sems):
-    label_masks(masks)
+def x_wait_kernel(labels, _, blocks, faces, tent, bounds, w, inverse, coefficients, t16, plus_y, minus_y, local, column, columns,
+                  stage, fstage, w32, tt, masks, big):
+    own_operators(blocks, faces, bounds, w, inverse, coefficients, stage, fstage, w32)
+    prolongator(tent, t16, plus_y, minus_y, fstage, w32)
+    galerkin(0, None, labels, t16, plus_y, minus_y, w, local, column, columns, tt, masks, big)
+
+
+def y_wait_kernel(labels, side_labels, t16, plus_y, minus_y, w, before_local, column0, x_low, x_high, guess, b, inverse,
+                  local, columns, wx, t_ref, r_ref, i_ref, ghost,
+                  stage, fstage, w32, x_ref, a_ref, rows, masks, side, result, sems, column1, tt, big):
+    galerkin(1, before_local, labels, t16, plus_y, minus_y, w, local, column1, columns, tt, masks, big)
     copies = []
     for f, (message, column) in enumerate(((x_low, column0), (x_high, column1))):
         elements = [(24 * f + iy, iy * 64) for iy in range(EY)]
@@ -682,39 +693,28 @@
         (blocks, faces, tentative, guess, rhs), 10**6, 2**20, [HBM] * 5, room=62,
     )
     even, odd = exchange((even, odd), "bx")
-    w, inverse, coefficients = call(
-        own_kernel, [shaped(2048, 128), wide(NE, 64), wide(8, 128)], STAGES,
-        (blocks, faces, bounds.reshape(1, 2)), 10**9, 2**20,
+    half = [wide(256, 256), shaped(256, 512), shaped(2, 256, 256)]
+    halves_scratch = [pltpu.VMEM((256, 1024), BF16), GHOST[1], pltpu.VMEM((5, 1024, 256), BF16)]
+    w, inverse, coefficients, t16, plus_y, minus_y, local, column0, columns0 = call(
+        x_wait_kernel,
+        [shaped(2048, 128), wide(NE, 64), wide(8, 128), shaped(2048, 128), shaped(512, 128), shaped(512, 128)] + half,
+        STAGES + halves_scratch,
+        (labels, side_labels, blocks, faces, tentative, bounds.reshape(1, 2)), 4 * 10**9, 2**22, [SMEM] * 2 + [VMEM] * 4,
     )
-    t16, plus_y, minus_y = call(
-        prolong_kernel, [shaped(2048, 128), shaped(512, 128), shaped(512, 128)],
-        [STAGES[0], STAGES[2]], (tentative,), 5 * 10**8, 2**20,
-    )
-
-    def galerkin(half, *more):
-        return call(
-            lambda *refs: galerkin_kernel(half, *refs),
-            [wide(256, 256), shaped(256, 512), shaped(2, 256, 256)],
-            [pltpu.VMEM((256, 1024), BF16), GHOST[1], pltpu.VMEM((5, 1024, 256), BF16)],
-            (labels, t16, plus_y, minus_y, w, *more),
-            2 * 10**9, 2 * 2**20, [SMEM] + [VMEM] * 4 + [VMEM, ANY][: len(more)],
-        )
-
-    local, column0, columns0 = galerkin(0)
     even, odd, x_low, x_high = call(
         pack_y_kernel, [shaped(16, YLEN)] * 2 + [shaped(16, XLEN)] * 2, [],
         (blocks, faces, tentative, traces_packed, b_packed, diagonal, even, odd, column0), 10**8, 2**20,
         [VMEM] * 8 + [ANY],
     )
     even, odd = exchange((even, odd), "by")
-    local, column1, columns1 = galerkin(1, local, x_low)
     extended = [wide(SPAN, 128)] * 2 + [wide(EXT, 128)]
     fields = [pltpu.VMEM(a.shape, F32) for a in extended]
     pads = [pltpu.VMEM((8 * EXT, 128), F32)] * 2
-    wx, traces, residue, inverses, ghost = call(
-        middle_kernel, [shaped(2048, 128)] + extended + [wide(4, 256, 256)], STAGES + pads + GHOST,
-        (side_labels, w, column0, column1, x_low, x_high, guess, b, inverse), 10**9, 2**20,
-        [SMEM] + [VMEM] * 8, [VMEM] * 4 + [HBM],
+    local, columns1, wx, traces, residue, inverses, ghost = call(
+        y_wait_kernel, [half[0], half[2], shaped(2048, 128)] + extended + [wide(4, 256, 256)],
+        STAGES + pads + GHOST + [pltpu.VMEM((256, 512), BF16), halves_scratch[0], halves_scratch[2]],
+        (labels, side_labels, t16, plus_y, minus_y, w, local, column0, x_low, x_high, guess, b, inverse), 4 * 10**9, 2**22,
+        [SMEM] * 2 + [VMEM] * 11, [VMEM] * 6 + [HBM],
     )
     smoothed, ghost = call(
         finish_kernel, [wide(NRHS, NE, 64), wide(4, 256, 256)],

time: 36.7 us -> 35.6 us (0.970)
  the two profiles are of different devices: /device:TPU:102 before, /device:TPU:281 now
where the time goes in v6:
time: 35.6 us; the launch traced here: 35.4 us
  Pallas kernels  16.4 us (46%)
  starting transfers between devices  12.7 us (36%)
  waiting for transfers between devices  4.77 us (13%)
  between operations  0.82 us (2%)
  local copies, waits for them, and re-layouts  0.67 us (2%)
    pallas_call x5, Pallas kernels, call(): pl.pallas_call(kernel, out_shape=outs, in_specs=in_specs or [VMEM] * len(...  16.4 us
    ppermute x4, starting transfers between devices, exchange(): out.append(lax.ppermute(message, axis, pairs))  12.7 us
    ppermute x4, waiting for transfers between devices, exchange(): out.append(lax.ppermute(message, axis, pairs))  4.77 us
  transfers between devices with their start and end apart: 4, of which 2 were waited for; matrix products, arithmetic and copies ran while one was open for 0% of the time, Pallas kernels for 23%

profile of v6, /device:TPU:281, one launch (start us, length us, event | category | flops | bytes accessed | tf_op | source)
XLA Modules:
  0.0 35.4 jit_solution(3993892491750813619)
XLA Ops:
  0.6 0.0 copy-start
  0.6 0.0 copy-start.1
  0.7 0.0 copy-start.2
  0.7 2.8 %shard_map.104 = (bf16[16,5120]{1,0:T(8,128)(2,1)}, bf16[16,5120]{1,0:T(8,128)(2,1)}, bf16[32,768]{1,0:T(8,128)(2,1)}, bf16[32,768]{1,0:T(8,128)(2,1)}, f32[192,64]{1,0:T(8,128)}, /*index=5*/bf16[32,128]{1,0:T(8,128)(2,1)}) custom-call(bf16[32,4096]{1,0:T(8,128)(2,1)} %bitcast.17, bf16[32,4096]{1,0:T(8,128)(2,1)} %bitcast.20, bf16[32,4096]{1,0:T(8,128)(2,1)} %bitcast.23, ...), custom_call_target="tpu_custom_call" | custom-call | flops 1000000 | bytes 1048576 | tf_op jit(solution)/shard_map/pallas_call | solution.py:643
  3.5 3.1 %collective-permute-start = (bf16[16,5120]{1,0:T(8,128)(2,1)}, bf16[16,5120]{1,0:T(8,128)(2,1)S(1)}, u32[]{:S(2)}, u32[]{:S(2)}) collective-permute-start(bf16[16,5120]{1,0:T(8,128)(2,1)} %get-tuple-element.40), channel_id=1, source_target_pairs={{0,16},{16,0},{32,48},{48,32},{64,80},{80,64},{96,112},{112,96},{1... | collective-permute-start | bytes 491528 | tf_op jit(solution)/shard_map/ppermute | solution.py:661
  6.6 1.9 %collective-permute-start.1 = (bf16[16,5120]{1,0:T(8,128)(2,1)}, bf16[16,5120]{1,0:T(8,128)(2,1)S(1)}, u32[]{:S(2)}, u32[]{:S(2)}) collective-permute-start(bf16[16,5120]{1,0:T(8,128)(2,1)} %get-tuple-element.41), channel_id=1, source_target_pairs={{16,32},{32,16},{48,64},{64,48},{80,96},{96,80},{112,128},{128,112... | collective-permute-start | bytes 491528 | tf_op jit(solution)/shard_map/ppermute | solution.py:661
  8.6 0.0 copy-start.7
  8.6 0.0 copy-start.9
  8.6 0.0 copy-start.10
  8.6 0.0 copy-done
  8.6 0.0 copy-done.1
  8.6 0.0 copy-done.2
  8.6 0.6 %copy-done.7 = s32[1,1,24]{2,1,0:T(1,128)S(1)} copy-done((s32[1,1,24]{2,1,0:T(1,128)S(1)}, s32[1,1,24]{2,1,0:T(1,128)}, u32[]{:S(2)}) %copy-start.7) | copy-done | bytes 120
  9.2 0.0 copy-done.9
  9.2 0.0 copy-done.10
  9.3 0.0 copy-start.4
  9.3 0.0 copy-start.5
  9.3 0.0 copy-start.6
  9.3 3.4 %shard_map.103 = (bf16[2048,128]{1,0:T(8,128)(2,1)S(1)}, f32[32,64]{1,0:T(8,128)S(1)}, f32[8,128]{1,0:T(8,128)S(1)}, bf16[2048,128]{1,0:T(8,128)(2,1)S(1)}, bf16...) custom-call(s32[32]{0:T(128)S(1)} %bitcast.33, ...), custom_call_target="tpu_custom_call" | custom-call | flops 4000000000 | bytes 4194304 | tf_op jit(solution)/shard_map/pallas_call | solution.py:643
  12.7 0.0 collective-permute-done.x_even
  12.7 2.9 %collective-permute-done.1.x_odd = bf16[16,5120]{1,0:T(8,128)(2,1)S(1)} collective-permute-done((bf16[16,5120]{1,0:T(8,128)(2,1)}, bf16[16,5120]{1,0:T(8,128)(2,1)S(1)}, u32[]{:S(2)}, u32[]{:S(2)}) %collective-permute-start.1) | collective-permute-done | bytes 163872 | tf_op jit(solution)/shard_map/ppermute | solution.py:661
  15.6 0.0 copy-done.4
  15.6 0.0 copy-done.5
  15.6 0.0 copy-done.6
  15.6 0.0 copy-start.3
  15.6 0.0 copy-start.8
  15.6 0.4 %shard_map.105 = (bf16[16,6144]{1,0:T(8,128)(2,1)S(1)}, bf16[16,6144]{1,0:T(8,128)(2,1)S(1)}, bf16[16,5120]{1,0:T(8,128)(2,1)S(1)}, bf16[16,5120]{1,0:T(8,128)(2,1)S(1)}) custom-call(bf16[32,4096]{1,0:T(8,128)(2,1)S(1)} %bitcast.19, bf16[32,4096]{1,0:T(8,128)(2,1)S(1)} %bitcast.22, bf16[32,4096]{1,0:T(8,128)(2,1)S(1)} %bitcast.25, ...), custom_call_target="tpu_custom_call" | custom-call | flops 100000000 | bytes 1048576 | tf_op jit(solution)/shard_map/pallas_call | solution.py:643
  16.0 3.8 %collective-permute-start.2 = (bf16[16,6144]{1,0:T(8,128)(2,1)S(1)}, bf16[16,6144]{1,0:T(8,128)(2,1)S(1)}, u32[]{:S(2)}, u32[]{:S(2)}) collective-permute-start(bf16[16,6144]{1,0:T(8,128)(2,1)S(1)} %get-tuple-element.48), channel_id=1, source_target_pairs={{0,1},{1,0},{2,3},{3,2},{4,5},{5,4},{6,7},{7,6},{8,9},{9,8},{10,11... | collective-permute-start | bytes 589832 | tf_op jit(solution)/shard_map/ppermute | solution.py:661
  19.8 3.9 %collective-permute-start.3 = (bf16[16,6144]{1,0:T(8,128)(2,1)S(1)}, bf16[16,6144]{1,0:T(8,128)(2,1)S(1)}, u32[]{:S(2)}, u32[]{:S(2)}) collective-permute-start(bf16[16,6144]{1,0:T(8,128)(2,1)S(1)} %get-tuple-element.49), channel_id=1, source_target_pairs={{1,2},{2,1},{3,4},{4,3},{5,6},{6,5},{7,8},{8,7},{9,10},{10,9},{11,... | collective-permute-start | bytes 589832 | tf_op jit(solution)/shard_map/ppermute | solution.py:661
  23.7 0.0 copy-done.3
  23.8 0.0 copy-done.8
  23.8 4.8 %shard_map.106 = (f32[256,256]{1,0:T(8,128)}, bf16[2,256,256]{2,1,0:T(8,128)(2,1)S(1)}, bf16[2048,128]{1,0:T(8,128)(2,1)S(1)}, f32[960,128]{1,0:T(8,128)S(1)}, f...) custom-call(s32[32]{0:T(128)S(1)} %bitcast.34, s32[24]{0:T(128)S(1)} %bitcast.30, ...), custom_call_target="tpu_custom_call" | custom-call | flops 4000000000 | bytes 4194304 | tf_op jit(solution)/shard_map/pallas_call | solution.py:643
  28.6 0.0 collective-permute-done.2.y_even
  28.6 1.9 %collective-permute-done.3.y_odd = bf16[16,6144]{1,0:T(8,128)(2,1)S(1)} collective-permute-done((bf16[16,6144]{1,0:T(8,128)(2,1)S(1)}, bf16[16,6144]{1,0:T(8,128)(2,1)S(1)}, u32[]{:S(2)}, u32[]{:S(2)}) %collective-permute-start.3) | collective-permute-done | bytes 196640 | tf_op jit(solution)/shard_map/ppermute | solution.py:661
  30.4 5.0 %shard_map.107 = (f32[6,32,64]{2,1,0:T(8,128)}, f32[4,256,256]{2,1,0:T(8,128)}) custom-call(s32[24]{0:T(128)S(1)} %bitcast.31, f32[6,32,64]{2,1,0:T(8,128)S(1)} %bitcast.28, bf16[2048,128]{1,0:T(8,128)(2,1)S(1)} %get-tuple-element.31.w, bf16[2048,128]{1,0:T(8,128)(2,1)S(1)} %get-tuple-element.46.wx, ...), custom_call_target="tpu_custom_call", output_to_operand_aliasing={{1}: (12, {})} | custom-call | flops 1000000000 | bytes 1048576 | tf_op jit(solution)/shard_map/pallas_call | solution.py:643
Async XLA Ops:
  0.6 8.0 %copy-start = (bf16[1,1,32,4096]{3,2,1,0:T(8,128)(2,1)S(1)}, bf16[1,1,32,4096]{3,2,1,0:T(8,128)(2,1)}, u32[]{:S(2)}) copy-start(bf16[1,1,32,4096]{3,2,1,0:T(8,128)(2,1)} %param.8) | copy-start | bytes 786436
  0.6 8.0 %copy-start.1 = (bf16[1,1,32,4096]{3,2,1,0:T(8,128)(2,1)S(1)}, bf16[1,1,32,4096]{3,2,1,0:T(8,128)(2,1)}, u32[]{:S(2)}) copy-start(bf16[1,1,32,4096]{3,2,1,0:T(8,128)(2,1)} %param.9) | copy-start | bytes 786436
  0.7 8.0 %copy-start.2 = (bf16[1,1,32,4096]{3,2,1,0:T(8,128)(2,1)S(1)}, bf16[1,1,32,4096]{3,2,1,0:T(8,128)(2,1)}, u32[]{:S(2)}) copy-start(bf16[1,1,32,4096]{3,2,1,0:T(8,128)(2,1)} %param.10) | copy-start | bytes 786436
  3.5 9.2 %collective-permute-start = (bf16[16,5120]{1,0:T(8,128)(2,1)}, bf16[16,5120]{1,0:T(8,128)(2,1)S(1)}, u32[]{:S(2)}, u32[]{:S(2)}) collective-permute-start(bf16[16,5120]{1,0:T(8,128)(2,1)} %get-tuple-element.40), channel_id=1, source_target_pairs={{0,16},{16,0},{32,48},{48,32},{64,80},{80,64},{96,112},{112,96},{1... | collective-permute-start | bytes 491528 | tf_op jit(solution)/shard_map/ppermute | solution.py:661
  6.6 9.0 %collective-permute-start.1 = (bf16[16,5120]{1,0:T(8,128)(2,1)}, bf16[16,5120]{1,0:T(8,128)(2,1)S(1)}, u32[]{:S(2)}, u32[]{:S(2)}) collective-permute-start(bf16[16,5120]{1,0:T(8,128)(2,1)} %get-tuple-element.41), channel_id=1, source_target_pairs={{16,32},{32,16},{48,64},{64,48},{80,96},{96,80},{112,128},{128,112... | collective-permute-start | bytes 491528 | tf_op jit(solution)/shard_map/ppermute | solution.py:661
  8.6 0.7 %copy-start.7 = (s32[1,1,24]{2,1,0:T(1,128)S(1)}, s32[1,1,24]{2,1,0:T(1,128)}, u32[]{:S(2)}) copy-start(s32[1,1,24]{2,1,0:T(1,128)} %param.12) | copy-start | bytes 292
  8.6 0.7 %copy-start.9 = (f32[2]{0:T(128)S(1)}, f32[2]{0:T(128)}, u32[]{:S(2)}) copy-start(f32[2]{0:T(128)} %param.15) | copy-start | bytes 28
  8.6 0.7 %copy-start.10 = (s32[1,1,32]{2,1,0:T(1,128)S(1)}, s32[1,1,32]{2,1,0:T(1,128)}, u32[]{:S(2)}) copy-start(s32[1,1,32]{2,1,0:T(1,128)} %param.11) | copy-start | bytes 388
  9.3 6.3 %copy-start.4 = (bf16[32,768]{1,0:T(8,128)(2,1)S(1)}, bf16[32,768]{1,0:T(8,128)(2,1)}, u32[]{:S(2)}) copy-start(bf16[32,768]{1,0:T(8,128)(2,1)} %get-tuple-element.37.traces_packed) | copy-start | bytes 147460
  9.3 6.3 %copy-start.5 = (bf16[32,768]{1,0:T(8,128)(2,1)S(1)}, bf16[32,768]{1,0:T(8,128)(2,1)}, u32[]{:S(2)}) copy-start(bf16[32,768]{1,0:T(8,128)(2,1)} %get-tuple-element.38.b_packed) | copy-start | bytes 147460
  9.3 6.3 %copy-start.6 = (bf16[32,128]{1,0:T(8,128)(2,1)S(1)}, bf16[32,128]{1,0:T(8,128)(2,1)}, u32[]{:S(2)}) copy-start(bf16[32,128]{1,0:T(8,128)(2,1)} %get-tuple-element.39.diagonal) | copy-start | bytes 24580
  15.6 8.1 %copy-start.3 = (f32[1,1,6,64,32]{3,4,2,1,0:T(8,128)S(1)}, f32[1,1,6,64,32]{3,4,2,1,0:T(8,128)}, u32[]{:S(2)}) copy-start(f32[1,1,6,64,32]{3,4,2,1,0:T(8,128)} %param.14) | copy-start | bytes 147460
  15.6 8.1 %copy-start.8 = (f32[192,64]{1,0:T(8,128)S(1)}, f32[192,64]{1,0:T(8,128)}, u32[]{:S(2)}) copy-start(f32[192,64]{1,0:T(8,128)} %get-tuple-element.44.b) | copy-start | bytes 147460
  16.0 12.5 %collective-permute-start.2 = (bf16[16,6144]{1,0:T(8,128)(2,1)S(1)}, bf16[16,6144]{1,0:T(8,128)(2,1)S(1)}, u32[]{:S(2)}, u32[]{:S(2)}) collective-permute-start(bf16[16,6144]{1,0:T(8,128)(2,1)S(1)} %get-tuple-element.48), channel_id=1, source_target_pairs={{0,1},{1,0},{2,3},{3,2},{4,5},{5,4},{6,7},{7,6},{8,9},{9,8},{10,11... | collective-permute-start | bytes 589832 | tf_op jit(solution)/shard_map/ppermute | solution.py:661
  19.8 10.6 %collective-permute-start.3 = (bf16[16,6144]{1,0:T(8,128)(2,1)S(1)}, bf16[16,6144]{1,0:T(8,128)(2,1)S(1)}, u32[]{:S(2)}, u32[]{:S(2)}) collective-permute-start(bf16[16,6144]{1,0:T(8,128)(2,1)S(1)} %get-tuple-element.49), channel_id=1, source_target_pairs={{1,2},{2,1},{3,4},{4,3},{5,6},{6,5},{7,8},{8,7},{9,10},{10,9},{11,... | collective-permute-start | bytes 589832 | tf_op jit(solution)/shard_map/ppermute | solution.py:661

commit v7 on v6

--- a/solution.py
+++ b/solution.py
@@ -119,7 +119,7 @@
 TRACE_OFFSET, VALUE_OFFSET = (16, 0), (0, 48)
 
 
-def pack_x_kernel(blocks_in, faces_in, tent_in, guess_in, rhs_in, even, odd, traces_packed, b_packed, b_out, diagonal,
+def pack_x_kernel(blocks_in, faces_in, tent_in, guess_in, rhs_in, odd, even, traces_packed, b_packed, b_out, diagonal,
                   blocks, faces, tent, guess, rhs, stage, w32, w16, x_ref, a_ref, sems):
     copies = [
         pltpu.make_async_copy(source, target, sems.at[i])
@@ -189,7 +189,7 @@
     put(XE, 128, lambda s: over(packed(diag, 0, s), packed(diag, 1, s)))
 
 
-def pack_y_kernel(blocks, faces, tent, traces_packed, b_packed, diagonal, x_even, x_odd, _, even, odd, low, high):
+def pack_y_kernel(blocks, faces, tent, traces_packed, b_packed, diagonal, x_odd, x_even, _, odd, even, low, high):
     first = parity("bx") == 0
     for start in range(0, XLEN, 128):
         a = x_even[:, start : start + 128].astype(F32)
@@ -470,7 +470,7 @@
     t_ref[...] = t_in[...]
     r_ref[...] = r_in[...]
     i_ref[...] = i_in[...]
-    a_ref[...] = jnp.zeros((8 * EXT, 128), F32)
+    a_ref[:SPAN, :] = jnp.zeros((SPAN, 128), F32)
     for side, message in enumerate((y_low, y_high)):
         column = [16 + (8 + k if side else 15 - k) for k in range(3)]
         diagonal = reciprocal(message[:, YE : YE + 128].astype(F32))
@@ -486,24 +486,38 @@
                 r_ref[pl.ds(n * EXT + column[k], 8, stride=16), :] = joined(value)
     tables = (w, wx, wy)
     centre, half_width, first, second, third = [coefficients[i : i + 1, 0:64] for i in range(5)]
-    inverse = jnp.concatenate([i_ref[:, 0:64]] * NRHS, 0)
+
+    def put_traces(parts, start):
+        rows = parts[0].shape[0]
+        traces = with_traces(jnp.concatenate(parts, 0))
+        for n in range(NRHS):
+            t_ref[n * EXT + start : n * EXT + start + rows, :] = traces[n * rows : n * rows + rows]
+
     apply(LATE, False, tables, t_ref, x_ref, a_ref)
-    r = r_ref[:, 0:64] - a_ref[:SPAN, 0:64]
-    u = inverse * r / centre
-    t_ref[...] = with_traces(u)
+    inverse = i_ref[16:144, 0:64]
+    residues, updates = [], []
+    for n in range(NRHS):
+        rows = slice(n * EXT + 16, n * EXT + 144)
+        r = r_ref[rows, 0:64] - a_ref[rows, 0:64]
+        residues.append(r[16:112])
+        updates.append(inverse * r / centre)
+    put_traces(updates, 16)
     apply(SECOND, True, tables, t_ref, x_ref, a_ref)
-    r = r - a_ref[:SPAN, 0:64]
-    last = second * first * u + (2.0 * second / half_width) * inverse * r
-    total = u + last
-    t_ref[...] = with_traces(last)
+    inverse = i_ref[32:128, 0:64]
+    lasts = []
+    for n in range(NRHS):
+        residues[n] = residues[n] - a_ref[n * EXT + 32 : n * EXT + 128, 0:64]
+        updates[n] = updates[n][16:112]
+        lasts.append(second * first * updates[n] + (2.0 * second / half_width) * inverse * residues[n])
+    put_traces(lasts, 32)
     apply(THIRD, True, tables, t_ref, x_ref, a_ref)
     for n in range(NRHS):
         for ix in range(EX):
-            row = n * EXT + (ix + 3) * 16
-            own, place = slice(row, row + 8), slice(ix * 8, ix * 8 + 8)
-            residue = r[own] - a_ref[row : row + 8, 0:64]
-            update = third * second * last[own] + (2.0 * third / half_width) * inverse[own] * residue
-            smoothed[n, place, :] = guess[n, place, :] + total[own] + update
+            row, place = n * EXT + (ix + 3) * 16, slice(ix * 8, ix * 8 + 8)
+            own = slice(ix * 16 + 16, ix * 16 + 24)
+            residue = residues[n][own] - a_ref[row : row + 8, 0:64]
+            update = third * second * lasts[n][own] + (2.0 * third / half_width) * inverse[own] * residue
+            smoothed[n, place, :] = guess[n, place, :] + updates[n][own] + lasts[n][own] + update
 
 
 def ghost_rows(message, start, out):
@@ -521,9 +535,16 @@
         masks[b * 16 : b * 16 + 16, :] = onehot(lane // 64 == b)
 
 
+def mask_of(masks, label):
+    return masks[pl.ds(pl.multiple_of(label * 16, 16), 16), :]
+
+
+def times(piece, mask):
+    return jnp.concatenate([piece, piece], 1) * jnp.concatenate([mask] * 4, 0)
+
+
 def masked(masks, piece, label):
-    mask = masks[pl.ds(pl.multiple_of(label * 16, 16), 16), :]
-    return jnp.concatenate([piece, piece], 1) * jnp.concatenate([mask] * 4, 0)
+    return times(piece, mask_of(masks, label))
 
 
 def face_column(f, rows):
@@ -588,12 +609,12 @@
     local[...] = total
 
 
-def ghost_block(face, message, start, first_row, elements, side_labels, label_start, w, columns, rows, masks, side, result):
+def ghost_block(face, message, start, first_row, elements, mask, w, columns, rows, side, result):
     ghost_rows(message, start, rows)
     for i, (e, place) in enumerate(elements):
         near = rows[(i + first_row) * 16 : (i + first_row) * 16 + 16, :].astype(BF16)
         piece = dot(w[e * 64 : e * 64 + 64, :], face_column(face, near)).astype(BF16)
-        side[place : place + 64, :] = masked(masks, piece, side_labels[label_start + i])
+        side[place : place + 64, :] = times(piece, mask(i))
     width = 512 // len(columns)
     result[...] = sum(dot(c[...], side[i * width : (i + 1) * width, :]) for i, c in enumerate(columns))
 
@@ -606,32 +627,35 @@
 
 
 def y_wait_kernel(labels, side_labels, t16, plus_y, minus_y, w, before_local, column0, x_low, x_high, guess, b, inverse,
-                  local, columns, wx, t_ref, r_ref, i_ref, ghost,
+                  local, columns, wx, mask_rows, t_ref, r_ref, i_ref, ghost,
                   stage, fstage, w32, x_ref, a_ref, rows, masks, side, result, sems, column1, tt, big):
     galerkin(1, before_local, labels, t16, plus_y, minus_y, w, local, column1, columns, tt, masks, big)
     copies = []
     for f, (message, column) in enumerate(((x_low, column0), (x_high, column1))):
         elements = [(24 * f + iy, iy * 64) for iy in range(EY)]
-        ghost_block(f, message, XT, 0, elements, side_labels, 8 * f, w, (column,), rows, masks, side, result.at[f])
+        mask = lambda i: mask_of(masks, side_labels[8 * f + i])
+        ghost_block(f, message, XT, 0, elements, mask, w, (column,), rows, side, result.at[f])
         copies.append(pltpu.make_async_copy(result.at[f], ghost.at[f], sems.at[f]))
         copies[-1].start()
+    for i in range(8):
+        mask_rows[i * 16 : i * 16 + 16, :] = mask_of(masks, side_labels[16 + i])
     halo_x(x_low, x_high, wx, stage, fstage, w32)
     start_smoothing(guess, b, inverse, w, wx, x_low, x_high, t_ref, r_ref, i_ref, x_ref, a_ref)
     for copy in copies:
         copy.wait()
 
 
-def finish_kernel(side_labels, guess, w, wx, coefficients, y_even, y_odd, columns0, columns1, t_in, r_in, i_in, ghost_in,
+def finish_kernel(mask_rows, guess, w, wx, coefficients, y_odd, y_even, columns0, columns1, t_in, r_in, i_in, ghost_in,
                   smoothed, ghost, wy, y_low, y_high, stage, fstage, w32, t_ref, r_ref, i_ref, x_ref, a_ref,
-                  rows, masks, side, result, sems):
+                  rows, side, result, sems):
     halo_y(y_even, y_odd, wy, y_low, y_high, stage, fstage, w32)
-    label_masks(masks)
     copies = []
     for f, message in enumerate((y_low, y_high)):
         side[...] = jnp.zeros((512, 256), BF16)
         elements = [(8 * ix + 7 * f, ix * 128 + 64 * f) for ix in range(EX)]
         columns = (columns0.at[f], columns1.at[f])
-        ghost_block(2 + f, message, YT, 2, elements, side_labels, 16 + 4 * f, w, columns, rows, masks, side, result.at[f])
+        mask = lambda i: mask_rows[(4 * f + i) * 16 : (4 * f + i) * 16 + 16, :]
+        ghost_block(2 + f, message, YT, 2, elements, mask, w, columns, rows, side, result.at[f])
         copies.append(pltpu.make_async_copy(result.at[f], ghost.at[2 + f], sems.at[f]))
         copies[-1].start()
     smooth(guess, w, wx, wy, coefficients, y_low, y_high, t_in, r_in, i_in, smoothed, t_ref, r_ref, i_ref, x_ref, a_ref)
@@ -654,7 +678,7 @@
 
 def exchange(messages, axis):
     out = []
-    for first, message in enumerate(messages):
+    for first, message in zip((1, 0), messages):
         pairs = []
         for i in range(first, lax.axis_size(axis) - 1, 2):
             pairs += [(i, i + 1), (i + 1, i)]
@@ -684,7 +708,7 @@
     guess = jnp.swapaxes(guess[0, 0], 1, 2)
     labels, side_labels = aggregate.reshape(NE), ghost_labels.reshape(24)
     blocks, faces, tentative = [a.reshape(NE, 4096) for a in (blocks, faces, tentative)]
-    even, odd, traces_packed, b_packed, b, diagonal = call(
+    odd, even, traces_packed, b_packed, b, diagonal = call(
         pack_x_kernel,
         [shaped(16, XLEN)] * 2 + [shaped(NE, 768)] * 2 + [wide(NRHS * NE, 64), shaped(NE, 128)],
         [pltpu.VMEM((NE, 4096), BF16)] * 3 + [pltpu.VMEM((NRHS, NE, 64), F32)] * 2
@@ -692,7 +716,7 @@
         + [pltpu.SemaphoreType.DMA((5,))],
         (blocks, faces, tentative, guess, rhs), 10**6, 2**20, [HBM] * 5, room=62,
     )
-    even, odd = exchange((even, odd), "bx")
+    odd, even = exchange((odd, even), "bx")
     half = [wide(256, 256), shaped(256, 512), shaped(2, 256, 256)]
     halves_scratch = [pltpu.VMEM((256, 1024), BF16), GHOST[1], pltpu.VMEM((5, 1024, 256), BF16)]
     w, inverse, coefficients, t16, plus_y, minus_y, local, column0, columns0 = call(
@@ -701,26 +725,26 @@
         STAGES + halves_scratch,
         (labels, side_labels, blocks, faces, tentative, bounds.reshape(1, 2)), 4 * 10**9, 2**22, [SMEM] * 2 + [VMEM] * 4,
     )
-    even, odd, x_low, x_high = call(
+    odd, even, x_low, x_high = call(
         pack_y_kernel, [shaped(16, YLEN)] * 2 + [shaped(16, XLEN)] * 2, [],
-        (blocks, faces, tentative, traces_packed, b_packed, diagonal, even, odd, column0), 10**8, 2**20,
+        (blocks, faces, tentative, traces_packed, b_packed, diagonal, odd, even, column0), 10**8, 2**20,
         [VMEM] * 8 + [ANY],
     )
-    even, odd = exchange((even, odd), "by")
+    odd, even = exchange((odd, even), "by")
     extended = [wide(SPAN, 128)] * 2 + [wide(EXT, 128)]
     fields = [pltpu.VMEM(a.shape, F32) for a in extended]
     pads = [pltpu.VMEM((8 * EXT, 128), F32)] * 2
-    local, columns1, wx, traces, residue, inverses, ghost = call(
-        y_wait_kernel, [half[0], half[2], shaped(2048, 128)] + extended + [wide(4, 256, 256)],
+    local, columns1, wx, mask_rows, traces, residue, inverses, ghost = call(
+        y_wait_kernel, [half[0], half[2], shaped(2048, 128), shaped(128, 256)] + extended + [wide(4, 256, 256)],
         STAGES + pads + GHOST + [pltpu.VMEM((256, 512), BF16), halves_scratch[0], halves_scratch[2]],
         (labels, side_labels, t16, plus_y, minus_y, w, local, column0, x_low, x_high, guess, b, inverse), 4 * 10**9, 2**22,
-        [SMEM] * 2 + [VMEM] * 11, [VMEM] * 6 + [HBM],
+        [SMEM] * 2 + [VMEM] * 11, [VMEM] * 7 + [HBM],
     )
     smoothed, ghost = call(
         finish_kernel, [wide(NRHS, NE, 64), wide(4, 256, 256)],
-        [pltpu.VMEM((2048, 128), BF16)] + [pltpu.VMEM((16, YLEN), BF16)] * 2 + STAGES + fields + pads + GHOST,
-        (side_labels, guess, w, wx, coefficients, even, odd, columns0, columns1, traces, residue, inverses, ghost),
-        10**9, 2**20, [SMEM] + [VMEM] * 11 + [HBM], [VMEM, HBM], {12: 1},
+        [pltpu.VMEM((2048, 128), BF16)] + [pltpu.VMEM((16, YLEN), BF16)] * 2 + STAGES + fields + pads + GHOST[:1] + GHOST[2:],
+        (mask_rows, guess, w, wx, coefficients, odd, even, columns0, columns1, traces, residue, inverses, ghost),
+        10**9, 2**20, [VMEM] * 12 + [HBM], [VMEM, HBM], {12: 1},
     )
     return jnp.swapaxes(smoothed, 1, 2)[None, None], local[None, None], ghost[None, None]
 

time: 35.6 us -> 34.9 us (0.980)
  the two profiles are of different devices: /device:TPU:281 before, /device:TPU:359 now
where the time goes in v7:
time: 34.9 us; the launch traced here: 34.7 us
  Pallas kernels  15.7 us (45%)
  starting transfers between devices  13.5 us (39%)
  waiting for transfers between devices  3.99 us (11%)
  between operations  0.83 us (2%)
  local copies, waits for them, and re-layouts  0.67 us (2%)
    pallas_call x5, Pallas kernels, call(): pl.pallas_call(kernel, out_shape=outs, in_specs=in_specs or [VMEM] * len(...  15.7 us
    ppermute x4, starting transfers between devices, exchange(): out.append(lax.ppermute(message, axis, pairs))  13.5 us
    ppermute x4, waiting for transfers between devices, exchange(): out.append(lax.ppermute(message, axis, pairs))  3.99 us
  transfers between devices with their start and end apart: 4, of which 1 were waited for; matrix products, arithmetic and copies ran while one was open for 0% of the time, Pallas kernels for 24%

profile of v7, /device:TPU:359, one launch (start us, length us, event | category | flops | bytes accessed | tf_op | source)
XLA Modules:
  0.0 34.7 jit_solution(10818405525427518656)
XLA Ops:
  0.6 0.0 copy-start
  0.6 0.0 copy-start.1
  0.7 0.0 copy-start.2
  0.7 2.8 %shard_map.104 = (bf16[16,5120]{1,0:T(8,128)(2,1)}, bf16[16,5120]{1,0:T(8,128)(2,1)}, bf16[32,768]{1,0:T(8,128)(2,1)}, bf16[32,768]{1,0:T(8,128)(2,1)}, f32[192,64]{1,0:T(8,128)}, /*index=5*/bf16[32,128]{1,0:T(8,128)(2,1)}) custom-call(bf16[32,4096]{1,0:T(8,128)(2,1)} %bitcast.17, bf16[32,4096]{1,0:T(8,128)(2,1)} %bitcast.20, bf16[32,4096]{1,0:T(8,128)(2,1)} %bitcast.23, ...), custom_call_target="tpu_custom_call" | custom-call | flops 1000000 | bytes 1048576 | tf_op jit(solution)/shard_map/pallas_call | solution.py:667
  3.5 2.9 %collective-permute-start = (bf16[16,5120]{1,0:T(8,128)(2,1)}, bf16[16,5120]{1,0:T(8,128)(2,1)S(1)}, u32[]{:S(2)}, u32[]{:S(2)}) collective-permute-start(bf16[16,5120]{1,0:T(8,128)(2,1)} %get-tuple-element.41), channel_id=1, source_target_pairs={{16,32},{32,16},{48,64},{64,48},{80,96},{96,80},{112,128},{128,112... | collective-permute-start | bytes 491528 | tf_op jit(solution)/shard_map/ppermute | solution.py:685
  6.4 2.8 %collective-permute-start.1 = (bf16[16,5120]{1,0:T(8,128)(2,1)}, bf16[16,5120]{1,0:T(8,128)(2,1)S(1)}, u32[]{:S(2)}, u32[]{:S(2)}) collective-permute-start(bf16[16,5120]{1,0:T(8,128)(2,1)} %get-tuple-element.42), channel_id=1, source_target_pairs={{0,16},{16,0},{32,48},{48,32},{64,80},{80,64},{96,112},{112,96},{1... | collective-permute-start | bytes 491528 | tf_op jit(solution)/shard_map/ppermute | solution.py:685
  9.3 0.0 copy-start.8
  9.3 0.0 copy-start.9
  9.3 0.0 copy-start.10
  9.3 0.0 copy-done
  9.3 0.0 copy-done.1
  9.3 0.0 copy-done.2
  9.3 0.6 %copy-done.8 = f32[2]{0:T(128)S(1)} copy-done((f32[2]{0:T(128)S(1)}, f32[2]{0:T(128)}, u32[]{:S(2)}) %copy-start.8) | copy-done | bytes 32
  9.9 0.0 copy-done.9
  9.9 0.0 copy-done.10
  9.9 0.0 copy-start.4
  9.9 0.0 copy-start.5
  9.9 0.0 copy-start.6
  10.0 3.4 %shard_map.103 = (bf16[2048,128]{1,0:T(8,128)(2,1)S(1)}, f32[32,64]{1,0:T(8,128)S(1)}, f32[8,128]{1,0:T(8,128)S(1)}, bf16[2048,128]{1,0:T(8,128)(2,1)S(1)}, bf16...) custom-call(s32[32]{0:T(128)S(1)} %bitcast.30, ...), custom_call_target="tpu_custom_call" | custom-call | flops 4000000000 | bytes 4194304 | tf_op jit(solution)/shard_map/pallas_call | solution.py:667
  13.4 0.0 collective-permute-done.x_odd
  13.4 4.0 %collective-permute-done.1.x_even = bf16[16,5120]{1,0:T(8,128)(2,1)S(1)} collective-permute-done((bf16[16,5120]{1,0:T(8,128)(2,1)}, bf16[16,5120]{1,0:T(8,128)(2,1)S(1)}, u32[]{:S(2)}, u32[]{:S(2)}) %collective-permute-start.1) | collective-permute-done | bytes 163872 | tf_op jit(solution)/shard_map/ppermute | solution.py:685
  17.4 0.0 copy-done.4
  17.4 0.0 copy-done.5
  17.4 0.0 copy-done.6
  17.4 0.0 copy-start.3
  17.4 0.0 copy-start.7
  17.4 0.4 %shard_map.105 = (bf16[16,6144]{1,0:T(8,128)(2,1)S(1)}, bf16[16,6144]{1,0:T(8,128)(2,1)S(1)}, bf16[16,5120]{1,0:T(8,128)(2,1)S(1)}, bf16[16,5120]{1,0:T(8,128)(2,1)S(1)}) custom-call(bf16[32,4096]{1,0:T(8,128)(2,1)S(1)} %bitcast.19, bf16[32,4096]{1,0:T(8,128)(2,1)S(1)} %bitcast.22, bf16[32,4096]{1,0:T(8,128)(2,1)S(1)} %bitcast.25, ...), custom_call_target="tpu_custom_call" | custom-call | flops 100000000 | bytes 1048576 | tf_op jit(solution)/shard_map/pallas_call | solution.py:667
  17.8 3.6 %collective-permute-start.2 = (bf16[16,6144]{1,0:T(8,128)(2,1)S(1)}, bf16[16,6144]{1,0:T(8,128)(2,1)S(1)}, u32[]{:S(2)}, u32[]{:S(2)}) collective-permute-start(bf16[16,6144]{1,0:T(8,128)(2,1)S(1)} %get-tuple-element.50), channel_id=1, source_target_pairs={{1,2},{2,1},{3,4},{4,3},{5,6},{6,5},{7,8},{8,7},{9,10},{10,9},{11,... | collective-permute-start | bytes 589832 | tf_op jit(solution)/shard_map/ppermute | solution.py:685
  21.4 4.2 %collective-permute-start.3 = (bf16[16,6144]{1,0:T(8,128)(2,1)S(1)}, bf16[16,6144]{1,0:T(8,128)(2,1)S(1)}, u32[]{:S(2)}, u32[]{:S(2)}) collective-permute-start(bf16[16,6144]{1,0:T(8,128)(2,1)S(1)} %get-tuple-element.51), channel_id=1, source_target_pairs={{0,1},{1,0},{2,3},{3,2},{4,5},{5,4},{6,7},{7,6},{8,9},{9,8},{10,11... | collective-permute-start | bytes 589832 | tf_op jit(solution)/shard_map/ppermute | solution.py:685
  25.6 0.0 copy-done.3
  25.6 0.0 copy-done.7
  25.6 4.8 %shard_map.106 = (f32[256,256]{1,0:T(8,128)}, bf16[2,256,256]{2,1,0:T(8,128)(2,1)S(1)}, bf16[2048,128]{1,0:T(8,128)(2,1)S(1)}, bf16[128,256]{1,0:T(8,128)(2,1)S(...) custom-call(s32[32]{0:T(128)S(1)} %bitcast.31, ...), custom_call_target="tpu_custom_call" | custom-call | flops 4000000000 | bytes 4194304 | tf_op jit(solution)/shard_map/pallas_call | solution.py:667
  30.4 0.0 collective-permute-done.2.y_odd
  30.4 0.0 collective-permute-done.3.y_even
  30.4 4.3 %shard_map.107 = (f32[6,32,64]{2,1,0:T(8,128)}, f32[4,256,256]{2,1,0:T(8,128)}) custom-call(bf16[128,256]{1,0:T(8,128)(2,1)S(1)} %get-tuple-element.47.mask_rows, f32[6,32,64]{2,1,0:T(8,128)S(1)} %bitcast.28, bf16[2048,128]{1,0:T(8,128)(2,1)S(1)} %get-tuple-element.35.w, ...), custom_call_target="tpu_custom_call", output_to_operand_aliasing={{1}: (12, {})} | custom-call | flops 1000000000 | bytes 1048576 | tf_op jit(solution)/shard_map/pallas_call | solution.py:667
Async XLA Ops:
  0.6 8.7 %copy-start = (bf16[1,1,32,4096]{3,2,1,0:T(8,128)(2,1)S(1)}, bf16[1,1,32,4096]{3,2,1,0:T(8,128)(2,1)}, u32[]{:S(2)}) copy-start(bf16[1,1,32,4096]{3,2,1,0:T(8,128)(2,1)} %param.8) | copy-start | bytes 786436
  0.6 8.7 %copy-start.1 = (bf16[1,1,32,4096]{3,2,1,0:T(8,128)(2,1)S(1)}, bf16[1,1,32,4096]{3,2,1,0:T(8,128)(2,1)}, u32[]{:S(2)}) copy-start(bf16[1,1,32,4096]{3,2,1,0:T(8,128)(2,1)} %param.9) | copy-start | bytes 786436
  0.7 8.7 %copy-start.2 = (bf16[1,1,32,4096]{3,2,1,0:T(8,128)(2,1)S(1)}, bf16[1,1,32,4096]{3,2,1,0:T(8,128)(2,1)}, u32[]{:S(2)}) copy-start(bf16[1,1,32,4096]{3,2,1,0:T(8,128)(2,1)} %param.10) | copy-start | bytes 786436
  3.5 9.9 %collective-permute-start = (bf16[16,5120]{1,0:T(8,128)(2,1)}, bf16[16,5120]{1,0:T(8,128)(2,1)S(1)}, u32[]{:S(2)}, u32[]{:S(2)}) collective-permute-start(bf16[16,5120]{1,0:T(8,128)(2,1)} %get-tuple-element.41), channel_id=1, source_target_pairs={{16,32},{32,16},{48,64},{64,48},{80,96},{96,80},{112,128},{128,112... | collective-permute-start | bytes 491528 | tf_op jit(solution)/shard_map/ppermute | solution.py:685
  6.4 10.9 %collective-permute-start.1 = (bf16[16,5120]{1,0:T(8,128)(2,1)}, bf16[16,5120]{1,0:T(8,128)(2,1)S(1)}, u32[]{:S(2)}, u32[]{:S(2)}) collective-permute-start(bf16[16,5120]{1,0:T(8,128)(2,1)} %get-tuple-element.42), channel_id=1, source_target_pairs={{0,16},{16,0},{32,48},{48,32},{64,80},{80,64},{96,112},{112,96},{1... | collective-permute-start | bytes 491528 | tf_op jit(solution)/shard_map/ppermute | solution.py:685
  9.3 0.7 %copy-start.8 = (f32[2]{0:T(128)S(1)}, f32[2]{0:T(128)}, u32[]{:S(2)}) copy-start(f32[2]{0:T(128)} %param.15) | copy-start | bytes 28
  9.3 0.7 %copy-start.9 = (s32[1,1,32]{2,1,0:T(1,128)S(1)}, s32[1,1,32]{2,1,0:T(1,128)}, u32[]{:S(2)}) copy-start(s32[1,1,32]{2,1,0:T(1,128)} %param.11) | copy-start | bytes 388
  9.3 0.7 %copy-start.10 = (s32[1,1,24]{2,1,0:T(1,128)S(1)}, s32[1,1,24]{2,1,0:T(1,128)}, u32[]{:S(2)}) copy-start(s32[1,1,24]{2,1,0:T(1,128)} %param.12) | copy-start | bytes 292
  9.9 7.4 %copy-start.4 = (bf16[32,768]{1,0:T(8,128)(2,1)S(1)}, bf16[32,768]{1,0:T(8,128)(2,1)}, u32[]{:S(2)}) copy-start(bf16[32,768]{1,0:T(8,128)(2,1)} %get-tuple-element.38.traces_packed) | copy-start | bytes 147460
  9.9 7.4 %copy-start.5 = (bf16[32,768]{1,0:T(8,128)(2,1)S(1)}, bf16[32,768]{1,0:T(8,128)(2,1)}, u32[]{:S(2)}) copy-start(bf16[32,768]{1,0:T(8,128)(2,1)} %get-tuple-element.39.b_packed) | copy-start | bytes 147460
  9.9 7.4 %copy-start.6 = (bf16[32,128]{1,0:T(8,128)(2,1)S(1)}, bf16[32,128]{1,0:T(8,128)(2,1)}, u32[]{:S(2)}) copy-start(bf16[32,128]{1,0:T(8,128)(2,1)} %get-tuple-element.40.diagonal) | copy-start | bytes 24580
  17.4 8.2 %copy-start.3 = (f32[1,1,6,64,32]{3,4,2,1,0:T(8,128)S(1)}, f32[1,1,6,64,32]{3,4,2,1,0:T(8,128)}, u32[]{:S(2)}) copy-start(f32[1,1,6,64,32]{3,4,2,1,0:T(8,128)} %param.14) | copy-start | bytes 147460
  17.4 8.2 %copy-start.7 = (f32[192,64]{1,0:T(8,128)S(1)}, f32[192,64]{1,0:T(8,128)}, u32[]{:S(2)}) copy-start(f32[192,64]{1,0:T(8,128)} %get-tuple-element.45.b) | copy-start | bytes 147460
  17.8 12.6 %collective-permute-start.2 = (bf16[16,6144]{1,0:T(8,128)(2,1)S(1)}, bf16[16,6144]{1,0:T(8,128)(2,1)S(1)}, u32[]{:S(2)}, u32[]{:S(2)}) collective-permute-start(bf16[16,6144]{1,0:T(8,128)(2,1)S(1)} %get-tuple-element.50), channel_id=1, source_target_pairs={{1,2},{2,1},{3,4},{4,3},{5,6},{6,5},{7,8},{8,7},{9,10},{10,9},{11,... | collective-permute-start | bytes 589832 | tf_op jit(solution)/shard_map/ppermute | solution.py:685
  21.4 9.0 %collective-permute-start.3 = (bf16[16,6144]{1,0:T(8,128)(2,1)S(1)}, bf16[16,6144]{1,0:T(8,128)(2,1)S(1)}, u32[]{:S(2)}, u32[]{:S(2)}) collective-permute-start(bf16[16,6144]{1,0:T(8,128)(2,1)S(1)} %get-tuple-element.51), channel_id=1, source_target_pairs={{0,1},{1,0},{2,3},{3,2},{4,5},{5,4},{6,7},{7,6},{8,9},{9,8},{10,11... | collective-permute-start | bytes 589832 | tf_op jit(solution)/shard_map/ppermute | solution.py:685

commit v8 on v7

--- a/solution.py
+++ b/solution.py
@@ -119,7 +119,7 @@
 TRACE_OFFSET, VALUE_OFFSET = (16, 0), (0, 48)
 
 
-def pack_x_kernel(blocks_in, faces_in, tent_in, guess_in, rhs_in, odd, even, traces_packed, b_packed, b_out, diagonal,
+def pack_x_kernel(blocks_in, faces_in, tent_in, guess_in, rhs_in, even, odd, traces_packed, b_packed, b_out, diagonal,
                   blocks, faces, tent, guess, rhs, stage, w32, w16, x_ref, a_ref, sems):
     copies = [
         pltpu.make_async_copy(source, target, sems.at[i])
@@ -189,7 +189,7 @@
     put(XE, 128, lambda s: over(packed(diag, 0, s), packed(diag, 1, s)))
 
 
-def pack_y_kernel(blocks, faces, tent, traces_packed, b_packed, diagonal, x_odd, x_even, _, odd, even, low, high):
+def pack_y_kernel(blocks, faces, tent, traces_packed, b_packed, diagonal, x_even, x_odd, _, odd, even, low, high):
     first = parity("bx") == 0
     for start in range(0, XLEN, 128):
         a = x_even[:, start : start + 128].astype(F32)
@@ -551,11 +551,16 @@
     return jnp.concatenate([none(64 + 16 * f), rows] + ([none(48 - 16 * f)] if f < 3 else []), 0)
 
 
-def galerkin(half, before_local, labels, t16, plus_y, minus_y, w, local, edge_column, edge_columns, tt, masks, big):
+ROWS_EARLY = 3
+
+
+def galerkin(late, before_local, labels, t16, plus_y, minus_y, w, local, edge_column, edge_columns, tt, masks, big):
+    first_row, last_row = (ROWS_EARLY, EX) if late else (0, ROWS_EARLY)
+    rows = last_row - first_row
     label_masks(masks)
     lane128 = iota((64, 128), 1)
-    for pair in range(8):
-        e = 16 * half + 2 * pair
+    for pair in range(4 * rows):
+        e = 8 * first_row + 2 * pair
         turned = t16[e * 64 : e * 64 + 128, :].astype(F32).T[:64]
         first, second = labels[e], labels[e + 1]
         for a in range(4):
@@ -565,9 +570,9 @@
                 jnp.where(second == a, 1.0, 0.0),
             )
             tt[a * 64 : a * 64 + 64, pair * 128 : pair * 128 + 128] = (turned * keep).astype(BF16)
-    edge_column[...] = tt[:, 512 * half : 512 * half + 512]
+    edge_column[...] = tt[:, 512 * rows - 512 :] if late else tt[:, :512]
     for f in range(2):
-        for i in range(2):
+        for i in range(rows):
             start = (4 * i + 3 * f) * 128
             edge_columns[f, :, i * 128 : i * 128 + 128] = tt[:, start : start + 128]
 
@@ -575,7 +580,7 @@
         for iy in range(EY):
             e = ix * EY + iy
             own = pl.ds(pl.multiple_of(e * 64, 64), 64)
-            here = pl.ds(pl.multiple_of((e - 16 * half) * 64, 64), 64)
+            here = pl.ds(pl.multiple_of((e - 8 * first_row) * 64, 64), 64)
             before = pl.multiple_of(jnp.maximum(e - 8, 0) * 64, 64)
             after = pl.multiple_of(jnp.minimum(e + 8, 31) * 64, 64)
             rows = [
@@ -600,12 +605,16 @@
             big[4, here, :] = masked(masks, piece(4), labels[e + 1]) if iy < 7 else nothing
         return carry
 
-    lax.fori_loop(2 * half, 2 * half + 2, row_of_elements, 0)
+    lax.fori_loop(first_row, last_row, row_of_elements, 0)
     total = dot(tt[...], big[0]) + dot(tt[...], big[3]) + dot(tt[...], big[4])
-    if half:
-        total = before_local[...] + total + dot(tt[...], big[1]) + dot(tt[:, :512], big[2, :512, :])
+    if late:
+        total = before_local[...] + total + dot(tt[...], big[1])
+        if rows > 1:
+            total = total + dot(tt[:, : 512 * rows - 512], big[2, : 512 * rows - 512, :])
     else:
-        total = total + dot(tt[:, 512:], big[1, 512:, :]) + dot(tt[...], big[2])
+        total = total + dot(tt[...], big[2])
+        if rows > 1:
+            total = total + dot(tt[:, 512:], big[1, 512:, :])
     local[...] = total
 
 
@@ -615,8 +624,12 @@
         near = rows[(i + first_row) * 16 : (i + first_row) * 16 + 16, :].astype(BF16)
         piece = dot(w[e * 64 : e * 64 + 64, :], face_column(face, near)).astype(BF16)
         side[place : place + 64, :] = times(piece, mask(i))
-    width = 512 // len(columns)
-    result[...] = sum(dot(c[...], side[i * width : (i + 1) * width, :]) for i, c in enumerate(columns))
+    total, start = 0.0, 0
+    for c in columns:
+        width = c.shape[-1]
+        total = total + dot(c[...], side[start : start + width, :])
+        start += width
+    result[...] = total
 
 
 def x_wait_kernel(labels, _, blocks, faces, tent, bounds, w, inverse, coefficients, t16, plus_y, minus_y, local, column, columns,
@@ -676,9 +689,9 @@
     )(*operands)
 
 
-def exchange(messages, axis):
+def exchange(messages, axis, firsts):
     out = []
-    for first, message in zip((1, 0), messages):
+    for first, message in zip(firsts, messages):
         pairs = []
         for i in range(first, lax.axis_size(axis) - 1, 2):
             pairs += [(i, i + 1), (i + 1, i)]
@@ -708,7 +721,7 @@
     guess = jnp.swapaxes(guess[0, 0], 1, 2)
     labels, side_labels = aggregate.reshape(NE), ghost_labels.reshape(24)
     blocks, faces, tentative = [a.reshape(NE, 4096) for a in (blocks, faces, tentative)]
-    odd, even, traces_packed, b_packed, b, diagonal = call(
+    even, odd, traces_packed, b_packed, b, diagonal = call(
         pack_x_kernel,
         [shaped(16, XLEN)] * 2 + [shaped(NE, 768)] * 2 + [wide(NRHS * NE, 64), shaped(NE, 128)],
         [pltpu.VMEM((NE, 4096), BF16)] * 3 + [pltpu.VMEM((NRHS, NE, 64), F32)] * 2
@@ -716,27 +729,31 @@
         + [pltpu.SemaphoreType.DMA((5,))],
         (blocks, faces, tentative, guess, rhs), 10**6, 2**20, [HBM] * 5, room=62,
     )
-    odd, even = exchange((odd, even), "bx")
-    half = [wide(256, 256), shaped(256, 512), shaped(2, 256, 256)]
-    halves_scratch = [pltpu.VMEM((256, 1024), BF16), GHOST[1], pltpu.VMEM((5, 1024, 256), BF16)]
+    even, odd = exchange((even, odd), "bx", (0, 1))
+    def part_of(rows):
+        outs = [wide(256, 256), shaped(256, 512), shaped(2, 256, 128 * rows)]
+        return outs, [pltpu.VMEM((256, 512 * rows), BF16), GHOST[1], pltpu.VMEM((5, 512 * rows, 256), BF16)]
+
+    early, early_scratch = part_of(ROWS_EARLY)
+    late, late_scratch = part_of(EX - ROWS_EARLY)
     w, inverse, coefficients, t16, plus_y, minus_y, local, column0, columns0 = call(
         x_wait_kernel,
-        [shaped(2048, 128), wide(NE, 64), wide(8, 128), shaped(2048, 128), shaped(512, 128), shaped(512, 128)] + half,
-        STAGES + halves_scratch,
+        [shaped(2048, 128), wide(NE, 64), wide(8, 128), shaped(2048, 128), shaped(512, 128), shaped(512, 128)] + early,
+        STAGES + early_scratch,
         (labels, side_labels, blocks, faces, tentative, bounds.reshape(1, 2)), 4 * 10**9, 2**22, [SMEM] * 2 + [VMEM] * 4,
     )
     odd, even, x_low, x_high = call(
         pack_y_kernel, [shaped(16, YLEN)] * 2 + [shaped(16, XLEN)] * 2, [],
-        (blocks, faces, tentative, traces_packed, b_packed, diagonal, odd, even, column0), 10**8, 2**20,
+        (blocks, faces, tentative, traces_packed, b_packed, diagonal, even, odd, column0), 10**8, 2**20,
         [VMEM] * 8 + [ANY],
     )
-    odd, even = exchange((odd, even), "by")
+    odd, even = exchange((odd, even), "by", (1, 0))
     extended = [wide(SPAN, 128)] * 2 + [wide(EXT, 128)]
     fields = [pltpu.VMEM(a.shape, F32) for a in extended]
     pads = [pltpu.VMEM((8 * EXT, 128), F32)] * 2
     local, columns1, wx, mask_rows, traces, residue, inverses, ghost = call(
-        y_wait_kernel, [half[0], half[2], shaped(2048, 128), shaped(128, 256)] + extended + [wide(4, 256, 256)],
-        STAGES + pads + GHOST + [pltpu.VMEM((256, 512), BF16), halves_scratch[0], halves_scratch[2]],
+        y_wait_kernel, [late[0], late[2], shaped(2048, 128), shaped(128, 256)] + extended + [wide(4, 256, 256)],
+        STAGES + pads + GHOST + [pltpu.VMEM((256, 512), BF16), late_scratch[0], late_scratch[2]],
         (labels, side_labels, t16, plus_y, minus_y, w, local, column0, x_low, x_high, guess, b, inverse), 4 * 10**9, 2**22,
         [SMEM] * 2 + [VMEM] * 11, [VMEM] * 7 + [HBM],
     )

time: 34.9 us -> 32.7 us (0.937)
  the two profiles are of different devices: /device:TPU:359 before, /device:TPU:102 now
where the time goes in v8:
time: 32.7 us; the launch traced here: 32.2 us
  Pallas kernels  15.3 us (47%)
  starting transfers between devices  15 us (46%)
  between operations  0.84 us (3%)
  local copies, waits for them, and re-layouts  0.67 us (2%)
  waiting for transfers between devices  0.49 us (1%)
    pallas_call x5, Pallas kernels, call(): pl.pallas_call(kernel, out_shape=outs, in_specs=in_specs or [VMEM] * len(...  15.3 us
    ppermute x4, starting transfers between devices, exchange(): out.append(lax.ppermute(message, axis, pairs))  15 us
    unnamed x22, local copies, waits for them, and re-layouts  0.67 us
  transfers between devices with their start and end apart: 4, of which 1 were waited for; matrix products, arithmetic and copies ran while one was open for 0% of the time, Pallas kernels for 24%

profile of v8, /device:TPU:102, one launch (start us, length us, event | category | flops | bytes accessed | tf_op | source)
XLA Modules:
  0.0 32.2 jit_solution(8194547964994044243)
XLA Ops:
  0.6 0.0 copy-start
  0.6 0.0 copy-start.1
  0.7 0.0 copy-start.2
  0.7 2.8 %shard_map.104 = (bf16[16,5120]{1,0:T(8,128)(2,1)}, bf16[16,5120]{1,0:T(8,128)(2,1)}, bf16[32,768]{1,0:T(8,128)(2,1)}, bf16[32,768]{1,0:T(8,128)(2,1)}, f32[192,64]{1,0:T(8,128)}, /*index=5*/bf16[32,128]{1,0:T(8,128)(2,1)}) custom-call(bf16[32,4096]{1,0:T(8,128)(2,1)} %bitcast.17, bf16[32,4096]{1,0:T(8,128)(2,1)} %bitcast.20, bf16[32,4096]{1,0:T(8,128)(2,1)} %bitcast.23, ...), custom_call_target="tpu_custom_call" | custom-call | flops 1000000 | bytes 1048576 | tf_op jit(solution)/shard_map/pallas_call | solution.py:680
  3.5 2.7 %collective-permute-start = (bf16[16,5120]{1,0:T(8,128)(2,1)}, bf16[16,5120]{1,0:T(8,128)(2,1)S(1)}, u32[]{:S(2)}, u32[]{:S(2)}) collective-permute-start(bf16[16,5120]{1,0:T(8,128)(2,1)} %get-tuple-element.41), channel_id=1, source_target_pairs={{0,16},{16,0},{32,48},{48,32},{64,80},{80,64},{96,112},{112,96},{1... | collective-permute-start | bytes 491528 | tf_op jit(solution)/shard_map/ppermute | solution.py:698
  6.3 5.7 %collective-permute-start.1 = (bf16[16,5120]{1,0:T(8,128)(2,1)}, bf16[16,5120]{1,0:T(8,128)(2,1)S(1)}, u32[]{:S(2)}, u32[]{:S(2)}) collective-permute-start(bf16[16,5120]{1,0:T(8,128)(2,1)} %get-tuple-element.42), channel_id=1, source_target_pairs={{16,32},{32,16},{48,64},{64,48},{80,96},{96,80},{112,128},{128,112... | collective-permute-start | bytes 491528 | tf_op jit(solution)/shard_map/ppermute | solution.py:698
  11.9 0.0 copy-start.8
  11.9 0.0 copy-start.9
  12.0 0.0 copy-start.10
  12.0 0.0 copy-done
  12.0 0.0 copy-done.1
  12.0 0.0 copy-done.2
  12.0 0.6 %copy-done.8 = f32[2]{0:T(128)S(1)} copy-done((f32[2]{0:T(128)S(1)}, f32[2]{0:T(128)}, u32[]{:S(2)}) %copy-start.8) | copy-done | bytes 32
  12.6 0.0 copy-done.9
  12.6 0.0 copy-done.10
  12.6 0.0 copy-start.4
  12.6 0.0 copy-start.5
  12.6 0.0 copy-start.6
  12.6 4.2 %shard_map.103 = (bf16[2048,128]{1,0:T(8,128)(2,1)S(1)}, f32[32,64]{1,0:T(8,128)S(1)}, f32[8,128]{1,0:T(8,128)S(1)}, bf16[2048,128]{1,0:T(8,128)(2,1)S(1)}, bf16...) custom-call(s32[32]{0:T(128)S(1)} %bitcast.30, ...), custom_call_target="tpu_custom_call" | custom-call | flops 4000000000 | bytes 4194304 | tf_op jit(solution)/shard_map/pallas_call | solution.py:680
  16.8 0.0 collective-permute-done.x_even
  16.8 0.0 collective-permute-done.1.x_odd
  16.8 0.0 copy-done.4
  16.9 0.0 copy-done.5
  16.9 0.0 copy-done.6
  16.9 0.0 copy-start.3
  16.9 0.0 copy-start.7
  16.9 0.4 %shard_map.105 = (bf16[16,6144]{1,0:T(8,128)(2,1)S(1)}, bf16[16,6144]{1,0:T(8,128)(2,1)S(1)}, bf16[16,5120]{1,0:T(8,128)(2,1)S(1)}, bf16[16,5120]{1,0:T(8,128)(2,1)S(1)}) custom-call(bf16[32,4096]{1,0:T(8,128)(2,1)S(1)} %bitcast.19, bf16[32,4096]{1,0:T(8,128)(2,1)S(1)} %bitcast.22, bf16[32,4096]{1,0:T(8,128)(2,1)S(1)} %bitcast.25, ...), custom_call_target="tpu_custom_call" | custom-call | flops 100000000 | bytes 1048576 | tf_op jit(solution)/shard_map/pallas_call | solution.py:680
  17.3 4.6 %collective-permute-start.2 = (bf16[16,6144]{1,0:T(8,128)(2,1)S(1)}, bf16[16,6144]{1,0:T(8,128)(2,1)S(1)}, u32[]{:S(2)}, u32[]{:S(2)}) collective-permute-start(bf16[16,6144]{1,0:T(8,128)(2,1)S(1)} %get-tuple-element.50), channel_id=1, source_target_pairs={{1,2},{2,1},{3,4},{4,3},{5,6},{6,5},{7,8},{8,7},{9,10},{10,9},{11,... | collective-permute-start | bytes 589832 | tf_op jit(solution)/shard_map/ppermute | solution.py:698
  22.0 1.9 %collective-permute-start.3 = (bf16[16,6144]{1,0:T(8,128)(2,1)S(1)}, bf16[16,6144]{1,0:T(8,128)(2,1)S(1)}, u32[]{:S(2)}, u32[]{:S(2)}) collective-permute-start(bf16[16,6144]{1,0:T(8,128)(2,1)S(1)} %get-tuple-element.51), channel_id=1, source_target_pairs={{0,1},{1,0},{2,3},{3,2},{4,5},{5,4},{6,7},{7,6},{8,9},{9,8},{10,11... | collective-permute-start | bytes 589832 | tf_op jit(solution)/shard_map/ppermute | solution.py:698
  23.9 0.0 copy-done.3
  23.9 0.0 copy-done.7
  23.9 3.5 %shard_map.106 = (f32[256,256]{1,0:T(8,128)}, bf16[2,256,128]{2,1,0:T(8,128)(2,1)S(1)}, bf16[2048,128]{1,0:T(8,128)(2,1)S(1)}, bf16[128,256]{1,0:T(8,128)(2,1)S(...) custom-call(s32[32]{0:T(128)S(1)} %bitcast.31, ...), custom_call_target="tpu_custom_call" | custom-call | flops 4000000000 | bytes 4194304 | tf_op jit(solution)/shard_map/pallas_call | solution.py:680
  27.4 0.5 %collective-permute-done.2.y_odd = bf16[16,6144]{1,0:T(8,128)(2,1)S(1)} collective-permute-done((bf16[16,6144]{1,0:T(8,128)(2,1)S(1)}, bf16[16,6144]{1,0:T(8,128)(2,1)S(1)}, u32[]{:S(2)}, u32[]{:S(2)}) %collective-permute-start.2) | collective-permute-done | bytes 196640 | tf_op jit(solution)/shard_map/ppermute | solution.py:698
  27.9 0.0 collective-permute-done.3.y_even
  27.9 4.3 %shard_map.107 = (f32[6,32,64]{2,1,0:T(8,128)}, f32[4,256,256]{2,1,0:T(8,128)}) custom-call(bf16[128,256]{1,0:T(8,128)(2,1)S(1)} %get-tuple-element.47.mask_rows, f32[6,32,64]{2,1,0:T(8,128)S(1)} %bitcast.28, bf16[2048,128]{1,0:T(8,128)(2,1)S(1)} %get-tuple-element.35.w, ...), custom_call_target="tpu_custom_call", output_to_operand_aliasing={{1}: (12, {})} | custom-call | flops 1000000000 | bytes 1048576 | tf_op jit(solution)/shard_map/pallas_call | solution.py:680
Async XLA Ops:
  0.6 11.3 %copy-start = (bf16[1,1,32,4096]{3,2,1,0:T(8,128)(2,1)S(1)}, bf16[1,1,32,4096]{3,2,1,0:T(8,128)(2,1)}, u32[]{:S(2)}) copy-start(bf16[1,1,32,4096]{3,2,1,0:T(8,128)(2,1)} %param.8) | copy-start | bytes 786436
  0.6 11.3 %copy-start.1 = (bf16[1,1,32,4096]{3,2,1,0:T(8,128)(2,1)S(1)}, bf16[1,1,32,4096]{3,2,1,0:T(8,128)(2,1)}, u32[]{:S(2)}) copy-start(bf16[1,1,32,4096]{3,2,1,0:T(8,128)(2,1)} %param.9) | copy-start | bytes 786436
  0.7 11.3 %copy-start.2 = (bf16[1,1,32,4096]{3,2,1,0:T(8,128)(2,1)S(1)}, bf16[1,1,32,4096]{3,2,1,0:T(8,128)(2,1)}, u32[]{:S(2)}) copy-start(bf16[1,1,32,4096]{3,2,1,0:T(8,128)(2,1)} %param.10) | copy-start | bytes 786436
  3.5 13.3 %collective-permute-start = (bf16[16,5120]{1,0:T(8,128)(2,1)}, bf16[16,5120]{1,0:T(8,128)(2,1)S(1)}, u32[]{:S(2)}, u32[]{:S(2)}) collective-permute-start(bf16[16,5120]{1,0:T(8,128)(2,1)} %get-tuple-element.41), channel_id=1, source_target_pairs={{0,16},{16,0},{32,48},{48,32},{64,80},{80,64},{96,112},{112,96},{1... | collective-permute-start | bytes 491528 | tf_op jit(solution)/shard_map/ppermute | solution.py:698
  6.3 10.6 %collective-permute-start.1 = (bf16[16,5120]{1,0:T(8,128)(2,1)}, bf16[16,5120]{1,0:T(8,128)(2,1)S(1)}, u32[]{:S(2)}, u32[]{:S(2)}) collective-permute-start(bf16[16,5120]{1,0:T(8,128)(2,1)} %get-tuple-element.42), channel_id=1, source_target_pairs={{16,32},{32,16},{48,64},{64,48},{80,96},{96,80},{112,128},{128,112... | collective-permute-start | bytes 491528 | tf_op jit(solution)/shard_map/ppermute | solution.py:698
  11.9 0.7 %copy-start.8 = (f32[2]{0:T(128)S(1)}, f32[2]{0:T(128)}, u32[]{:S(2)}) copy-start(f32[2]{0:T(128)} %param.15) | copy-start | bytes 28
  11.9 0.7 %copy-start.9 = (s32[1,1,32]{2,1,0:T(1,128)S(1)}, s32[1,1,32]{2,1,0:T(1,128)}, u32[]{:S(2)}) copy-start(s32[1,1,32]{2,1,0:T(1,128)} %param.11) | copy-start | bytes 388
  12.0 0.7 %copy-start.10 = (s32[1,1,24]{2,1,0:T(1,128)S(1)}, s32[1,1,24]{2,1,0:T(1,128)}, u32[]{:S(2)}) copy-start(s32[1,1,24]{2,1,0:T(1,128)} %param.12) | copy-start | bytes 292
  12.6 4.2 %copy-start.4 = (bf16[32,768]{1,0:T(8,128)(2,1)S(1)}, bf16[32,768]{1,0:T(8,128)(2,1)}, u32[]{:S(2)}) copy-start(bf16[32,768]{1,0:T(8,128)(2,1)} %get-tuple-element.38.traces_packed) | copy-start | bytes 147460
  12.6 4.2 %copy-start.5 = (bf16[32,768]{1,0:T(8,128)(2,1)S(1)}, bf16[32,768]{1,0:T(8,128)(2,1)}, u32[]{:S(2)}) copy-start(bf16[32,768]{1,0:T(8,128)(2,1)} %get-tuple-element.39.b_packed) | copy-start | bytes 147460
  12.6 4.2 %copy-start.6 = (bf16[32,128]{1,0:T(8,128)(2,1)S(1)}, bf16[32,128]{1,0:T(8,128)(2,1)}, u32[]{:S(2)}) copy-start(bf16[32,128]{1,0:T(8,128)(2,1)} %get-tuple-element.40.diagonal) | copy-start | bytes 24580
  16.9 7.0 %copy-start.3 = (f32[1,1,6,64,32]{3,4,2,1,0:T(8,128)S(1)}, f32[1,1,6,64,32]{3,4,2,1,0:T(8,128)}, u32[]{:S(2)}) copy-start(f32[1,1,6,64,32]{3,4,2,1,0:T(8,128)} %param.14) | copy-start | bytes 147460
  16.9 7.0 %copy-start.7 = (f32[192,64]{1,0:T(8,128)S(1)}, f32[192,64]{1,0:T(8,128)}, u32[]{:S(2)}) copy-start(f32[192,64]{1,0:T(8,128)} %get-tuple-element.45.b) | copy-start | bytes 147460
  17.3 10.6 %collective-permute-start.2 = (bf16[16,6144]{1,0:T(8,128)(2,1)S(1)}, bf16[16,6144]{1,0:T(8,128)(2,1)S(1)}, u32[]{:S(2)}, u32[]{:S(2)}) collective-permute-start(bf16[16,6144]{1,0:T(8,128)(2,1)S(1)} %get-tuple-element.50), channel_id=1, source_target_pairs={{1,2},{2,1},{3,4},{4,3},{5,6},{6,5},{7,8},{8,7},{9,10},{10,9},{11,... | collective-permute-start | bytes 589832 | tf_op jit(solution)/shard_map/ppermute | solution.py:698
  22.0 6.0 %collective-permute-start.3 = (bf16[16,6144]{1,0:T(8,128)(2,1)S(1)}, bf16[16,6144]{1,0:T(8,128)(2,1)S(1)}, u32[]{:S(2)}, u32[]{:S(2)}) collective-permute-start(bf16[16,6144]{1,0:T(8,128)(2,1)S(1)} %get-tuple-element.51), channel_id=1, source_target_pairs={{0,1},{1,0},{2,3},{3,2},{4,5},{5,4},{6,7},{7,6},{8,9},{9,8},{10,11... | collective-permute-start | bytes 589832 | tf_op jit(solution)/shard_map/ppermute | solution.py:698

commit v9 on v8

--- a/solution.py
+++ b/solution.py
@@ -119,12 +119,14 @@
 TRACE_OFFSET, VALUE_OFFSET = (16, 0), (0, 48)
 
 
-def pack_x_kernel(blocks_in, faces_in, tent_in, guess_in, rhs_in, even, odd, traces_packed, b_packed, b_out, diagonal,
-                  blocks, faces, tent, guess, rhs, stage, w32, w16, x_ref, a_ref, sems):
+def pack_x_kernel(blocks_in, faces_in, tent_in, guess_in, rhs_in, bounds_in, labels_in, sides_in,
+                  even, odd, traces_packed, b_packed, b_out, diagonal, labels_out,
+                  blocks, faces, tent, guess, rhs, bounds, labels, sides, stage, w32, w16, x_ref, a_ref, sems):
     copies = [
         pltpu.make_async_copy(source, target, sems.at[i])
         for i, (source, target) in enumerate(
-            ((guess_in, guess), (blocks_in, blocks), (rhs_in, rhs), (faces_in, faces), (tent_in, tent))
+            ((guess_in, guess), (blocks_in, blocks), (rhs_in, rhs), (faces_in, faces), (tent_in, tent),
+             (bounds_in, bounds), (labels_in, labels), (sides_in, sides))
         )
     ]
     for copy in copies:
@@ -154,7 +156,13 @@
     for copy in copies[2:]:
         copy.wait()
     b = rhs[...].reshape(NRHS * NE, 64) - a_ref[0:192, 0:64]
-    b_out[...] = b
+    b_out[0:192, :] = b
+    b_out[192:200, :] = jnp.concatenate(
+        [jnp.broadcast_to(c, (1, 64)) for c in factors(bounds)] + [jnp.zeros((3, 64), F32)], 0
+    )
+    labels_out[...] = jnp.zeros((8, 128), jnp.int32)
+    labels_out[0:1, 0:NE] = labels[...]
+    labels_out[1:2, 0:24] = sides[...]
     r = pack_lanes(b)
     b_packed[...] = r.astype(BF16)
     first = parity("bx") == 0
@@ -319,11 +327,9 @@
     w[...] = w32[...].astype(BF16)
 
 
-def own_operators(blocks, faces, bounds, w, inverse, coefficients, *scratch):
-    coefficients[...] = jnp.concatenate([jnp.broadcast_to(c, (1, 128)) for c in factors(bounds)] + [jnp.zeros((3, 128), F32)], 0)
+def own_operators(blocks, faces, w, *scratch):
     chunk = lambda ref: lambda c: ref[:, c * 128 : (c + 1) * 128].astype(F32)
     operators(chunk(blocks), chunk(faces), w, *scratch)
-    inverse[...] = 1.0 / diagonals(chunk(blocks))[:, :64]
 
 
 NOTHING = (8, 128)
@@ -435,15 +441,16 @@
         a_ref[pl.ds(row, 8, stride=EXT), 0:64] = out[:8] + out[8:]
 
 
-def start_smoothing(guess, b, inverse, w, wx, x_low, x_high, t_ref, r_ref, i_ref, x_ref, a_ref):
+def start_smoothing(guess, b, diagonal, w, wx, x_low, x_high, t_ref, r_ref, i_ref, x_ref, a_ref):
     t_ref[...] = jnp.zeros((SPAN, 128), F32)
     r_ref[...] = jnp.zeros((SPAN, 128), F32)
     i_ref[...] = jnp.ones((EXT, 128), F32)
     a_ref[...] = jnp.zeros((8 * EXT, 128), F32)
     traces = with_traces(guess[...].reshape(NRHS * NE, 64))
+    inverse = 1.0 / diagonal[...].astype(F32)
     for ix in range(EX):
         row = (ix + 3) * 16
-        i_ref[row : row + 8, 0:64] = inverse[ix * 8 : ix * 8 + 8, :]
+        i_ref[row : row + 8, :] = inverse[ix * 8 : ix * 8 + 8]
         for n in range(NRHS):
             source = n * NE + ix * 8
             t_ref[n * EXT + row : n * EXT + row + 8, :] = traces[source : source + 8]
@@ -562,7 +569,7 @@
     for pair in range(4 * rows):
         e = 8 * first_row + 2 * pair
         turned = t16[e * 64 : e * 64 + 128, :].astype(F32).T[:64]
-        first, second = labels[e], labels[e + 1]
+        first, second = labels[0, e], labels[0, e + 1]
         for a in range(4):
             keep = jnp.where(
                 lane128 < 64,
@@ -597,12 +604,12 @@
             columns += [face_column(f, value) for f, value in enumerate(rows)]
             pieces = dot(w[own, :], jnp.concatenate(columns, 1)).astype(BF16)
             piece = lambda s: pieces[:, s * 128 : s * 128 + 128]
-            big[0, here, :] = masked(masks, piece(0), labels[e])
-            big[1, here, :] = masked(masks, piece(1), labels[jnp.maximum(e - 8, 0)])
-            big[2, here, :] = masked(masks, piece(2), labels[jnp.minimum(e + 8, 31)])
+            big[0, here, :] = masked(masks, piece(0), labels[0, e])
+            big[1, here, :] = masked(masks, piece(1), labels[0, jnp.maximum(e - 8, 0)])
+            big[2, here, :] = masked(masks, piece(2), labels[0, jnp.minimum(e + 8, 31)])
             nothing = jnp.zeros((64, 256), BF16)
-            big[3, here, :] = masked(masks, piece(3), labels[e - 1]) if iy > 0 else nothing
-            big[4, here, :] = masked(masks, piece(4), labels[e + 1]) if iy < 7 else nothing
+            big[3, here, :] = masked(masks, piece(3), labels[0, e - 1]) if iy > 0 else nothing
+            big[4, here, :] = masked(masks, piece(4), labels[0, e + 1]) if iy < 7 else nothing
         return carry
 
     lax.fori_loop(first_row, last_row, row_of_elements, 0)
@@ -632,28 +639,35 @@
     result[...] = total
 
 
-def x_wait_kernel(labels, _, blocks, faces, tent, bounds, w, inverse, coefficients, t16, plus_y, minus_y, local, column, columns,
-                  stage, fstage, w32, tt, masks, big):
-    own_operators(blocks, faces, bounds, w, inverse, coefficients, stage, fstage, w32)
+def x_wait_kernel(labels_in, blocks, faces, tent, w, t16, plus_y, minus_y, local, column, columns, _,
+                  stage, fstage, w32, tt, masks, big, labels, label_sem):
+    fetch = pltpu.make_async_copy(labels_in, labels, label_sem.at[0])
+    fetch.start()
+    own_operators(blocks, faces, w, stage, fstage, w32)
     prolongator(tent, t16, plus_y, minus_y, fstage, w32)
+    fetch.wait()
     galerkin(0, None, labels, t16, plus_y, minus_y, w, local, column, columns, tt, masks, big)
 
 
-def y_wait_kernel(labels, side_labels, t16, plus_y, minus_y, w, before_local, column0, x_low, x_high, guess, b, inverse,
-                  local, columns, wx, mask_rows, t_ref, r_ref, i_ref, ghost,
-                  stage, fstage, w32, x_ref, a_ref, rows, masks, side, result, sems, column1, tt, big):
+def y_wait_kernel(labels_in, t16, plus_y, minus_y, w, before_local, column0, x_low, x_high, guess, b, diagonal,
+                  local, columns, wx, mask_rows, t_ref, r_ref, i_ref, coefficients, ghost, _,
+                  stage, fstage, w32, x_ref, a_ref, rows, masks, side, result, sems, column1, tt, big, labels, label_sem):
+    fetch = pltpu.make_async_copy(labels_in, labels, label_sem.at[0])
+    fetch.start()
+    coefficients[...] = b[192:200, :]
+    halo_x(x_low, x_high, wx, stage, fstage, w32)
+    start_smoothing(guess, b, diagonal, w, wx, x_low, x_high, t_ref, r_ref, i_ref, x_ref, a_ref)
+    fetch.wait()
     galerkin(1, before_local, labels, t16, plus_y, minus_y, w, local, column1, columns, tt, masks, big)
     copies = []
     for f, (message, column) in enumerate(((x_low, column0), (x_high, column1))):
         elements = [(24 * f + iy, iy * 64) for iy in range(EY)]
-        mask = lambda i: mask_of(masks, side_labels[8 * f + i])
+        mask = lambda i: mask_of(masks, labels[1, 8 * f + i])
         ghost_block(f, message, XT, 0, elements, mask, w, (column,), rows, side, result.at[f])
         copies.append(pltpu.make_async_copy(result.at[f], ghost.at[f], sems.at[f]))
         copies[-1].start()
     for i in range(8):
-        mask_rows[i * 16 : i * 16 + 16, :] = mask_of(masks, side_labels[16 + i])
-    halo_x(x_low, x_high, wx, stage, fstage, w32)
-    start_smoothing(guess, b, inverse, w, wx, x_low, x_high, t_ref, r_ref, i_ref, x_ref, a_ref)
+        mask_rows[i * 16 : i * 16 + 16, :] = mask_of(masks, labels[1, 16 + i])
     for copy in copies:
         copy.wait()
 
@@ -719,15 +733,16 @@
     wide = lambda *shape: shaped(*shape, dtype=F32)
     rhs = jnp.swapaxes(rhs[0, 0], 1, 2)
     guess = jnp.swapaxes(guess[0, 0], 1, 2)
-    labels, side_labels = aggregate.reshape(NE), ghost_labels.reshape(24)
     blocks, faces, tentative = [a.reshape(NE, 4096) for a in (blocks, faces, tentative)]
-    even, odd, traces_packed, b_packed, b, diagonal = call(
+    even, odd, traces_packed, b_packed, b, diagonal, labels = call(
         pack_x_kernel,
-        [shaped(16, XLEN)] * 2 + [shaped(NE, 768)] * 2 + [wide(NRHS * NE, 64), shaped(NE, 128)],
+        [shaped(16, XLEN)] * 2 + [shaped(NE, 768)] * 2 + [wide(NRHS * NE + 8, 64), shaped(NE, 128), shaped(8, 128, dtype=jnp.int32)],
         [pltpu.VMEM((NE, 4096), BF16)] * 3 + [pltpu.VMEM((NRHS, NE, 64), F32)] * 2
+        + [pltpu.VMEM((1, 2), F32), pltpu.VMEM((1, NE), jnp.int32), pltpu.VMEM((1, 24), jnp.int32)]
         + [STAGES[0], STAGES[2], pltpu.VMEM((2048, 128), BF16)] + [pltpu.VMEM((256, 128), F32)] * 2
-        + [pltpu.SemaphoreType.DMA((5,))],
-        (blocks, faces, tentative, guess, rhs), 10**6, 2**20, [HBM] * 5, room=62,
+        + [pltpu.SemaphoreType.DMA((8,))],
+        (blocks, faces, tentative, guess, rhs, bounds.reshape(1, 2), aggregate.reshape(1, NE), ghost_labels.reshape(1, 24)),
+        10**6, 2**20, [HBM] * 8, room=62,
     )
     even, odd = exchange((even, odd), "bx", (0, 1))
     def part_of(rows):
@@ -736,11 +751,13 @@
 
     early, early_scratch = part_of(ROWS_EARLY)
     late, late_scratch = part_of(EX - ROWS_EARLY)
-    w, inverse, coefficients, t16, plus_y, minus_y, local, column0, columns0 = call(
+    scalars = [pltpu.SMEM((8, 128), jnp.int32), pltpu.SemaphoreType.DMA((1,))]
+    passed = shaped(8, 128, dtype=jnp.int32)
+    w, t16, plus_y, minus_y, local, column0, columns0, labels = call(
         x_wait_kernel,
-        [shaped(2048, 128), wide(NE, 64), wide(8, 128), shaped(2048, 128), shaped(512, 128), shaped(512, 128)] + early,
-        STAGES + early_scratch,
-        (labels, side_labels, blocks, faces, tentative, bounds.reshape(1, 2)), 4 * 10**9, 2**22, [SMEM] * 2 + [VMEM] * 4,
+        [shaped(2048, 128), shaped(2048, 128), shaped(512, 128), shaped(512, 128)] + early + [passed],
+        STAGES + early_scratch + scalars,
+        (labels, blocks, faces, tentative), 4 * 10**9, 2**22, [HBM] + [VMEM] * 3, [VMEM] * 7 + [HBM], {0: 7},
     )
     odd, even, x_low, x_high = call(
         pack_y_kernel, [shaped(16, YLEN)] * 2 + [shaped(16, XLEN)] * 2, [],
@@ -751,11 +768,12 @@
     extended = [wide(SPAN, 128)] * 2 + [wide(EXT, 128)]
     fields = [pltpu.VMEM(a.shape, F32) for a in extended]
     pads = [pltpu.VMEM((8 * EXT, 128), F32)] * 2
-    local, columns1, wx, mask_rows, traces, residue, inverses, ghost = call(
-        y_wait_kernel, [late[0], late[2], shaped(2048, 128), shaped(128, 256)] + extended + [wide(4, 256, 256)],
-        STAGES + pads + GHOST + [pltpu.VMEM((256, 512), BF16), late_scratch[0], late_scratch[2]],
-        (labels, side_labels, t16, plus_y, minus_y, w, local, column0, x_low, x_high, guess, b, inverse), 4 * 10**9, 2**22,
-        [SMEM] * 2 + [VMEM] * 11, [VMEM] * 7 + [HBM],
+    local, columns1, wx, mask_rows, traces, residue, inverses, coefficients, ghost, _ = call(
+        y_wait_kernel,
+        [late[0], late[2], shaped(2048, 128), shaped(128, 256)] + extended + [wide(8, 64), wide(4, 256, 256), passed],
+        STAGES + pads + GHOST + [pltpu.VMEM((256, 512), BF16), late_scratch[0], late_scratch[2]] + scalars,
+        (labels, t16, plus_y, minus_y, w, local, column0, x_low, x_high, guess, b, diagonal), 4 * 10**9, 2**22,
+        [HBM] + [VMEM] * 11, [VMEM] * 8 + [HBM] * 2, {0: 9},
     )
     smoothed, ghost = call(
         finish_kernel, [wide(NRHS, NE, 64), wide(4, 256, 256)],

time: 32.7 us -> 32.3 us (0.988)
  the two profiles are of different devices: /device:TPU:102 before, /device:TPU:281 now
where the time goes in v9:
time: 32.3 us; the launch traced here: 32.1 us
  Pallas kernels  15.1 us (47%)
  starting transfers between devices  12.7 us (39%)
  waiting for transfers between devices  3.37 us (10%)
  between operations  0.84 us (3%)
    pallas_call x5, Pallas kernels, call(): pl.pallas_call(kernel, out_shape=outs, in_specs=in_specs or [VMEM] * len(...  15.1 us
    ppermute x4, starting transfers between devices, exchange(): out.append(lax.ppermute(message, axis, pairs))  12.7 us
    ppermute x4, waiting for transfers between devices, exchange(): out.append(lax.ppermute(message, axis, pairs))  3.37 us
  transfers between devices with their start and end apart: 4, of which 1 were waited for; matrix products, arithmetic and copies ran while one was open for 0% of the time, Pallas kernels for 23%

profile of v9, /device:TPU:281, one launch (start us, length us, event | category | flops | bytes accessed | tf_op | source)
XLA Modules:
  0.0 32.1 jit_solution(11459779154642605044)
XLA Ops:
  0.6 0.0 copy-start
  0.6 0.0 copy-start.1
  0.7 0.0 copy-start.2
  0.7 2.9 %shard_map.103 = (bf16[16,5120]{1,0:T(8,128)(2,1)}, bf16[16,5120]{1,0:T(8,128)(2,1)}, bf16[32,768]{1,0:T(8,128)(2,1)}, bf16[32,768]{1,0:T(8,128)(2,1)}, f32[200,...) custom-call(bf16[32,4096]{1,0:T(8,128)(2,1)} %bitcast.17, bf16[32,4096]{1,0:T(8,128)(2,1)} %bitcast.20, ...), custom_call_target="tpu_custom_call" | custom-call | flops 1000000 | bytes 1048576 | tf_op jit(solution)/shard_map/pallas_call | solution.py:694
  3.6 0.0 copy-start.8
  3.6 3.1 %collective-permute-start = (bf16[16,5120]{1,0:T(8,128)(2,1)}, bf16[16,5120]{1,0:T(8,128)(2,1)S(1)}, u32[]{:S(2)}, u32[]{:S(2)}) collective-permute-start(bf16[16,5120]{1,0:T(8,128)(2,1)} %get-tuple-element.44), channel_id=1, source_target_pairs={{0,16},{16,0},{32,48},{48,32},{64,80},{80,64},{96,112},{112,96},{1... | collective-permute-start | bytes 491528 | tf_op jit(solution)/shard_map/ppermute | solution.py:712
  6.7 1.9 %collective-permute-start.1 = (bf16[16,5120]{1,0:T(8,128)(2,1)}, bf16[16,5120]{1,0:T(8,128)(2,1)S(1)}, u32[]{:S(2)}, u32[]{:S(2)}) collective-permute-start(bf16[16,5120]{1,0:T(8,128)(2,1)} %get-tuple-element.45), channel_id=1, source_target_pairs={{16,32},{32,16},{48,64},{64,48},{80,96},{96,80},{112,128},{128,112... | collective-permute-start | bytes 491528 | tf_op jit(solution)/shard_map/ppermute | solution.py:712
  8.7 0.0 copy-done
  8.7 0.0 copy-done.1
  8.7 0.0 copy-done.2
  8.7 0.0 copy-done.8
  8.7 0.0 copy-start.4
  8.7 0.0 copy-start.5
  8.7 0.0 copy-start.6
  8.7 3.6 %shard_map.104 = (bf16[2048,128]{1,0:T(8,128)(2,1)S(1)}, bf16[2048,128]{1,0:T(8,128)(2,1)S(1)}, bf16[512,128]{1,0:T(8,128)(2,1)S(1)}, bf16[512,128]{1,0:T(8,128)...) custom-call(s32[8,128]{1,0:T(8,128)S(1)} %copy-done.8, ...), custom_call_target="tpu_custom_call", output_to_operand_aliasing={{7}: (0, {})} | custom-call | flops 4000000000 | bytes 4194304 | tf_op jit(solution)/shard_map/pallas_call | solution.py:694
  12.3 0.0 collective-permute-done.x_even
  12.3 3.4 %collective-permute-done.1.x_odd = bf16[16,5120]{1,0:T(8,128)(2,1)S(1)} collective-permute-done((bf16[16,5120]{1,0:T(8,128)(2,1)}, bf16[16,5120]{1,0:T(8,128)(2,1)S(1)}, u32[]{:S(2)}, u32[]{:S(2)}) %collective-permute-start.1) | collective-permute-done | bytes 163872 | tf_op jit(solution)/shard_map/ppermute | solution.py:712
  15.7 0.0 copy-done.4
  15.7 0.0 copy-done.5
  15.7 0.0 copy-done.6
  15.7 0.0 copy-start.3
  15.7 0.0 copy-start.7
  15.7 0.4 %shard_map.105 = (bf16[16,6144]{1,0:T(8,128)(2,1)S(1)}, bf16[16,6144]{1,0:T(8,128)(2,1)S(1)}, bf16[16,5120]{1,0:T(8,128)(2,1)S(1)}, bf16[16,5120]{1,0:T(8,128)(2,1)S(1)}) custom-call(bf16[32,4096]{1,0:T(8,128)(2,1)S(1)} %bitcast.19, bf16[32,4096]{1,0:T(8,128)(2,1)S(1)} %bitcast.22, bf16[32,4096]{1,0:T(8,128)(2,1)S(1)} %bitcast.25, ...), custom_call_target="tpu_custom_call" | custom-call | flops 100000000 | bytes 1048576 | tf_op jit(solution)/shard_map/pallas_call | solution.py:694
  16.1 5.8 %collective-permute-start.2 = (bf16[16,6144]{1,0:T(8,128)(2,1)S(1)}, bf16[16,6144]{1,0:T(8,128)(2,1)S(1)}, u32[]{:S(2)}, u32[]{:S(2)}) collective-permute-start(bf16[16,6144]{1,0:T(8,128)(2,1)S(1)} %get-tuple-element.52), channel_id=1, source_target_pairs={{1,2},{2,1},{3,4},{4,3},{5,6},{6,5},{7,8},{8,7},{9,10},{10,9},{11,... | collective-permute-start | bytes 589832 | tf_op jit(solution)/shard_map/ppermute | solution.py:712
  21.9 1.9 %collective-permute-start.3 = (bf16[16,6144]{1,0:T(8,128)(2,1)S(1)}, bf16[16,6144]{1,0:T(8,128)(2,1)S(1)}, u32[]{:S(2)}, u32[]{:S(2)}) collective-permute-start(bf16[16,6144]{1,0:T(8,128)(2,1)S(1)} %get-tuple-element.53), channel_id=1, source_target_pairs={{0,1},{1,0},{2,3},{3,2},{4,5},{5,4},{6,7},{7,6},{8,9},{9,8},{10,11... | collective-permute-start | bytes 589832 | tf_op jit(solution)/shard_map/ppermute | solution.py:712
  23.8 0.0 copy-done.3
  23.8 0.0 copy-done.7
  23.8 3.9 %shard_map.106 = (f32[256,256]{1,0:T(8,128)}, bf16[2,256,128]{2,1,0:T(8,128)(2,1)S(1)}, bf16[2048,128]{1,0:T(8,128)(2,1)S(1)}, bf16[128,256]{1,0:T(8,128)(2,1)S(...) custom-call(s32[8,128]{1,0:T(8,128)S(1)} %get-tuple-element.34.label, ...), custom_call_target="tpu_custom_call", output_to_operand_aliasing={{9}: (0, {})} | custom-call | flops 4000000000 | bytes 4194304 | tf_op jit(solution)/shard_map/pallas_call | solution.py:694
  27.8 0.0 collective-permute-done.2.y_odd
  27.8 0.0 collective-permute-done.3.y_even
  27.8 4.3 %shard_map.107 = (f32[6,32,64]{2,1,0:T(8,128)}, f32[4,256,256]{2,1,0:T(8,128)}) custom-call(bf16[128,256]{1,0:T(8,128)(2,1)S(1)} %get-tuple-element.49.mask_rows, f32[6,32,64]{2,1,0:T(8,128)S(1)} %bitcast.28, bf16[2048,128]{1,0:T(8,128)(2,1)S(1)} %get-tuple-element.38.w, ...), custom_call_target="tpu_custom_call", output_to_operand_aliasing={{1}: (12, {})} | custom-call | flops 1000000000 | bytes 1048576 | tf_op jit(solution)/shard_map/pallas_call | solution.py:694
Async XLA Ops:
  0.6 8.0 %copy-start = (bf16[1,1,32,4096]{3,2,1,0:T(8,128)(2,1)S(1)}, bf16[1,1,32,4096]{3,2,1,0:T(8,128)(2,1)}, u32[]{:S(2)}) copy-start(bf16[1,1,32,4096]{3,2,1,0:T(8,128)(2,1)} %param.8) | copy-start | bytes 786436
  0.6 8.0 %copy-start.1 = (bf16[1,1,32,4096]{3,2,1,0:T(8,128)(2,1)S(1)}, bf16[1,1,32,4096]{3,2,1,0:T(8,128)(2,1)}, u32[]{:S(2)}) copy-start(bf16[1,1,32,4096]{3,2,1,0:T(8,128)(2,1)} %param.9) | copy-start | bytes 786436
  0.7 8.0 %copy-start.2 = (bf16[1,1,32,4096]{3,2,1,0:T(8,128)(2,1)S(1)}, bf16[1,1,32,4096]{3,2,1,0:T(8,128)(2,1)}, u32[]{:S(2)}) copy-start(bf16[1,1,32,4096]{3,2,1,0:T(8,128)(2,1)} %param.10) | copy-start | bytes 786436
  3.6 5.1 %copy-start.8 = (s32[8,128]{1,0:T(8,128)S(1)}, s32[8,128]{1,0:T(8,128)}, u32[]{:S(2)}) copy-start(s32[8,128]{1,0:T(8,128)} %get-tuple-element.33.labels_in) | copy-start | bytes 12292
  3.6 8.7 %collective-permute-start = (bf16[16,5120]{1,0:T(8,128)(2,1)}, bf16[16,5120]{1,0:T(8,128)(2,1)S(1)}, u32[]{:S(2)}, u32[]{:S(2)}) collective-permute-start(bf16[16,5120]{1,0:T(8,128)(2,1)} %get-tuple-element.44), channel_id=1, source_target_pairs={{0,16},{16,0},{32,48},{48,32},{64,80},{80,64},{96,112},{112,96},{1... | collective-permute-start | bytes 491528 | tf_op jit(solution)/shard_map/ppermute | solution.py:712
  6.7 9.0 %collective-permute-start.1 = (bf16[16,5120]{1,0:T(8,128)(2,1)}, bf16[16,5120]{1,0:T(8,128)(2,1)S(1)}, u32[]{:S(2)}, u32[]{:S(2)}) collective-permute-start(bf16[16,5120]{1,0:T(8,128)(2,1)} %get-tuple-element.45), channel_id=1, source_target_pairs={{16,32},{32,16},{48,64},{64,48},{80,96},{96,80},{112,128},{128,112... | collective-permute-start | bytes 491528 | tf_op jit(solution)/shard_map/ppermute | solution.py:712
  8.7 7.0 %copy-start.4 = (bf16[32,768]{1,0:T(8,128)(2,1)S(1)}, bf16[32,768]{1,0:T(8,128)(2,1)}, u32[]{:S(2)}) copy-start(bf16[32,768]{1,0:T(8,128)(2,1)} %get-tuple-element.41.traces_packed) | copy-start | bytes 147460
  8.7 7.0 %copy-start.5 = (bf16[32,768]{1,0:T(8,128)(2,1)S(1)}, bf16[32,768]{1,0:T(8,128)(2,1)}, u32[]{:S(2)}) copy-start(bf16[32,768]{1,0:T(8,128)(2,1)} %get-tuple-element.42.b_packed) | copy-start | bytes 147460
  8.7 7.0 %copy-start.6 = (bf16[32,128]{1,0:T(8,128)(2,1)S(1)}, bf16[32,128]{1,0:T(8,128)(2,1)}, u32[]{:S(2)}) copy-start(bf16[32,128]{1,0:T(8,128)(2,1)} %get-tuple-element.43.diagonal) | copy-start | bytes 24580
  15.7 8.1 %copy-start.3 = (f32[1,1,6,64,32]{3,4,2,1,0:T(8,128)S(1)}, f32[1,1,6,64,32]{3,4,2,1,0:T(8,128)}, u32[]{:S(2)}) copy-start(f32[1,1,6,64,32]{3,4,2,1,0:T(8,128)} %param.14) | copy-start | bytes 147460
  15.7 8.1 %copy-start.7 = (f32[200,64]{1,0:T(8,128)S(1)}, f32[200,64]{1,0:T(8,128)}, u32[]{:S(2)}) copy-start(f32[200,64]{1,0:T(8,128)} %get-tuple-element.48.b) | copy-start | bytes 153604
  16.1 11.7 %collective-permute-start.2 = (bf16[16,6144]{1,0:T(8,128)(2,1)S(1)}, bf16[16,6144]{1,0:T(8,128)(2,1)S(1)}, u32[]{:S(2)}, u32[]{:S(2)}) collective-permute-start(bf16[16,6144]{1,0:T(8,128)(2,1)S(1)} %get-tuple-element.52), channel_id=1, source_target_pairs={{1,2},{2,1},{3,4},{4,3},{5,6},{6,5},{7,8},{8,7},{9,10},{10,9},{11,... | collective-permute-start | bytes 589832 | tf_op jit(solution)/shard_map/ppermute | solution.py:712
  21.9 5.9 %collective-permute-start.3 = (bf16[16,6144]{1,0:T(8,128)(2,1)S(1)}, bf16[16,6144]{1,0:T(8,128)(2,1)S(1)}, u32[]{:S(2)}, u32[]{:S(2)}) collective-permute-start(bf16[16,6144]{1,0:T(8,128)(2,1)S(1)} %get-tuple-element.53), channel_id=1, source_target_pairs={{0,1},{1,0},{2,3},{3,2},{4,5},{5,4},{6,7},{7,6},{8,9},{9,8},{10,11... | collective-permute-start | bytes 589832 | tf_op jit(solution)/shard_map/ppermute | solution.py:712

commit v10 on v9

--- a/solution.py
+++ b/solution.py
@@ -656,7 +656,6 @@
     fetch.start()
     coefficients[...] = b[192:200, :]
     halo_x(x_low, x_high, wx, stage, fstage, w32)
-    start_smoothing(guess, b, diagonal, w, wx, x_low, x_high, t_ref, r_ref, i_ref, x_ref, a_ref)
     fetch.wait()
     galerkin(1, before_local, labels, t16, plus_y, minus_y, w, local, column1, columns, tt, masks, big)
     copies = []
@@ -668,6 +667,7 @@
         copies[-1].start()
     for i in range(8):
         mask_rows[i * 16 : i * 16 + 16, :] = mask_of(masks, labels[1, 16 + i])
+    start_smoothing(guess, b, diagonal, w, wx, x_low, x_high, t_ref, r_ref, i_ref, x_ref, a_ref)
     for copy in copies:
         copy.wait()
 

time: 32.3 us -> 32.1 us (level)
  the two profiles are of different devices: /device:TPU:281 before, /device:TPU:388 now
where the time goes in v10:
time: 32.1 us; the launch traced here: 31.9 us
  Pallas kernels  14.8 us (46%)
  starting transfers between devices  13 us (40%)
  waiting for transfers between devices  3.22 us (10%)
  between operations  0.83 us (3%)
    pallas_call x5, Pallas kernels, call(): pl.pallas_call(kernel, out_shape=outs, in_specs=in_specs or [VMEM] * len(...  14.8 us
    ppermute x4, starting transfers between devices, exchange(): out.append(lax.ppermute(message, axis, pairs))  13 us
    ppermute x4, waiting for transfers between devices, exchange(): out.append(lax.ppermute(message, axis, pairs))  3.22 us
  transfers between devices with their start and end apart: 4, of which 2 were waited for; matrix products, arithmetic and copies ran while one was open for 0% of the time, Pallas kernels for 23%

profile of v10, /device:TPU:388, one launch (start us, length us, event | category | flops | bytes accessed | tf_op | source)
XLA Modules:
  0.0 31.9 jit_solution(4066410601989613213)
XLA Ops:
  0.6 0.0 copy-start
  0.6 0.0 copy-start.1
  0.7 0.0 copy-start.2
  0.7 2.9 %shard_map.103 = (bf16[16,5120]{1,0:T(8,128)(2,1)}, bf16[16,5120]{1,0:T(8,128)(2,1)}, bf16[32,768]{1,0:T(8,128)(2,1)}, bf16[32,768]{1,0:T(8,128)(2,1)}, f32[200,...) custom-call(bf16[32,4096]{1,0:T(8,128)(2,1)} %bitcast.17, bf16[32,4096]{1,0:T(8,128)(2,1)} %bitcast.20, ...), custom_call_target="tpu_custom_call" | custom-call | flops 1000000 | bytes 1048576 | tf_op jit(solution)/shard_map/pallas_call | solution.py:694
  3.6 0.0 copy-start.8
  3.6 3.1 %collective-permute-start = (bf16[16,5120]{1,0:T(8,128)(2,1)}, bf16[16,5120]{1,0:T(8,128)(2,1)S(1)}, u32[]{:S(2)}, u32[]{:S(2)}) collective-permute-start(bf16[16,5120]{1,0:T(8,128)(2,1)} %get-tuple-element.44), channel_id=1, source_target_pairs={{0,16},{16,0},{32,48},{48,32},{64,80},{80,64},{96,112},{112,96},{1... | collective-permute-start | bytes 491528 | tf_op jit(solution)/shard_map/ppermute | solution.py:712
  6.7 4.4 %collective-permute-start.1 = (bf16[16,5120]{1,0:T(8,128)(2,1)}, bf16[16,5120]{1,0:T(8,128)(2,1)S(1)}, u32[]{:S(2)}, u32[]{:S(2)}) collective-permute-start(bf16[16,5120]{1,0:T(8,128)(2,1)} %get-tuple-element.45), channel_id=1, source_target_pairs={{16,32},{32,16},{48,64},{64,48},{80,96},{96,80},{112,128},{128,112... | collective-permute-start | bytes 491528 | tf_op jit(solution)/shard_map/ppermute | solution.py:712
  11.1 0.0 copy-done
  11.1 0.0 copy-done.1
  11.1 0.0 copy-done.2
  11.1 0.0 copy-done.8
  11.1 0.0 copy-start.4
  11.2 0.0 copy-start.5
  11.2 0.0 copy-start.6
  11.2 3.6 %shard_map.104 = (bf16[2048,128]{1,0:T(8,128)(2,1)S(1)}, bf16[2048,128]{1,0:T(8,128)(2,1)S(1)}, bf16[512,128]{1,0:T(8,128)(2,1)S(1)}, bf16[512,128]{1,0:T(8,128)...) custom-call(s32[8,128]{1,0:T(8,128)S(1)} %copy-done.8, ...), custom_call_target="tpu_custom_call", output_to_operand_aliasing={{7}: (0, {})} | custom-call | flops 4000000000 | bytes 4194304 | tf_op jit(solution)/shard_map/pallas_call | solution.py:694
  14.8 0.0 collective-permute-done.x_even
  14.8 1.8 %collective-permute-done.1.x_odd = bf16[16,5120]{1,0:T(8,128)(2,1)S(1)} collective-permute-done((bf16[16,5120]{1,0:T(8,128)(2,1)}, bf16[16,5120]{1,0:T(8,128)(2,1)S(1)}, u32[]{:S(2)}, u32[]{:S(2)}) %collective-permute-start.1) | collective-permute-done | bytes 163872 | tf_op jit(solution)/shard_map/ppermute | solution.py:712
  16.6 0.0 copy-done.4
  16.6 0.0 copy-done.5
  16.6 0.0 copy-done.6
  16.6 0.0 copy-start.3
  16.6 0.0 copy-start.7
  16.6 0.4 %shard_map.105 = (bf16[16,6144]{1,0:T(8,128)(2,1)S(1)}, bf16[16,6144]{1,0:T(8,128)(2,1)S(1)}, bf16[16,5120]{1,0:T(8,128)(2,1)S(1)}, bf16[16,5120]{1,0:T(8,128)(2,1)S(1)}) custom-call(bf16[32,4096]{1,0:T(8,128)(2,1)S(1)} %bitcast.19, bf16[32,4096]{1,0:T(8,128)(2,1)S(1)} %bitcast.22, bf16[32,4096]{1,0:T(8,128)(2,1)S(1)} %bitcast.25, ...), custom_call_target="tpu_custom_call" | custom-call | flops 100000000 | bytes 1048576 | tf_op jit(solution)/shard_map/pallas_call | solution.py:694
  17.0 3.4 %collective-permute-start.2 = (bf16[16,6144]{1,0:T(8,128)(2,1)S(1)}, bf16[16,6144]{1,0:T(8,128)(2,1)S(1)}, u32[]{:S(2)}, u32[]{:S(2)}) collective-permute-start(bf16[16,6144]{1,0:T(8,128)(2,1)S(1)} %get-tuple-element.52), channel_id=1, source_target_pairs={{1,2},{2,1},{3,4},{4,3},{5,6},{6,5},{7,8},{8,7},{9,10},{10,9},{11,... | collective-permute-start | bytes 589832 | tf_op jit(solution)/shard_map/ppermute | solution.py:712
  20.4 2.1 %collective-permute-start.3 = (bf16[16,6144]{1,0:T(8,128)(2,1)S(1)}, bf16[16,6144]{1,0:T(8,128)(2,1)S(1)}, u32[]{:S(2)}, u32[]{:S(2)}) collective-permute-start(bf16[16,6144]{1,0:T(8,128)(2,1)S(1)} %get-tuple-element.53), channel_id=1, source_target_pairs={{0,1},{1,0},{2,3},{3,2},{4,5},{5,4},{6,7},{7,6},{8,9},{9,8},{10,11... | collective-permute-start | bytes 589832 | tf_op jit(solution)/shard_map/ppermute | solution.py:712
  22.5 0.0 copy-done.3
  22.6 0.0 copy-done.7
  22.6 3.7 %shard_map.106 = (f32[256,256]{1,0:T(8,128)}, bf16[2,256,128]{2,1,0:T(8,128)(2,1)S(1)}, bf16[2048,128]{1,0:T(8,128)(2,1)S(1)}, bf16[128,256]{1,0:T(8,128)(2,1)S(...) custom-call(s32[8,128]{1,0:T(8,128)S(1)} %get-tuple-element.34.label, ...), custom_call_target="tpu_custom_call", output_to_operand_aliasing={{9}: (0, {})} | custom-call | flops 4000000000 | bytes 4194304 | tf_op jit(solution)/shard_map/pallas_call | solution.py:694
  26.2 1.4 %collective-permute-done.2.y_odd = bf16[16,6144]{1,0:T(8,128)(2,1)S(1)} collective-permute-done((bf16[16,6144]{1,0:T(8,128)(2,1)S(1)}, bf16[16,6144]{1,0:T(8,128)(2,1)S(1)}, u32[]{:S(2)}, u32[]{:S(2)}) %collective-permute-start.2) | collective-permute-done | bytes 196640 | tf_op jit(solution)/shard_map/ppermute | solution.py:712
  27.6 0.0 collective-permute-done.3.y_even
  27.6 4.3 %shard_map.107 = (f32[6,32,64]{2,1,0:T(8,128)}, f32[4,256,256]{2,1,0:T(8,128)}) custom-call(bf16[128,256]{1,0:T(8,128)(2,1)S(1)} %get-tuple-element.49.mask_rows, f32[6,32,64]{2,1,0:T(8,128)S(1)} %bitcast.28, bf16[2048,128]{1,0:T(8,128)(2,1)S(1)} %get-tuple-element.38.w, ...), custom_call_target="tpu_custom_call", output_to_operand_aliasing={{1}: (12, {})} | custom-call | flops 1000000000 | bytes 1048576 | tf_op jit(solution)/shard_map/pallas_call | solution.py:694
Async XLA Ops:
  0.6 10.5 %copy-start = (bf16[1,1,32,4096]{3,2,1,0:T(8,128)(2,1)S(1)}, bf16[1,1,32,4096]{3,2,1,0:T(8,128)(2,1)}, u32[]{:S(2)}) copy-start(bf16[1,1,32,4096]{3,2,1,0:T(8,128)(2,1)} %param.8) | copy-start | bytes 786436
  0.6 10.5 %copy-start.1 = (bf16[1,1,32,4096]{3,2,1,0:T(8,128)(2,1)S(1)}, bf16[1,1,32,4096]{3,2,1,0:T(8,128)(2,1)}, u32[]{:S(2)}) copy-start(bf16[1,1,32,4096]{3,2,1,0:T(8,128)(2,1)} %param.9) | copy-start | bytes 786436
  0.7 10.5 %copy-start.2 = (bf16[1,1,32,4096]{3,2,1,0:T(8,128)(2,1)S(1)}, bf16[1,1,32,4096]{3,2,1,0:T(8,128)(2,1)}, u32[]{:S(2)}) copy-start(bf16[1,1,32,4096]{3,2,1,0:T(8,128)(2,1)} %param.10) | copy-start | bytes 786436
  3.6 7.6 %copy-start.8 = (s32[8,128]{1,0:T(8,128)S(1)}, s32[8,128]{1,0:T(8,128)}, u32[]{:S(2)}) copy-start(s32[8,128]{1,0:T(8,128)} %get-tuple-element.33.labels_in) | copy-start | bytes 12292
  3.6 11.2 %collective-permute-start = (bf16[16,5120]{1,0:T(8,128)(2,1)}, bf16[16,5120]{1,0:T(8,128)(2,1)S(1)}, u32[]{:S(2)}, u32[]{:S(2)}) collective-permute-start(bf16[16,5120]{1,0:T(8,128)(2,1)} %get-tuple-element.44), channel_id=1, source_target_pairs={{0,16},{16,0},{32,48},{48,32},{64,80},{80,64},{96,112},{112,96},{1... | collective-permute-start | bytes 491528 | tf_op jit(solution)/shard_map/ppermute | solution.py:712
  6.7 9.9 %collective-permute-start.1 = (bf16[16,5120]{1,0:T(8,128)(2,1)}, bf16[16,5120]{1,0:T(8,128)(2,1)S(1)}, u32[]{:S(2)}, u32[]{:S(2)}) collective-permute-start(bf16[16,5120]{1,0:T(8,128)(2,1)} %get-tuple-element.45), channel_id=1, source_target_pairs={{16,32},{32,16},{48,64},{64,48},{80,96},{96,80},{112,128},{128,112... | collective-permute-start | bytes 491528 | tf_op jit(solution)/shard_map/ppermute | solution.py:712
  11.1 5.4 %copy-start.4 = (bf16[32,768]{1,0:T(8,128)(2,1)S(1)}, bf16[32,768]{1,0:T(8,128)(2,1)}, u32[]{:S(2)}) copy-start(bf16[32,768]{1,0:T(8,128)(2,1)} %get-tuple-element.41.traces_packed) | copy-start | bytes 147460
  11.2 5.4 %copy-start.5 = (bf16[32,768]{1,0:T(8,128)(2,1)S(1)}, bf16[32,768]{1,0:T(8,128)(2,1)}, u32[]{:S(2)}) copy-start(bf16[32,768]{1,0:T(8,128)(2,1)} %get-tuple-element.42.b_packed) | copy-start | bytes 147460
  11.2 5.4 %copy-start.6 = (bf16[32,128]{1,0:T(8,128)(2,1)S(1)}, bf16[32,128]{1,0:T(8,128)(2,1)}, u32[]{:S(2)}) copy-start(bf16[32,128]{1,0:T(8,128)(2,1)} %get-tuple-element.43.diagonal) | copy-start | bytes 24580
  16.6 5.9 %copy-start.3 = (f32[1,1,6,64,32]{3,4,2,1,0:T(8,128)S(1)}, f32[1,1,6,64,32]{3,4,2,1,0:T(8,128)}, u32[]{:S(2)}) copy-start(f32[1,1,6,64,32]{3,4,2,1,0:T(8,128)} %param.14) | copy-start | bytes 147460
  16.6 5.9 %copy-start.7 = (f32[200,64]{1,0:T(8,128)S(1)}, f32[200,64]{1,0:T(8,128)}, u32[]{:S(2)}) copy-start(f32[200,64]{1,0:T(8,128)} %get-tuple-element.48.b) | copy-start | bytes 153604
  17.0 10.6 %collective-permute-start.2 = (bf16[16,6144]{1,0:T(8,128)(2,1)S(1)}, bf16[16,6144]{1,0:T(8,128)(2,1)S(1)}, u32[]{:S(2)}, u32[]{:S(2)}) collective-permute-start(bf16[16,6144]{1,0:T(8,128)(2,1)S(1)} %get-tuple-element.52), channel_id=1, source_target_pairs={{1,2},{2,1},{3,4},{4,3},{5,6},{6,5},{7,8},{8,7},{9,10},{10,9},{11,... | collective-permute-start | bytes 589832 | tf_op jit(solution)/shard_map/ppermute | solution.py:712
  20.4 7.2 %collective-permute-start.3 = (bf16[16,6144]{1,0:T(8,128)(2,1)S(1)}, bf16[16,6144]{1,0:T(8,128)(2,1)S(1)}, u32[]{:S(2)}, u32[]{:S(2)}) collective-permute-start(bf16[16,6144]{1,0:T(8,128)(2,1)S(1)} %get-tuple-element.53), channel_id=1, source_target_pairs={{0,1},{1,0},{2,3},{3,2},{4,5},{5,4},{6,7},{7,6},{8,9},{9,8},{10,11... | collective-permute-start | bytes 589832 | tf_op jit(solution)/shard_map/ppermute | solution.py:712
